TPU v7x, 32 devices: a whole 2x2x4 slice. The times are simulated.
32 devices in a mesh: lon: 8 (over z, y), lat: 4 (over x, core).
Axes of the slice: x: 2, y: 2, z: 4, core: 2. Of those that a mesh axis runs over, the one named last changes fastest.
Arguments:
- spectrum: float32 [36, 36, 32, 512], P(None, None, 'lon', 'lat'), may hold values from 0.05 to 2
- sea_mask: int32 [32, 512], P('lon', 'lat'), may hold values 0 or 1
- refraction: float32 [2, 32, 512], P(None, 'lon', 'lat'), may hold values from -0.35 to 0.35
- atm_wind: float32 [2, 2, 4096], P(None, None, ('lon', 'lat')), may hold values from -20 to 20
- hour_fraction: float32 [1], replicated, may hold values from 0 to 1
- send_cells: int32 [32, 192], P(('lon', 'lat')), may hold values from 0 to 127, as said below
- recv_slots: int32 [4, 32, 512], P(None, 'lon', 'lat'), may hold values from 0 to 191, as said below
- recv_weights: float32 [4, 32, 512], P(None, 'lon', 'lat'), may hold values from 0.05 to 0.45
Outputs:
- spectrum_next: float32 [36, 36, 32, 512], P(None, None, 'lon', 'lat')
- surface_wind: float32 [2, 32, 512], P(None, 'lon', 'lat')
Inputs may be any that keep to these rules, and one draw needn't show every extreme that they name: `send_cells`: row t holds, for each of the 8 wave tiles of tile t's latitude band in lon order, a block of 24 local atmosphere cells of tile t; every entry is read by some wave cell. `recv_slots`: entry e of a wave cell refers to position e % 24 of the block that the atmosphere tile at lon index e // 24 of the same latitude band lists for this cell's wave tile.
All inputs are finite; a program needn't handle non-finite values. No bound on the sum of `sea_mask` on one device may be relied on, other than what follows from the above.
Results may differ from a plain program's by a relative error of at most 0.0003.
Values sent between devices are 32-bit elements; how exact they have to be, the bound alone decides.
No kernel may reach another device: no remote copies, remote signals or barrier semaphores. Data moves between devices by JAX's collectives and lax.ppermute only.
A program may use at most 128 MiB of HBM per device.

v0:
```python
import math

import jax
import jax.numpy as jnp
from jax import lax
from jax.sharding import PartitionSpec as P

base_freq = 0.035
freq_step = 1.1
courant_max = 0.9
gravity = 9.81
input_rate = 0.05
damping_rate = 0.8
energy_ref = 0.5


def padded_2(value, sides, width, wrap):
    for axis, dim in sides:
        size, length = (lax.axis_size(axis), value.shape[dim])
        up = [(i, (i + 1) % size) for i in range(size if wrap else size - 1)]
        down = [(j, i) for i, j in up]
        last = lax.slice_in_dim(value, length - width, length, axis=dim)
        initial = lax.slice_in_dim(value, 0, width, axis=dim)
        before = lax.ppermute(last, axis, up)
        after = lax.ppermute(initial, axis, down)
        value = jnp.concatenate([before, value, after], axis=dim)
    return value


def spectral_tables(freq_count, dir_count):
    frequencies = base_freq * freq_step ** jnp.arange(freq_count, dtype=jnp.float32)
    spacing = 2.0 * math.pi / dir_count
    angles = (jnp.arange(dir_count, dtype=jnp.float32) + 0.5) * spacing
    face_angles = (jnp.arange(dir_count, dtype=jnp.float32) + 1.0) * spacing
    return (frequencies, angles, face_angles)


def transport(padded, courant, dimension):
    length = padded.shape[dimension] - 4
    far_left = lax.slice_in_dim(padded, 0, length + 1, axis=dimension)
    left_cell = lax.slice_in_dim(padded, 1, length + 2, axis=dimension)
    right_cell = lax.slice_in_dim(padded, 2, length + 3, axis=dimension)
    far_right = lax.slice_in_dim(padded, 3, length + 4, axis=dimension)
    forward = courant > 0
    upwind = jnp.where(forward, left_cell, right_cell)
    downwind = jnp.where(forward, right_cell, left_cell)
    beyond = jnp.where(forward, far_left, far_right)
    magnitude = jnp.abs(courant)
    face_flux = courant * (
        upwind
        + 0.5 * (1.0 - magnitude) * (downwind - upwind)
        - (1.0 - magnitude * magnitude) / 6.0 * (downwind - 2.0 * upwind + beyond)
    )
    return lax.slice_in_dim(face_flux, 1, length + 1, axis=dimension) - lax.slice_in_dim(
        face_flux, 0, length, axis=dimension
    )


def local(
    spectrum, sea_mask, refraction, atm_wind, hour_fraction, send_cells, recv_slots, recv_weights
):
    freq_count = spectrum.shape[0]
    dir_count = spectrum.shape[1]
    sea_frac = sea_mask.astype(jnp.float32)
    frequencies, angles, face_angles = spectral_tables(freq_count, dir_count)
    period_ratio = base_freq / frequencies
    courant_lon = (courant_max * period_ratio[:, None] * jnp.cos(angles)[None, :])[:, :, None, None]
    courant_lat = (courant_max * period_ratio[:, None] * jnp.sin(angles)[None, :])[:, :, None, None]
    bending = jnp.sqrt(period_ratio)
    face_sin = jnp.sin(face_angles)[:, None, None]
    face_cos = jnp.cos(face_angles)[:, None, None]
    weight_late = hour_fraction[0]
    wind_now = (1.0 - weight_late) * atm_wind[0] + weight_late * atm_wind[1]
    packed = wind_now[:, send_cells[0]]
    received = lax.all_to_all(packed, "lon", split_axis=1, concat_axis=1, tiled=True)
    picked = received[:, recv_slots]
    surface_wind = jnp.sum(recv_weights[None] * picked, axis=1)
    density = spectrum
    padded = padded_2(density, (("lon", 2),), 2, True)
    density = (density - transport(padded, courant_lon, 2)) * sea_frac
    padded = padded_2(density, (("lat", 3),), 2, False)
    density = (density - transport(padded, courant_lat, 3)) * sea_frac
    face_speed = bending[:, None, None, None] * (
        refraction[0][None, None] * face_sin[None] - refraction[1][None, None] * face_cos[None]
    )
    next_dir = jnp.roll(density, -1, axis=1)
    face_flux = jnp.maximum(face_speed, 0.0) * density + jnp.minimum(face_speed, 0.0) * next_dir
    refracted = density - (face_flux - jnp.roll(face_flux, 1, axis=1))
    energy = jnp.mean(refracted, axis=(0, 1))
    energy_ratio = energy / energy_ref
    damping = energy_ratio * energy_ratio
    projected = (
        surface_wind[0][None] * jnp.cos(angles)[:, None, None]
        + surface_wind[1][None] * jnp.sin(angles)[:, None, None]
    )
    rel_freq = (frequencies / frequencies[freq_count - 1])[:, None, None, None]
    slowness = (2.0 * math.pi * frequencies / gravity)[:, None, None, None]
    growth = input_rate * rel_freq * jnp.maximum(projected[None] * slowness - 1.0, 0.0)
    decay_rate = damping_rate * rel_freq * damping[None, None]
    spectrum_next = refracted * jnp.exp(growth - decay_rate)
    return (spectrum_next, surface_wind)


def solution(mesh):
    in_specs = (
        P(None, None, "lon", "lat"),
        P("lon", "lat"),
        P(None, "lon", "lat"),
        P(None, None, ("lon", "lat")),
        P(),
        P(("lon", "lat"), None),
        P(None, "lon", "lat"),
        P(None, "lon", "lat"),
    )
    out_specs = (P(None, None, "lon", "lat"), P(None, "lon", "lat"))
    return jax.shard_map(local, mesh=mesh, in_specs=in_specs, out_specs=out_specs, check_vma=False)
```

profile of v0, /device:TPU:0, one launch (start us, length us, event | category | flops | bytes accessed | tf_op | source)
XLA Modules:
  0.0 234.3 jit_solution(7985758324481402877)
XLA Ops:
  0.6 0.0 copy-start.1
  0.6 0.0 copy-start.5
  0.7 0.0 copy-start.7
  0.7 0.0 copy-start.4
  0.7 0.0 copy-start.3
  0.7 3.8 %fusion.40 = (f32[36,36,2,128]{3,2,1,0:T(2,128)S(1)}, f32[36,36,2,128]{3,2,1,0:T(2,128)S(1)}) fusion(f32[36,36,4,128]{3,2,1,0:T(4,128)} %param.8), kind=kLoop, calls=%fused_computation.89 | loop fusion | bytes 5308416 | tf_op jit(solution)/shard_map/slice | solution.py:22
  4.5 0.0 copy-start.6
  4.5 0.0 copy-start.2
  4.5 1.2 copy.98
  5.8 3.0 %collective-permute-start = (f32[36,36,2,128]{3,1,2,0:T(8,128)}, f32[36,36,2,128]{3,1,2,0:T(8,128)}, u32[]{:S(2)}, u32[]{:S(2)}) collective-permute-start(f32[36,36,2,128]{3,1,2,0:T(8,128)} %copy.98), channel_id=1, source_target_pairs={{0,4},{4,8},{8,12},{12,16},{16,20},{20,24},{24,28},{28,0},{1,5},{5... | collective-permute-start | bytes 3981320 | tf_op jit(solution)/shard_map/ppermute | solution.py:24
  8.7 1.2 copy.99
  10.0 3.0 %collective-permute-start.1 = (f32[36,36,2,128]{3,1,2,0:T(8,128)}, f32[36,36,2,128]{3,1,2,0:T(8,128)}, u32[]{:S(2)}, u32[]{:S(2)}) collective-permute-start(f32[36,36,2,128]{3,1,2,0:T(8,128)} %copy.99), channel_id=1, source_target_pairs={{4,0},{8,4},{12,8},{16,12},{20,16},{24,20},{28,24},{0,28},{5,1},{9... | collective-permute-start | bytes 3981320 | tf_op jit(solution)/shard_map/ppermute | solution.py:25
  13.7 0.0 copy-done.5
  13.7 0.1 copy.93
  13.8 0.0 copy-done.7
  13.8 0.7 gather_fusion
  14.5 0.7 copy.94
  15.2 3.3 %all-to-all-start = ((f32[2,8,24]{2,0,1:T(2,128)}), f32[2,8,24]{2,0,1:T(2,128)S(1)}, u32[]{:S(2)}, u32[]{:S(2)}) async-start(f32[2,8,24]{2,0,1:T(2,128)} %copy.94), calls=%async_computation | async-start | bytes 16384 | tf_op jit(solution)/shard_map/all_to_all | solution.py:75
  18.6 0.1 fusion.34
  18.7 0.0 copy-done.4
  18.7 0.6 slice.115
  19.3 0.7 broadcast_multiply_fusion.3
  20.0 0.1 multiply_compare_fusion
  20.1 0.0 copy-done.3
  20.1 0.1 broadcast_multiply_fusion.1
  20.2 0.2 multiply_subtract_fusion
  20.4 0.0 copy-done.1
  20.4 6.9 %copy.92 = f32[36,36,4,128]{1,0,3,2:T(8,128)} copy(f32[36,36,4,128]{3,2,1,0:T(4,128)S(1)} %copy-done.1) | data formatting | bytes 5308416 | tf_op args[0]
  27.3 0.0 copy-done.6
  27.3 48.4 %all-to-all-done = f32[2,8,24]{2,0,1:T(2,128)S(1)} async-done(((f32[2,8,24]{2,0,1:T(2,128)}), f32[2,8,24]{2,0,1:T(2,128)S(1)}, u32[]{:S(2)}, u32[]{:S(2)}) %all-to-all-start) | async-done | bytes 1568 | tf_op jit(solution)/shard_map/all_to_all | solution.py:75
  75.7 0.1 copy.95
  75.8 5.5 %gather_fusion.1 = f32[2048,2]{1,0:T(8,128)S(1)} fusion(f32[2,192]{0,1:T(8,128)S(1)} %bitcast.27, s32[2048]{0:T(1024)S(1)} %broadcast_clamp_fusion), kind=kCustom, calls=%fused_computation.1 | custom fusion | bytes 40960 | tf_op jit(solution)/shard_map/gather | solution.py:76
  81.3 0.0 copy-done.2
  81.3 0.3 multiply_reduce_fusion
  81.7 0.3 slice_reduce_fusion.1
  82.0 0.0 collective-permute-done
  82.0 5.2 %copy.87 = f32[36,36,2,128]{1,0,3,2:T(8,128)} copy(f32[36,36,2,128]{3,1,2,0:T(8,128)} %collective-permute-done) | data formatting | bytes 2654208 | tf_op jit(solution)/shard_map/ppermute | solution.py:24
  87.2 0.0 collective-permute-done.1
  87.2 5.0 %copy.91 = f32[36,36,2,128]{1,0,3,2:T(8,128)} copy(f32[36,36,2,128]{3,1,2,0:T(8,128)} %collective-permute-done.1) | data formatting | bytes 2654208 | tf_op jit(solution)/shard_map/ppermute | solution.py:25
  92.2 23.2 %fusion.6 = f32[36,36,5,128]{1,0,3,2:T(8,128)} fusion(f32[36,36,2,128]{1,0,3,2:T(8,128)} %copy.91, f32[36,36,4,128]{1,0,3,2:T(8,128)} %copy.92, f32[36,36,2,128]{1,0,3,2:T(8,128)} %copy.87, f32[36,36]{1,0:T(8,128)S(1)} %get-tuple-element.31, f32[36,36]{1,0:T(8,128)S(1)} %get-tuple-element.30, f32[36,36]{1,0:T(8,128)S(1)} %get-tuple-element.32, ...), kind=kLoop, calls=%fused_computation.15 | loop fusion | flops 13271040 | bytes 8643024 | tf_op jit(solution)/shard_map/mul | solution.py:49
  115.5 10.8 %fusion.20 = f32[36,36,4,128]{1,0,3,2:T(8,128)S(1)} fusion(f32[36,36,4,128]{1,0,3,2:T(8,128)} %copy.92, f32[36,36,5,128]{1,0,3,2:T(8,128)} %fusion.6, f32[4,128]{1,0:T(4,128)S(1)} %convert_element_type.3), kind=kLoop, calls=%fused_computation.38 | loop fusion | flops 1990656 | bytes 10618880 | tf_op jit(solution)/shard_map/mul | solution.py:80
  126.3 0.0 copy-start
  126.3 3.8 %copy-done = f32[36,36,4,128]{1,0,3,2:T(8,128)} copy-done((f32[36,36,4,128]{1,0,3,2:T(8,128)}, f32[36,36,4,128]{1,0,3,2:T(8,128)S(1)}, u32[]{:S(2)}) %copy-start) | copy-done | bytes 2654232
  130.2 1.5 collective-permute-start.2
  131.7 1.3 collective-permute-start.3
  133.0 0.2 multiply_add_fusion
  133.2 0.7 copy.97
  133.9 0.0 collective-permute-done.2
  134.0 2.5 %collective-permute-done.3 = f32[36,36,4,2]{1,0,3,2:T(8,128)S(1)} collective-permute-done((f32[36,36,4,2]{1,0,3,2:T(8,128)S(1)}, f32[36,36,4,2]{1,0,3,2:T(8,128)S(1)}, u32[]{:S(2)}, u32[]{:S(2)}) %collective-permute-start.3) | collective-permute-done | bytes 41504 | tf_op jit(solution)/shard_map/ppermute | solution.py:25
  136.5 21.1 %fusion.13 = f32[36,36,4,129]{1,0,3,2:T(8,128)} fusion(f32[36,36,4,2]{1,0,3,2:T(8,128)S(1)} %collective-permute-done.3, f32[36,36,4,128]{1,0,3,2:T(8,128)} %copy-done, f32[36,36,4,2]{1,0,3,2:T(8,128)S(1)} %collective-permute-done.2, f32[36,36]{1,0:T(8,128)S(1)} %get-tuple-element.23, f32[36,36]{1,0:T(8,128)S(1)} %get-tuple-element.24, ...), kind=kLoop, calls=%fused_computation.28 | loop fusion | flops 10699776 | bytes 5428944 | tf_op jit(solution)/shard_map/mul | solution.py:49
  157.6 10.9 %fusion.18 = f32[36,36,4,128]{1,0,3,2:T(8,128)S(1)} fusion(f32[36,36,4,128]{1,0,3,2:T(8,128)} %copy-done, f32[36,36,4,129]{1,0,3,2:T(8,128)} %fusion.13, f32[4,128]{1,0:T(4,128)S(1)} %convert_element_type.3), kind=kLoop, calls=%fused_computation.35 | loop fusion | flops 1990656 | bytes 10618880 | tf_op jit(solution)/shard_map/mul | solution.py:82
  168.5 6.6 %slice.138 = f32[36,35,4,128]{1,0,3,2:T(8,128)} slice(f32[36,36,4,128]{1,0,3,2:T(8,128)S(1)} %fusion.18), slice={[0:36], [1:36], [0:4], [0:128]} | slice | bytes 5160960 | tf_op jit(solution)/shard_map/jit(_roll_static)/slice | solution.py:86
  175.0 10.9 %fusion.15 = f32[36,36,4,128]{1,0,3,2:T(8,128)} fusion(f32[36,36,4,128]{1,0,3,2:T(8,128)S(1)} %fusion.18, f32[36,1,4,128]{1,0,3,2:T(8,128)S(1)} %bitcast.22, f32[36,35,4,128]{1,0,3,2:T(8,128)} %slice.138, f32[36,4,128]{0,2,1:T(8,128)S(1)} %multiply_subtract_fusion, f32[36]{0:T(128)S(1)} %fusion.36), kind=kLoop, calls=%fused_computation.31 | loop fusion | flops 4644864 | bytes 8036496 | tf_op jit(solution)/shard_map/add | solution.py:87
  186.0 10.6 %slice.140 = f32[36,1,4,128]{1,0,3,2:T(8,128)} slice(f32[36,36,4,128]{1,0,3,2:T(8,128)} %fusion.15), slice={[0:36], [35:36], [0:4], [0:128]} | slice | bytes 147456 | tf_op jit(solution)/shard_map/jit(_roll_static)/slice | solution.py:88
  196.5 18.3 %fusion.37 = (f32[4,128]{1,0:T(4,128)S(1)}, f32[36,36,4,128]{1,0,3,2:T(8,128)}) fusion(f32[36,36,4,128]{1,0,3,2:T(8,128)S(1)} %fusion.18, f32[36,36,4,128]{1,0,3,2:T(8,128)} %fusion.15, f32[36,35,4,128]{1,0,3,2:T(8,128)} %bitcast.23, f32[36,1,4,128]{1,0,3,2:T(8,128)} %slice.140), kind=kLoop, calls=%fused_computation.87 | loop fusion | flops 2653696 | bytes 10618880 | tf_op jit(solution)/shard_map/reduce_sum | solution.py:89
  214.8 0.1 broadcast_multiply_fusion
  215.0 11.1 %exponential_multiply_fusion = f32[36,36,4,128]{1,0,3,2:T(8,128)} fusion(f32[36,36,4,128]{1,0,3,2:T(8,128)} %get-tuple-element.15, f32[36,4,128]{0,2,1:T(8,128)S(1)} %broadcast_multiply_fusion, f32[36]{0:T(128)S(1)} %fusion.30, f32[36,4,128]{0,2,1:T(8,128)S(1)} %multiply_add_fusion, f32[36]{0:T(128)S(1)} %get-tuple-element.38), kind=kLoop, calls=%fused_computation.41 | loop fusion | flops 3981312 | bytes 5456160 | tf_op jit(solution)/shard_map/mul | solution.py:100
  226.0 8.3 %copy.96 = f32[36,36,4,128]{3,2,1,0:T(4,128)} copy(f32[36,36,4,128]{1,0,3,2:T(8,128)} %exponential_multiply_fusion) | data formatting | bytes 5308416
  (14 shorter events, 0.2 us)
Async XLA Ops:
  0.6 19.8 %copy-start.1 = (f32[36,36,4,128]{3,2,1,0:T(4,128)S(1)}, f32[36,36,4,128]{3,2,1,0:T(4,128)}, u32[]{:S(2)}) copy-start(f32[36,36,4,128]{3,2,1,0:T(4,128)} %param.8) | copy-start | bytes 7962628
  0.6 13.0 %copy-start.5 = (f32[2,2,128]{2,1,0:T(2,128)S(1)}, f32[2,2,128]{2,1,0:T(2,128)}, u32[]{:S(2)}) copy-start(f32[2,2,128]{2,1,0:T(2,128)} %param.11) | copy-start | bytes 6148
  0.7 13.2 %copy-start.7 = (s32[1,192]{1,0:T(1,128)S(1)}, s32[1,192]{1,0:T(1,128)}, u32[]{:S(2)}) copy-start(s32[1,192]{1,0:T(1,128)} %param.13) | copy-start | bytes 2308
  0.7 18.0 %copy-start.4 = (f32[2,4,128]{2,1,0:T(4,128)S(1)}, f32[2,4,128]{2,1,0:T(4,128)}, u32[]{:S(2)}) copy-start(f32[2,4,128]{2,1,0:T(4,128)} %param.10) | copy-start | bytes 12292
  0.7 19.4 %copy-start.3 = (s32[4,4,128]{2,1,0:T(4,128)S(1)}, s32[4,4,128]{2,1,0:T(4,128)}, u32[]{:S(2)}) copy-start(s32[4,4,128]{2,1,0:T(4,128)} %param.14) | copy-start | bytes 24580
  4.5 22.8 %copy-start.6 = (s32[4,128]{1,0:T(4,128)S(1)}, s32[4,128]{1,0:T(4,128)}, u32[]{:S(2)}) copy-start(s32[4,128]{1,0:T(4,128)} %param.9) | copy-start | bytes 6148
  4.5 76.8 %copy-start.2 = (f32[4,4,128]{2,1,0:T(4,128)S(1)}, f32[4,4,128]{2,1,0:T(4,128)}, u32[]{:S(2)}) copy-start(f32[4,4,128]{2,1,0:T(4,128)} %param.15) | copy-start | bytes 24580
  5.8 76.2 %collective-permute-start = (f32[36,36,2,128]{3,1,2,0:T(8,128)}, f32[36,36,2,128]{3,1,2,0:T(8,128)}, u32[]{:S(2)}, u32[]{:S(2)}) collective-permute-start(f32[36,36,2,128]{3,1,2,0:T(8,128)} %copy.98), channel_id=1, source_target_pairs={{0,4},{4,8},{8,12},{12,16},{16,20},{20,24},{24,28},{28,0},{1,5},{5... | collective-permute-start | bytes 3981320 | tf_op jit(solution)/shard_map/ppermute | solution.py:24
  10.0 77.2 %collective-permute-start.1 = (f32[36,36,2,128]{3,1,2,0:T(8,128)}, f32[36,36,2,128]{3,1,2,0:T(8,128)}, u32[]{:S(2)}, u32[]{:S(2)}) collective-permute-start(f32[36,36,2,128]{3,1,2,0:T(8,128)} %copy.99), channel_id=1, source_target_pairs={{4,0},{8,4},{12,8},{16,12},{20,16},{24,20},{28,24},{0,28},{5,1},{9... | collective-permute-start | bytes 3981320 | tf_op jit(solution)/shard_map/ppermute | solution.py:25
  15.2 60.5 %all-to-all-start = ((f32[2,8,24]{2,0,1:T(2,128)}), f32[2,8,24]{2,0,1:T(2,128)S(1)}, u32[]{:S(2)}, u32[]{:S(2)}) async-start(f32[2,8,24]{2,0,1:T(2,128)} %copy.94), calls=%async_computation | async-start | bytes 16384 | tf_op jit(solution)/shard_map/all_to_all | solution.py:75
  126.3 3.8 %copy-start = (f32[36,36,4,128]{1,0,3,2:T(8,128)}, f32[36,36,4,128]{1,0,3,2:T(8,128)S(1)}, u32[]{:S(2)}) copy-start(f32[36,36,4,128]{1,0,3,2:T(8,128)S(1)} %fusion.20) | copy-start | bytes 7962628
  130.2 3.8 %collective-permute-start.2 = (f32[36,36,4,2]{1,0,3,2:T(8,128)S(1)}, f32[36,36,4,2]{1,0,3,2:T(8,128)S(1)}, u32[]{:S(2)}, u32[]{:S(2)}) collective-permute-start(f32[36,36,4,2]{1,0,3,2:T(8,128)S(1)} %get-tuple-element.16), channel_id=1, source_target_pairs={{0,1},{1,2},{2,3},{4,5},{5,6},{6,7},{8,9},{9,10},{10,11},{12,13},{... | collective-permute-start | bytes 124424 | tf_op jit(solution)/shard_map/ppermute | solution.py:24
  131.7 4.8 %collective-permute-start.3 = (f32[36,36,4,2]{1,0,3,2:T(8,128)S(1)}, f32[36,36,4,2]{1,0,3,2:T(8,128)S(1)}, u32[]{:S(2)}, u32[]{:S(2)}) collective-permute-start(f32[36,36,4,2]{1,0,3,2:T(8,128)S(1)} %get-tuple-element.17), channel_id=1, source_target_pairs={{1,0},{2,1},{3,2},{5,4},{6,5},{7,6},{9,8},{10,9},{11,10},{13,12},{... | collective-permute-start | bytes 124424 | tf_op jit(solution)/shard_map/ppermute | solution.py:25
where the time goes:
time: 238 us; the launch traced here: 234 us
  other arithmetic  108 us (45%)
  local copies, waits for them, and re-layouts  61.5 us (26%)
  waiting for transfers between devices  50.9 us (21%)
  starting transfers between devices  12.1 us (5%)
    all_to_all x1, waiting for transfers between devices, local(): lax.all_to_all(packed, 'lon', split_axis=1, concat_axis=1, tiled=True)  48.4 us
    mul x2, other arithmetic, transport(): courant * (upwind + 0.5 * (1.0 - magnitude) * (downwind - upwind) - (1.0...  44.3 us
    unnamed x21, local copies, waits for them, and re-layouts  22.2 us
    reduce_sum x1, other arithmetic, local(): energy = jnp.mean(refracted, axis=(0, 1))  18.3 us
    mul x1, other arithmetic, local(): spectrum_next = refracted * jnp.exp(growth - decay_rate)  11.1 us
    add x1, other arithmetic, local(): jnp.maximum(face_speed, 0.0) * density  10.9 us
    mul x1, other arithmetic, local(): density = (density - transport(padded, courant_lat, 3)) * sea_frac  10.9 us
    mul x1, other arithmetic, local(): density = (density - transport(padded, courant_lon, 2)) * sea_frac  10.8 us
  transfers between devices with their start and end apart: 5, of which 2 were waited for; matrix products, arithmetic and copies ran while one was open for 10% of the time, Pallas kernels for 0%

commit v1 on v0

v1 whole, which is shorter than its diff:
```python
import math

import jax
import jax.numpy as jnp
import numpy as np
from jax import lax
from jax.experimental import pallas as pl
from jax.experimental.pallas import tpu as pltpu
from jax.sharding import PartitionSpec as P

base_freq = 0.035
freq_step = 1.1
courant_max = 0.9
gravity = 9.81
input_rate = 0.05
damping_rate = 0.8
energy_ref = 0.5

F32 = jnp.float32
FREQS = 36
DIRS = 36
CELLS = 4
LANES = 128
ROWS = DIRS * CELLS
BLOCKS = (0, 8, 16, 24, 28)
GROUP = 4
HALO = DIRS + DIRS // 2
NEAR_SPLIT = 16
FAR = DIRS // 2
PACK = 6
CHUNKS = (4, 12, 16, 4)
VMEM = 48 * 1024 * 1024

freqs = base_freq * freq_step ** np.arange(FREQS, dtype=np.float64)
spacing = 2.0 * math.pi / DIRS
theta = (np.arange(DIRS) + 0.5) * spacing
phi = (np.arange(DIRS) + 1.0) * spacing
ratio = base_freq / freqs
SCALARS = np.stack(
    [
        courant_max * ratio,
        np.sqrt(ratio),
        input_rate * freqs / freqs[-1],
        2.0 * math.pi * freqs / gravity,
        freqs / freqs[-1],
    ]
).astype(np.float32)
ANGLES = np.broadcast_to(
    np.stack(
        [np.abs(np.cos(theta)), np.abs(np.sin(theta)), np.cos(theta), np.sin(theta), np.sin(phi), np.cos(phi)]
    )[:, :, None],
    (6, DIRS, LANES),
).astype(np.float32)


def stencil(a):
    one_m = 1.0 - a * a
    beyond = a * one_m * (-1.0 / 6.0)
    half = a * (0.5 - 0.5 * a)
    down = half + beyond
    up = a - half - 2.0 * beyond
    return beyond, up - beyond, 1.0 + down - up, -down


def packed_weights():
    out = np.zeros((5, FREQS // PACK, 8, LANES), np.float64)
    for k in range(FREQS):
        for b, j0 in enumerate(BLOCKS):
            c = courant_max * ratio[k] * np.cos(theta[j0 : j0 + 8])
            far, up, own, down = stencil(np.abs(c))
            zero = np.zeros(8)
            pos = c > 0
            five = [
                np.where(pos, far, zero),
                np.where(pos, up, down),
                own,
                np.where(pos, down, up),
                np.where(pos, zero, far),
            ]
            lane = 4 * ((k % PACK) * len(BLOCKS) + b)
            for d in range(5):
                out[d, k // PACK, :, lane : lane + 4] = five[d][:, None]
    return out.astype(np.float32)


PACKED = packed_weights()


def any_spec():
    return pl.BlockSpec(memory_space=pl.ANY)


def vmem_spec():
    return pl.BlockSpec(memory_space=pltpu.VMEM)


def smem_spec():
    return pl.BlockSpec(memory_space=pltpu.SMEM)


def prep_body(first, count, x_hbm, right_ref, left_ref, xbuf, sem):
    copy = pltpu.make_async_copy(x_hbm.at[pl.ds(first, count)], xbuf, sem)
    copy.start()
    copy.wait()

    def body(i, _):
        for kk in range(GROUP):
            k = i * GROUP + kk
            base = HALO * kk
            half = FAR // 2
            for ref, near, far in ((right_ref, 3, 2), (left_ref, 0, 1)):
                for row, j, n in ((0, 0, 8), (8, 8, 8), (34, 16, 8), (42, 24, 8), (50, 32, 4)):
                    ref[i, pl.ds(base + row, n), :] = xbuf[k, pl.ds(near + 4 * j, n, stride=4), :]
                if far == 2:
                    runs = ((16, 0, 8), (24, 8, 1), (25, 27, 8), (33, 35, 1))
                else:
                    runs = ((16, 9, 8), (24, 17, 8), (32, 25, 2))
                for row, j, n in runs:
                    ref[i, pl.ds(base + row, n), :] = xbuf[k, pl.ds(far + 4 * j, n, stride=4), :]
        return 0

    lax.fori_loop(0, count // GROUP, body, 0)


def prep(x, first, count):
    shape = jax.ShapeDtypeStruct((count // GROUP, GROUP * HALO, LANES), F32)
    return pl.pallas_call(
        lambda *refs: prep_body(first, count, *refs),
        out_shape=(shape, shape),
        in_specs=[any_spec()],
        out_specs=(vmem_spec(), vmem_spec()),
        scratch_shapes=[pltpu.VMEM((count, ROWS, LANES), F32), pltpu.SemaphoreType.DMA],
        compiler_params=pltpu.CompilerParams(vmem_limit_bytes=VMEM),
        cost_estimate=pl.CostEstimate(flops=count * 1000, bytes_accessed=count * 150000, transcendentals=0),
        name="halo_rows",
    )(x)


def lane_ids():
    return lax.broadcasted_iota(jnp.int32, (8, LANES), 1)


def pack_body(x_hbm, q_ref, xbuf, sem):
    copy = pltpu.make_async_copy(x_hbm, xbuf, sem)
    copy.start()
    copy.wait()
    lane = lane_ids()
    block = lane // 4

    def body(g, _):
        for cell in range(CELLS):
            acc = jnp.zeros((8, LANES), F32)
            for r in range(PACK):
                for b, j0 in enumerate(BLOCKS):
                    at = r * len(BLOCKS) + b
                    rows = xbuf[g * PACK + r, pl.ds(cell + 4 * j0, 8, stride=4), :]
                    acc = jnp.where(block == at, pltpu.roll(rows, (4 * at + 2) % LANES, 1), acc)
            q_ref[cell, g] = acc
        return 0

    lax.fori_loop(0, FREQS // PACK, body, 0)


def pack_edges(x):
    return pl.pallas_call(
        pack_body,
        out_shape=jax.ShapeDtypeStruct((CELLS, FREQS // PACK, 8, LANES), F32),
        in_specs=[any_spec()],
        out_specs=vmem_spec(),
        scratch_shapes=[pltpu.VMEM((FREQS, ROWS, LANES), F32), pltpu.SemaphoreType.DMA],
        compiler_params=pltpu.CompilerParams(vmem_limit_bytes=VMEM),
        cost_estimate=pl.CostEstimate(flops=4000000, bytes_accessed=4000000, transcendentals=0),
        name="edge_columns",
    )(x)


def setup_tables(ang, sea, refr, wind, sea8, turn, proj):
    for cell in range(CELLS):
        row = pl.ds(cell, 1)
        sea8[cell] = jnp.broadcast_to(sea[row, :], (8, LANES))
        for j0 in BLOCKS:
            j = pl.ds(j0, 8)
            turn[cell, j, :] = refr[0, row, :] * ang[4, j, :] - refr[1, row, :] * ang[5, j, :]
            proj[cell, j, :] = wind[0, row, :] * ang[2, j, :] + wind[1, row, :] * ang[3, j, :]


def chunk_pass(
    first, count, scal, ang, x, from_west, from_east, edges, sea8, turn, proj, zs, gs, out, out_first
):
    lane = lane_ids()
    sub = lax.broadcasted_iota(jnp.int32, (8, LANES), 0)
    near_rows = (0, 8, 34, 42, 46)

    def one(i, kk, sums):
        k = first + i * GROUP + kk
        base = HALO * kk
        cour = scal[0, k]
        bend = scal[1, k]
        rate = scal[2, k]
        slow = scal[3, k]
        group = k // PACK
        at0 = (k - group * PACK) * len(BLOCKS)
        for b, j0 in enumerate(BLOCKS):
            w0, w1, w2, w3 = stencil(cour * ang[0, pl.ds(j0, 8), :])
            v0, v1, v2, v3 = stencil(cour * ang[1, pl.ds(j0, 8), :])
            cells = [x[i * GROUP + kk, pl.ds(c + 4 * j0, 8, stride=4), :] for c in range(CELLS)]
            west = from_west[i, pl.ds(base + near_rows[b], 8), :]
            east = from_east[i, pl.ds(base + near_rows[b], 8), :]
            plus = [west, *cells, east]
            minus = plus[::-1]
            if b == 0:
                far, seq = from_west[i, pl.ds(base + 16, 8), :], plus
            elif b == 2:
                far, seq = from_east[i, pl.ds(base + 23, 8), :], minus
            elif b == 4:
                far, seq = from_west[i, pl.ds(base + 26, 8), :], plus
            else:
                if b == 1:
                    pos = sub < 1
                    far_p, far_m = from_west[i, pl.ds(base + 24, 8), :], from_east[i, pl.ds(base + 15, 8), :]
                else:
                    pos = sub >= 3
                    far_p, far_m = from_west[i, pl.ds(base + 22, 8), :], from_east[i, pl.ds(base + 31, 8), :]
                far = jnp.where(pos, far_p, far_m)
                seq = [jnp.where(pos, p, m) for p, m in zip(plus, minus)]
            seq = [far, *seq]
            moved = [
                w0 * seq[c] + w1 * seq[c + 1] + w2 * seq[c + 2] + w3 * seq[c + 3] for c in range(CELLS)
            ]
            if b == 2:
                moved = moved[::-1]
            elif b in (1, 3):
                moved = [jnp.where(pos, p, m) for p, m in zip(moved, moved[::-1])]
            shift = LANES - (4 * (at0 + b) + 2)
            for c in range(CELLS):
                z = moved[c] * sea8[c]
                ghost = pltpu.roll(edges[c, group], shift, 1)
                s1 = pltpu.roll(jnp.where(lane == LANES - 1, ghost, z), 1, 1)
                n1 = pltpu.roll(jnp.where(lane == 0, ghost, z), LANES - 1, 1)
                if b <= 2:
                    s2 = pltpu.roll(jnp.where(lane >= LANES - 2, ghost, z), 2, 1)
                if b >= 2:
                    n2 = pltpu.roll(jnp.where(lane < 2, ghost, z), LANES - 2, 1)
                if b < 2:
                    up, down, far = s1, n1, s2
                elif b > 2:
                    up, down, far = n1, s1, n2
                else:
                    p = sub < 2
                    up, down = jnp.where(p, s1, n1), jnp.where(p, n1, s1)
                    far = jnp.where(p, s2, n2)
                z = (v0 * far + v1 * up + v2 * z + v3 * down) * sea8[c]
                zs[kk, c, pl.ds(8 + j0, 8), :] = z
        out_sums = []
        for c in range(CELLS):
            zs[kk, c, pl.ds(8 + DIRS, 1), :] = zs[kk, c, pl.ds(8, 1), :]
            for b, j0 in enumerate(BLOCKS):
                own = zs[kk, c, pl.ds(8 + j0, 8), :]
                nxt = zs[kk, c, pl.ds(9 + j0, 8), :]
                s = bend * turn[c, pl.ds(j0, 8), :]
                gs[kk, c, pl.ds(8 + j0, 8), :] = jnp.maximum(s, 0.0) * own + jnp.minimum(s, 0.0) * nxt
            gs[kk, c, pl.ds(7, 1), :] = gs[kk, c, pl.ds(7 + DIRS, 1), :]
            total = sums[c]
            for b, j0 in enumerate(BLOCKS):
                own = zs[kk, c, pl.ds(8 + j0, 8), :]
                flux = gs[kk, c, pl.ds(8 + j0, 8), :]
                prev = gs[kk, c, pl.ds(7 + j0, 8), :]
                refracted = own - (flux - prev)
                total = total + (jnp.where(sub >= 4, refracted, 0.0) if b == 4 else refracted)
                growth = rate * jnp.maximum(proj[c, pl.ds(j0, 8), :] * slow - 1.0, 0.0)
                out[out_first + i * GROUP + kk, pl.ds(c + 4 * j0, 8, stride=4), :] = refracted * jnp.exp(growth)
            out_sums.append(total)
        return tuple(out_sums)

    def body(i, sums):
        for kk in range(GROUP):
            sums = one(i, kk, sums)
        return sums

    zero = jnp.zeros((8, LANES), F32)
    return lax.fori_loop(0, count // GROUP, body, (zero,) * CELLS)


def merge_edges(south_ref, north_ref, edges):
    pick = lane_ids() % 4 < 2
    for c in range(CELLS):
        for g in range(FREQS // PACK):
            edges[c, g] = jnp.where(pick, south_ref[c, g], north_ref[c, g])


def main_body(
    first, count, scal, ang, x_hbm, west, east, south, north, sea, refr, wind, out, energy,
    xbuf, edges, sea8, turn, proj, zs, gs, sem,
):
    copy = pltpu.make_async_copy(x_hbm.at[pl.ds(first, count)], xbuf, sem)
    copy.start()
    setup_tables(ang, sea, refr, wind, sea8, turn, proj)
    merge_edges(south, north, edges)
    copy.wait()
    sums = chunk_pass(
        first, count, scal, ang, xbuf, west, east, edges, sea8, turn, proj, zs, gs, out, 0
    )
    for c in range(CELLS):
        energy[c] = sums[c]


def pass_scratch():
    return [
        pltpu.VMEM((CELLS, FREQS // PACK, 8, LANES), F32),
        pltpu.VMEM((CELLS, 8, LANES), F32),
        pltpu.VMEM((CELLS, DIRS, LANES), F32),
        pltpu.VMEM((CELLS, DIRS, LANES), F32),
        pltpu.VMEM((GROUP, CELLS, 56, LANES), F32),
        pltpu.VMEM((GROUP, CELLS, 56, LANES), F32),
    ]


def main_chunk(first, count, x, west, east, south, north, sea, refr, wind):
    return pl.pallas_call(
        lambda *refs: main_body(first, count, *refs),
        out_shape=(
            jax.ShapeDtypeStruct((count, ROWS, LANES), F32),
            jax.ShapeDtypeStruct((CELLS, 8, LANES), F32),
        ),
        in_specs=[smem_spec(), vmem_spec(), any_spec()] + [vmem_spec()] * 7,
        out_specs=(vmem_spec(), vmem_spec()),
        scratch_shapes=[pltpu.VMEM((count, ROWS, LANES), F32), *pass_scratch(), pltpu.SemaphoreType.DMA],
        compiler_params=pltpu.CompilerParams(vmem_limit_bytes=VMEM),
        cost_estimate=pl.CostEstimate(
            flops=count * 1500000, bytes_accessed=count * 300000, transcendentals=count * 18432
        ),
        name="chunk",
    )(SCALARS, ANGLES, x, west, east, south, north, sea, refr, wind)


def tail_body(
    sizes, scal, ang, x_hbm, west, east, south, north, sea, refr, wind, *rest
):
    done = len(sizes) - 1
    parts, energies = rest[:done], rest[done : 2 * done]
    out_hbm = rest[2 * done]
    xbuf, obuf, edges, sea8, turn, proj, zs, gs, sem, part_sem, out_sem = rest[2 * done + 1 :]
    count = sizes[-1]
    first = FREQS - count
    copy = pltpu.make_async_copy(x_hbm.at[pl.ds(first, count)], xbuf, sem)
    copy.start()
    loads, at = [], 0
    for n, size in enumerate(sizes[:-1]):
        loads.append(pltpu.make_async_copy(parts[n], obuf.at[pl.ds(at, size)], part_sem.at[n]))
        loads[-1].start()
        at += size
    setup_tables(ang, sea, refr, wind, sea8, turn, proj)
    merge_edges(south, north, edges)
    copy.wait()
    sums = chunk_pass(
        first, count, scal, ang, xbuf, west, east, edges, sea8, turn, proj, zs, gs, obuf, first
    )
    sub = lax.broadcasted_iota(jnp.int32, (8, LANES), 0)
    pattern = jnp.zeros((8, LANES), F32)
    for c in range(CELLS):
        total = sums[c]
        for energy in energies:
            total = total + energy[c]
        mean = jnp.sum(total, axis=0, keepdims=True) * (1.0 / (FREQS * DIRS))
        level = mean * (1.0 / energy_ref)
        pattern = jnp.where(sub % CELLS == c, damping_rate * (level * level), pattern)
    for load in loads:
        load.wait()
    stores = []
    step = FREQS // 6
    for n in range(6):
        def body(i, _):
            k = n * step + i
            scale = jnp.exp(-(scal[4, k] * pattern))
            for r in range(0, ROWS, 8):
                obuf[k, pl.ds(r, 8), :] = obuf[k, pl.ds(r, 8), :] * scale
            return 0

        lax.fori_loop(0, step, body, 0)
        span = pl.ds(n * step, step)
        stores.append(pltpu.make_async_copy(obuf.at[span], out_hbm.at[span], out_sem.at[n]))
        stores[-1].start()
    for store in stores:
        store.wait()


def tail_chunk(sizes, x, west, east, south, north, sea, refr, wind, parts, energies):
    count = sizes[-1]
    done = len(sizes) - 1
    return pl.pallas_call(
        lambda *refs: tail_body(sizes, *refs),
        out_shape=jax.ShapeDtypeStruct((FREQS, ROWS, LANES), F32),
        in_specs=[smem_spec(), vmem_spec(), any_spec()]
        + [vmem_spec()] * 7
        + [any_spec()] * done
        + [vmem_spec()] * done,
        out_specs=any_spec(),
        scratch_shapes=[
            pltpu.VMEM((count, ROWS, LANES), F32),
            pltpu.VMEM((FREQS, ROWS, LANES), F32),
            *pass_scratch(),
            pltpu.SemaphoreType.DMA,
            pltpu.SemaphoreType.DMA((done,)),
            pltpu.SemaphoreType.DMA((6,)),
        ],
        compiler_params=pltpu.CompilerParams(vmem_limit_bytes=VMEM),
        cost_estimate=pl.CostEstimate(
            flops=count * 1500000, bytes_accessed=6000000, transcendentals=count * 18432
        ),
        name="last_chunk",
    )(SCALARS, ANGLES, x, west, east, south, north, sea, refr, wind, *parts, *energies)


def ring(axis, wrap):
    size = lax.axis_size(axis)
    up = [(i, (i + 1) % size) for i in range(size if wrap else size - 1)]
    return up, [(j, i) for i, j in up]


def local(
    spectrum, sea_mask, refraction, atm_wind, hour_fraction, send_cells, recv_slots, recv_weights
):
    east_way, west_way = ring("lon", True)
    north_way, south_way = ring("lat", False)
    x = spectrum.reshape(FREQS, ROWS, LANES)
    sea = sea_mask.astype(F32)

    firsts = [sum(CHUNKS[:n]) for n in range(len(CHUNKS))]
    halos = []
    for first, count in zip(firsts, CHUNKS):
        to_east, to_west = prep(x, first, count)
        halos.append((lax.ppermute(to_east, "lon", east_way), lax.ppermute(to_west, "lon", west_way)))

    late = hour_fraction[0]
    wind_now = (1.0 - late) * atm_wind[0] + late * atm_wind[1]
    packed = wind_now[:, send_cells[0]]
    received = lax.all_to_all(packed, "lon", split_axis=1, concat_axis=1, tiled=True)
    picked = received[:, recv_slots]
    surface_wind = jnp.sum(recv_weights[None] * picked, axis=1)

    q = pack_edges(x)
    q_west = lax.ppermute(q[2:], "lon", east_way)
    q_east = lax.ppermute(q[:2], "lon", west_way)
    ext = jnp.concatenate([q_west, q, q_east], axis=0)
    moved = sum(PACKED[d][None] * ext[d : d + CELLS] for d in range(5))
    sea_edge = jnp.tile(jnp.concatenate([sea[:, -2:], sea[:, :2]], axis=1), (1, LANES // 4))
    moved = moved * sea_edge[:, None, None, :]
    south = lax.ppermute(moved, "lat", north_way)
    north = lax.ppermute(moved, "lat", south_way)

    parts, energies = [], []
    for n, (first, count) in enumerate(zip(firsts, CHUNKS)):
        west, east = halos[n]
        if n < len(CHUNKS) - 1:
            part, energy = main_chunk(
                first, count, x, west, east, south, north, sea, refraction, surface_wind
            )
            parts.append(part)
            energies.append(energy)
        else:
            out = tail_chunk(
                CHUNKS, x, west, east, south, north, sea, refraction, surface_wind, parts, energies
            )
    return (out.reshape(spectrum.shape), surface_wind)


def solution(mesh):
    in_specs = (
        P(None, None, "lon", "lat"),
        P("lon", "lat"),
        P(None, "lon", "lat"),
        P(None, None, ("lon", "lat")),
        P(),
        P(("lon", "lat"), None),
        P(None, "lon", "lat"),
        P(None, "lon", "lat"),
    )
    out_specs = (P(None, None, "lon", "lat"), P(None, "lon", "lat"))
    return jax.shard_map(local, mesh=mesh, in_specs=in_specs, out_specs=out_specs, check_vma=False)
```

time: 238 us -> 104 us (0.44)
  other arithmetic: 108 us -> 6.03 us
  waiting for transfers between devices: 50.9 us -> 0.03 us
  local copies, waits for them, and re-layouts: 61.5 us -> 19.5 us
  Pallas kernels: 0 us -> 37.9 us
  starting transfers between devices: 12.1 us -> 37.1 us
    mul x11 -> x1, other arithmetic: 78 us -> 1.57 us  [local(): moved = moved * sea_edge[:, None, None, :]]
    all_to_all x1, waiting for transfers between devices: 48.4 us -> 0.01 us  [local(): lax.all_to_all(packed, 'lon', split_axis=1, concat_axis=1, tiled=True)]
    pallas_call x0 -> x9, Pallas kernels: none -> 37.9 us  [the longest x3 28.2 us: main_chunk(): pl.pallas_call(lambda *refs: main_body(first, count, *refs), out_shape=(j...]
    slice x6 -> x2, local copies, waits for them, and re-layouts: 21.9 us -> 0.71 us  [the longest x1 0.64 us: local(): q_west = lax.ppermute(q[2:], 'lon', east_way)]
    ppermute x4 -> x12, starting transfers between devices: 8.84 us -> 29.8 us  [the longest x4 22.4 us: local(): lax.ppermute(to_west, 'lon', west_way)]
    reduce_sum x1 -> x0, other arithmetic: 18.3 us -> none  [local(): energy = jnp.mean(refracted, axis=(0, 1))]
    unnamed x21 -> x28, local copies, waits for them, and re-layouts: 22.2 us -> 6.19 us
    add x3 -> x1, other arithmetic: 11.1 us -> 0.7 us  [local(): wind_now = (1.0 - late) * atm_wind[0] + late * atm_wind[1]]
  transfers between devices with their start and end apart: 5 -> 13, of which waited for: 2 -> 0; matrix products, arithmetic and copies ran while one was open for 10% -> 16% of each run, Pallas kernels for 0% -> 31%
where the time goes in v1:
time: 104 us; the launch traced here: 102 us
  Pallas kernels  37.9 us (36%)
  starting transfers between devices  37.1 us (36%)
  local copies, waits for them, and re-layouts  19.5 us (19%)
  other arithmetic  6.03 us (6%)
  between operations  1.55 us (1%)
    pallas_call x3, Pallas kernels, main_chunk(): pl.pallas_call(lambda *refs: main_body(first, count, *refs), out_shape=(j...  28.2 us
    ppermute x4, starting transfers between devices, local(): lax.ppermute(to_west, 'lon', west_way)  22.4 us
    gather x1, local copies, waits for them, and re-layouts, local(): picked = received[:, recv_slots]  8.52 us
    all_to_all x1, starting transfers between devices, local(): lax.all_to_all(packed, 'lon', split_axis=1, concat_axis=1, tiled=True)  7.28 us
    pallas_call x1, Pallas kernels, tail_chunk(): pl.pallas_call(lambda *refs: tail_body(sizes, *refs), out_shape=jax.Shape...  6.21 us
    unnamed x28, local copies, waits for them, and re-layouts  6.19 us
    ppermute x1, starting transfers between devices, local(): q_east = lax.ppermute(q[:2], 'lon', west_way)  2.7 us
    reduce_sum x1, other arithmetic, local(): surface_wind = jnp.sum(recv_weights[None] * picked, axis=1)  2.28 us
  transfers between devices with their start and end apart: 13, of which 0 were waited for; matrix products, arithmetic and copies ran while one was open for 16% of the time, Pallas kernels for 31%

profile of v1, /device:TPU:0, one launch (start us, length us, event | category | flops | bytes accessed | tf_op | source)
XLA Modules:
  0.0 102.2 jit_solution(8393766290161473478)
XLA Ops:
  1.3 0.7 compare_select_fusion.1
  2.0 0.7 add_bitcast_fusion
  2.7 0.1 copy.32
  2.8 0.7 gather_fusion
  3.5 0.7 copy.33
  4.2 7.3 %all-to-all-start = ((f32[2,8,24]{2,0,1:T(2,128)}), f32[2,8,24]{2,0,1:T(2,128)}, u32[]{:S(2)}, u32[]{:S(2)}) async-start(f32[2,8,24]{2,0,1:T(2,128)} %copy.33), calls=%async_computation | async-start | bytes 16384 | tf_op jit(solution)/shard_map/all_to_all | solution.py:437
  11.5 1.7 %copy-done = f32[36,36,4,128]{3,2,1,0:T(4,128)S(1)} copy-done((f32[36,36,4,128]{3,2,1,0:T(4,128)S(1)}, f32[36,36,4,128]{3,2,1,0:T(4,128)}, u32[]{:S(2)}) %copy-start) | copy-done | bytes 2654232
  13.2 1.4 %edge_columns.1 = f32[4,6,8,128]{3,2,1,0:T(8,128)S(1)} custom-call(f32[36,144,128]{2,1,0:T(8,128)S(1)} %bitcast.17), custom_call_target="tpu_custom_call" | custom-call | flops 4000000 | bytes 4000000 | tf_op jit(solution)/shard_map/edge_columns/pallas_call | solution.py:165
  14.6 0.6 fusion.11
  15.3 2.0 %collective-permute-start.2 = (f32[2,6,8,128]{3,2,1,0:T(8,128)}, f32[2,6,8,128]{3,2,1,0:T(8,128)}, u32[]{:S(2)}, u32[]{:S(2)}) collective-permute-start(f32[2,6,8,128]{3,2,1,0:T(8,128)} %get-tuple-element.30), channel_id=1, source_target_pairs={{0,4},{4,8},{8,12},{12,16},{16,20},{20,24},{24,28},{28,0},{1,5},{5... | collective-permute-start | bytes 147464 | tf_op jit(solution)/shard_map/ppermute | solution.py:442
  17.3 2.7 %collective-permute-start.3 = (f32[2,6,8,128]{3,2,1,0:T(8,128)}, f32[2,6,8,128]{3,2,1,0:T(8,128)}, u32[]{:S(2)}, u32[]{:S(2)}) collective-permute-start(f32[2,6,8,128]{3,2,1,0:T(8,128)} %get-tuple-element.31), channel_id=1, source_target_pairs={{4,0},{8,4},{12,8},{16,12},{20,16},{24,20},{28,24},{0,28},{5,1},{9... | collective-permute-start | bytes 147464 | tf_op jit(solution)/shard_map/ppermute | solution.py:443
  20.0 0.7 halo_rows.5
  20.7 0.1 collective-permute-start.6
  20.8 0.0 copy-start.1
  20.8 4.7 %collective-permute-start.7 = (f32[1,216,128]{2,1,0:T(8,128)S(1)}, f32[1,216,128]{2,1,0:T(8,128)}, u32[]{:S(2)}, u32[]{:S(2)}) collective-permute-start(f32[1,216,128]{2,1,0:T(8,128)S(1)} %get-tuple-element.19), channel_id=1, source_target_pairs={{4,0},{8,4},{12,8},{16,12},{20,16},{24,20},{28,24},{0,28},{5,1},{9... | collective-permute-start | bytes 331784 | tf_op jit(solution)/shard_map/ppermute | solution.py:432
  25.5 1.0 halo_rows.6
  26.5 0.0 copy-start.10
  26.5 0.7 copy-done.10
  27.2 0.0 collective-permute-start.8
  27.2 0.0 copy-done.13
  27.2 0.1 fusion.12
  27.3 0.1 pad_maximum_fusion.2
  27.4 0.3 halo_rows.7
  27.7 0.8 copy-done.8
  28.5 0.8 copy-done.9
  29.3 0.1 tile.9
  29.4 0.0 collective-permute-done.2
  29.4 0.1 collective-permute-start.10
  29.5 0.0 collective-permute-done.3
  29.5 4.8 %collective-permute-start.11 = (f32[4,216,128]{2,1,0:T(8,128)}, f32[4,216,128]{2,1,0:T(8,128)}, u32[]{:S(2)}, u32[]{:S(2)}) collective-permute-start(f32[4,216,128]{2,1,0:T(8,128)} %copy-done.8), channel_id=1, source_target_pairs={{4,0},{8,4},{12,8},{16,12},{20,16},{24,20},{28,24},{0,28},{5,1},{9... | collective-permute-start | bytes 1327112 | tf_op jit(solution)/shard_map/ppermute | solution.py:432
  34.3 1.6 %fusion.4 = f32[4,6,8,128]{3,2,1,0:T(8,128)} fusion(f32[4,6,8,128]{3,2,1,0:T(8,128)S(1)} %edge_columns.1, f32[2,6,8,128]{3,2,1,0:T(8,128)} %collective-permute-done.3, f32[2,6,8,128]{3,2,1,0:T(8,128)} %collective-permute-done.2, f32[4,128]{1,0:T(4,128)S(1)} %tile.9, f32[6,8,128]{2,1,0:T(8,128)} %constant.42, f32[6,8,128]{2,1,0:T(8,128)} %constant.41, ...), kind=kLoop, calls=%fused_computation.11 | loop fusion | flops 344064 | bytes 419840 | tf_op jit(solution)/shard_map/mul | solution.py:447
  35.8 0.0 collective-permute-done.6.refs_3_
  35.8 1.3 %collective-permute-start.5 = (f32[4,6,8,128]{3,2,1,0:T(8,128)}, f32[4,6,8,128]{3,2,1,0:T(8,128)S(1)}, u32[]{:S(2)}, u32[]{:S(2)}) collective-permute-start(f32[4,6,8,128]{3,2,1,0:T(8,128)} %fusion.4), channel_id=1, source_target_pairs={{1,0},{2,1},{3,2},{5,4},{6,5},{7,6},{9,8},{10,9},{11,10},{13,12},{... | collective-permute-start | bytes 294920 | tf_op jit(solution)/shard_map/ppermute | solution.py:449
  37.1 0.7 compare_select_fusion
  37.8 0.0 collective-permute-done.7.refs_4_
  37.8 8.2 %collective-permute-start.9 = (f32[3,216,128]{2,1,0:T(8,128)}, f32[3,216,128]{2,1,0:T(8,128)}, u32[]{:S(2)}, u32[]{:S(2)}) collective-permute-start(f32[3,216,128]{2,1,0:T(8,128)} %copy-done.10), channel_id=1, source_target_pairs={{4,0},{8,4},{12,8},{16,12},{20,16},{24,20},{28,24},{0,28},{5,1},{9... | collective-permute-start | bytes 995336 | tf_op jit(solution)/shard_map/ppermute | solution.py:432
  46.0 0.0 collective-permute-done.5.refs_6_
  46.0 1.3 %collective-permute-start.4 = (f32[4,6,8,128]{3,2,1,0:T(8,128)}, f32[4,6,8,128]{3,2,1,0:T(8,128)S(1)}, u32[]{:S(2)}, u32[]{:S(2)}) collective-permute-start(f32[4,6,8,128]{3,2,1,0:T(8,128)} %fusion.4), channel_id=1, source_target_pairs={{0,1},{1,2},{2,3},{4,5},{5,6},{6,7},{8,9},{9,10},{10,11},{12,13},{... | collective-permute-start | bytes 294920 | tf_op jit(solution)/shard_map/ppermute | solution.py:448
  47.3 0.1 halo_rows.4
  47.5 0.6 copy-done.11
  48.1 0.6 copy-done.12
  48.7 0.0 all-to-all-done
  48.7 1.4 %copy.34 = f32[2,8,24]{0,2,1:T(8,128)} copy(f32[2,8,24]{2,0,1:T(2,128)} %all-to-all-done) | data formatting | bytes 3072 | tf_op jit(solution)/shard_map/all_to_all | solution.py:437
  50.2 8.5 %gather_fusion.1 = f32[2048,2]{1,0:T(8,128)} fusion(f32[2,192]{0,1:T(8,128)} %bitcast.33, s32[2048]{0:T(1024)S(1)} %broadcast_clamp_fusion), kind=kCustom, calls=%fused_computation.1 | custom fusion | bytes 40960 | tf_op jit(solution)/shard_map/gather | solution.py:438
  58.7 0.0 collective-permute-done.4.refs_5_
  58.7 0.0 collective-permute-start
  58.7 0.0 collective-permute-done.8.refs_3_
  58.7 4.7 %collective-permute-start.1 = (f32[1,216,128]{2,1,0:T(8,128)}, f32[1,216,128]{2,1,0:T(8,128)}, u32[]{:S(2)}, u32[]{:S(2)}) collective-permute-start(f32[1,216,128]{2,1,0:T(8,128)} %copy-done.11), channel_id=1, source_target_pairs={{4,0},{8,4},{12,8},{16,12},{20,16},{24,20},{28,24},{0,28},{5,1},{9... | collective-permute-start | bytes 331784 | tf_op jit(solution)/shard_map/ppermute | solution.py:432
  63.4 2.3 %multiply_reduce_fusion = f32[4,128,2]{2,1,0:T(8,128)} fusion(f32[4,4,128,2]{3,2,1,0:T(8,128)} %bitcast.32, f32[4,4,128]{2,1,0:T(4,128)} %param.22), kind=kLoop, calls=%fused_computation.2 | loop fusion | flops 7168 | bytes 28672 | tf_op jit(solution)/shard_map/reduce_sum | solution.py:439
  65.7 1.1 %copy.35 = f32[4,128,2]{1,0,2:T(4,128)S(1)} copy(f32[4,128,2]{2,1,0:T(8,128)} %multiply_reduce_fusion) | data formatting | bytes 8192 | tf_op jit(solution)/shard_map/reduce_sum | solution.py:439
  66.8 0.0 copy-done.2
  66.8 0.0 copy-done.6
  66.8 0.0 copy-done.7
  66.8 0.0 copy-start.4
  66.8 0.9 copy-done.4
  67.7 4.3 %chunk.3 = (f32[4,144,128]{2,1,0:T(8,128)S(1)}, f32[4,8,128]{2,1,0:T(8,128)S(1)}) custom-call(f32[5,36]{1,0:T(8,128)S(1)} %copy-done.7, f32[6,36,128]{2,1,0:T(8,128)S(1)} %copy-done.2, f32[36,144,128]{2,1,0:T(8,128)S(1)} %bitcast.22, f32[1,216,128]{2,1,0:T(8,128)S(1)} %copy-done.4, f32[1,216,128]{2,1,0:T(8,128)} %collective-permute-done.7.refs_4_, ...), custom_call_target="tpu_custom_call" | custom-call | flops 6000000 | bytes 1200000 | tf_op jit(solution)/shard_map/chunk/pallas_call | solution.py:319
  72.0 0.0 collective-permute-done.9.refs_4_
  72.0 10.4 %chunk.4 = (f32[12,144,128]{2,1,0:T(8,128)S(1)}, f32[4,8,128]{2,1,0:T(8,128)S(1)}) custom-call(f32[5,36]{1,0:T(8,128)S(1)} %copy-done.7, f32[6,36,128]{2,1,0:T(8,128)S(1)} %copy-done.2, f32[36,144,128]{2,1,0:T(8,128)S(1)} %bitcast.23, f32[3,216,128]{2,1,0:T(8,128)} %collective-permute-done.8.refs_3_, f32[3,216,128]{2,1,0:T(8,128)} %collective-permute-done.9.refs_4_, ...), custom_call_target="tpu_custom_call" | custom-call | flops 18000000 | bytes 3600000 | tf_op jit(solution)/shard_map/chunk/pallas_call | solution.py:319
  82.4 0.0 collective-permute-done.10.refs_3_
  82.4 0.0 collective-permute-done.11.refs_4_
  82.4 13.5 %chunk.5 = (f32[16,144,128]{2,1,0:T(8,128)S(1)}, f32[4,8,128]{2,1,0:T(8,128)S(1)}) custom-call(f32[5,36]{1,0:T(8,128)S(1)} %copy-done.7, f32[6,36,128]{2,1,0:T(8,128)S(1)} %copy-done.2, f32[36,144,128]{2,1,0:T(8,128)S(1)} %bitcast.24, f32[4,216,128]{2,1,0:T(8,128)S(1)} %collective-permute-done.10.refs_3_, f32[4,216,128]{2,1,0:T(8,128)} %collective-permute-done.11.refs_4_, ...), custom_call_target="tpu_custom_call" | custom-call | flops 24000000 | bytes 4800000 | tf_op jit(solution)/shard_map/chunk/pallas_call | solution.py:319
  95.9 0.0 collective-permute-done.refs_3_
  95.9 0.0 collective-permute-done.1.refs_4_
  95.9 6.2 %last_chunk.1 = f32[36,144,128]{2,1,0:T(8,128)} custom-call(f32[5,36]{1,0:T(8,128)S(1)} %copy-done.7, f32[6,36,128]{2,1,0:T(8,128)S(1)} %copy-done.2, f32[36,144,128]{2,1,0:T(8,128)S(1)} %bitcast.25, f32[1,216,128]{2,1,0:T(8,128)S(1)} %collective-permute-done.refs_3_, f32[1,216,128]{2,1,0:T(8,128)} %collective-permute-done.1.refs_4_, ...), custom_call_target="tpu_custom_call" | custom-call | flops 6000000 | bytes 6000000 | tf_op jit(solution)/shard_map/last_chunk/pallas_call | solution.py:390
  (18 shorter events, 0.0 us)
Async XLA Ops:
  4.2 44.5 %all-to-all-start = ((f32[2,8,24]{2,0,1:T(2,128)}), f32[2,8,24]{2,0,1:T(2,128)}, u32[]{:S(2)}, u32[]{:S(2)}) async-start(f32[2,8,24]{2,0,1:T(2,128)} %copy.33), calls=%async_computation | async-start | bytes 16384 | tf_op jit(solution)/shard_map/all_to_all | solution.py:437
  11.5 1.7 %copy-start = (f32[36,36,4,128]{3,2,1,0:T(4,128)S(1)}, f32[36,36,4,128]{3,2,1,0:T(4,128)}, u32[]{:S(2)}) copy-start(f32[36,36,4,128]{3,2,1,0:T(4,128)} %param.15) | copy-start | bytes 7962628
  15.3 14.1 %collective-permute-start.2 = (f32[2,6,8,128]{3,2,1,0:T(8,128)}, f32[2,6,8,128]{3,2,1,0:T(8,128)}, u32[]{:S(2)}, u32[]{:S(2)}) collective-permute-start(f32[2,6,8,128]{3,2,1,0:T(8,128)} %get-tuple-element.30), channel_id=1, source_target_pairs={{0,4},{4,8},{8,12},{12,16},{16,20},{20,24},{24,28},{28,0},{1,5},{5... | collective-permute-start | bytes 147464 | tf_op jit(solution)/shard_map/ppermute | solution.py:442
  17.3 9.9 %copy-start.13 = (s32[4,128]{1,0:T(4,128)S(1)}, s32[4,128]{1,0:T(4,128)}, u32[]{:S(2)}) copy-start(s32[4,128]{1,0:T(4,128)} %param.16) | copy-start | bytes 6148
  17.3 12.2 %collective-permute-start.3 = (f32[2,6,8,128]{3,2,1,0:T(8,128)}, f32[2,6,8,128]{3,2,1,0:T(8,128)}, u32[]{:S(2)}, u32[]{:S(2)}) collective-permute-start(f32[2,6,8,128]{3,2,1,0:T(8,128)} %get-tuple-element.31), channel_id=1, source_target_pairs={{4,0},{8,4},{12,8},{16,12},{20,16},{24,20},{28,24},{0,28},{5,1},{9... | collective-permute-start | bytes 147464 | tf_op jit(solution)/shard_map/ppermute | solution.py:443
  20.7 15.1 %collective-permute-start.6 = (f32[1,216,128]{2,1,0:T(8,128)}, f32[1,216,128]{2,1,0:T(8,128)S(1)}, u32[]{:S(2)}, u32[]{:S(2)}) collective-permute-start(f32[1,216,128]{2,1,0:T(8,128)} %get-tuple-element.18), channel_id=1, source_target_pairs={{0,4},{4,8},{8,12},{12,16},{16,20},{20,24},{24,28},{28,0},{1,5},{5... | collective-permute-start | bytes 331784 | tf_op jit(solution)/shard_map/ppermute | solution.py:432
  20.8 26.5 %copy-start.1 = (f32[36,36,4,128]{3,2,1,0:T(4,128)S(1)}, f32[36,36,4,128]{3,2,1,0:T(4,128)}, u32[]{:S(2)}) copy-start(f32[36,36,4,128]{3,2,1,0:T(4,128)} %param.15) | copy-start | bytes 7962628
  20.8 17.0 %collective-permute-start.7 = (f32[1,216,128]{2,1,0:T(8,128)S(1)}, f32[1,216,128]{2,1,0:T(8,128)}, u32[]{:S(2)}, u32[]{:S(2)}) collective-permute-start(f32[1,216,128]{2,1,0:T(8,128)S(1)} %get-tuple-element.19), channel_id=1, source_target_pairs={{4,0},{8,4},{12,8},{16,12},{20,16},{24,20},{28,24},{0,28},{5,1},{9... | collective-permute-start | bytes 331784 | tf_op jit(solution)/shard_map/ppermute | solution.py:432
  26.5 0.7 copy-start.10
  27.2 31.5 %collective-permute-start.8 = (f32[3,216,128]{2,1,0:T(8,128)}, f32[3,216,128]{2,1,0:T(8,128)}, u32[]{:S(2)}, u32[]{:S(2)}) collective-permute-start(f32[3,216,128]{2,1,0:T(8,128)} %get-tuple-element.21), channel_id=1, source_target_pairs={{0,4},{4,8},{8,12},{12,16},{16,20},{20,24},{24,28},{28,0},{1,5},{5... | collective-permute-start | bytes 995336 | tf_op jit(solution)/shard_map/ppermute | solution.py:432
  27.7 0.8 copy-start.8
  28.5 0.8 copy-start.9
  29.3 37.5 %copy-start.2 = (f32[6,36,128]{2,1,0:T(8,128)S(1)}, f32[6,36,128]{2,1,0:T(8,128)}, u32[]{:S(2)}) copy-start(f32[6,36,128]{2,1,0:T(8,128)} %constant.31.clone.refs_1_) | copy-start | bytes 331780
  29.3 37.5 %copy-start.6 = (f32[2,4,128]{2,1,0:T(4,128)S(1)}, f32[2,4,128]{2,1,0:T(4,128)}, u32[]{:S(2)}) copy-start(f32[2,4,128]{2,1,0:T(4,128)} %refs_8_.7) | copy-start | bytes 12292
  29.3 37.5 %copy-start.7 = (f32[5,36]{1,0:T(8,128)S(1)}, f32[5,36]{1,0:T(8,128)}, u32[]{:S(2)}) copy-start(f32[5,36]{1,0:T(8,128)} %constant.30.clone.refs_0_) | copy-start | bytes 2164
  29.4 53.0 %collective-permute-start.10 = (f32[4,216,128]{2,1,0:T(8,128)}, f32[4,216,128]{2,1,0:T(8,128)S(1)}, u32[]{:S(2)}, u32[]{:S(2)}) collective-permute-start(f32[4,216,128]{2,1,0:T(8,128)} %copy-done.9), channel_id=1, source_target_pairs={{0,4},{4,8},{8,12},{12,16},{16,20},{20,24},{24,28},{28,0},{1,5},{5... | collective-permute-start | bytes 1327112 | tf_op jit(solution)/shard_map/ppermute | solution.py:432
  29.5 53.0 %collective-permute-start.11 = (f32[4,216,128]{2,1,0:T(8,128)}, f32[4,216,128]{2,1,0:T(8,128)}, u32[]{:S(2)}, u32[]{:S(2)}) collective-permute-start(f32[4,216,128]{2,1,0:T(8,128)} %copy-done.8), channel_id=1, source_target_pairs={{4,0},{8,4},{12,8},{16,12},{20,16},{24,20},{28,24},{0,28},{5,1},{9... | collective-permute-start | bytes 1327112 | tf_op jit(solution)/shard_map/ppermute | solution.py:432
  35.8 22.9 %copy-start.3 = (f32[1,216,128]{2,1,0:T(8,128)}, f32[1,216,128]{2,1,0:T(8,128)S(1)}, u32[]{:S(2)}) copy-start(f32[1,216,128]{2,1,0:T(8,128)S(1)} %collective-permute-done.6.refs_3_) | copy-start | bytes 331780
  35.8 10.2 %collective-permute-start.5 = (f32[4,6,8,128]{3,2,1,0:T(8,128)}, f32[4,6,8,128]{3,2,1,0:T(8,128)S(1)}, u32[]{:S(2)}, u32[]{:S(2)}) collective-permute-start(f32[4,6,8,128]{3,2,1,0:T(8,128)} %fusion.4), channel_id=1, source_target_pairs={{1,0},{2,1},{3,2},{5,4},{6,5},{7,6},{9,8},{10,9},{11,10},{13,12},{... | collective-permute-start | bytes 294920 | tf_op jit(solution)/shard_map/ppermute | solution.py:449
  37.8 34.1 %collective-permute-start.9 = (f32[3,216,128]{2,1,0:T(8,128)}, f32[3,216,128]{2,1,0:T(8,128)}, u32[]{:S(2)}, u32[]{:S(2)}) collective-permute-start(f32[3,216,128]{2,1,0:T(8,128)} %copy-done.10), channel_id=1, source_target_pairs={{4,0},{8,4},{12,8},{16,12},{20,16},{24,20},{28,24},{0,28},{5,1},{9... | collective-permute-start | bytes 995336 | tf_op jit(solution)/shard_map/ppermute | solution.py:432
  46.0 12.7 %collective-permute-start.4 = (f32[4,6,8,128]{3,2,1,0:T(8,128)}, f32[4,6,8,128]{3,2,1,0:T(8,128)S(1)}, u32[]{:S(2)}, u32[]{:S(2)}) collective-permute-start(f32[4,6,8,128]{3,2,1,0:T(8,128)} %fusion.4), channel_id=1, source_target_pairs={{0,1},{1,2},{2,3},{4,5},{5,6},{6,7},{8,9},{9,10},{10,11},{12,13},{... | collective-permute-start | bytes 294920 | tf_op jit(solution)/shard_map/ppermute | solution.py:448
  47.4 0.6 copy-start.11
  48.1 0.6 copy-start.12
  58.7 37.2 %collective-permute-start = (f32[1,216,128]{2,1,0:T(8,128)}, f32[1,216,128]{2,1,0:T(8,128)S(1)}, u32[]{:S(2)}, u32[]{:S(2)}) collective-permute-start(f32[1,216,128]{2,1,0:T(8,128)} %copy-done.12), channel_id=1, source_target_pairs={{0,4},{4,8},{8,12},{12,16},{16,20},{20,24},{24,28},{28,0},{1,5},{5... | collective-permute-start | bytes 331784 | tf_op jit(solution)/shard_map/ppermute | solution.py:432
  58.7 37.2 %collective-permute-start.1 = (f32[1,216,128]{2,1,0:T(8,128)}, f32[1,216,128]{2,1,0:T(8,128)}, u32[]{:S(2)}, u32[]{:S(2)}) collective-permute-start(f32[1,216,128]{2,1,0:T(8,128)} %copy-done.11), channel_id=1, source_target_pairs={{4,0},{8,4},{12,8},{16,12},{20,16},{24,20},{28,24},{0,28},{5,1},{9... | collective-permute-start | bytes 331784 | tf_op jit(solution)/shard_map/ppermute | solution.py:432
  66.8 29.2 %copy-start.5 = (f32[4,128,2]{1,0,2:T(4,128)}, f32[4,128,2]{1,0,2:T(4,128)S(1)}, u32[]{:S(2)}) copy-start(f32[4,128,2]{1,0,2:T(4,128)S(1)} %copy.35) | copy-start | bytes 12292
  66.8 0.9 copy-start.4

commit v2 on v1

v2 whole, which is shorter than its diff:
```python
import math

import jax
import jax.numpy as jnp
import numpy as np
from jax import lax
from jax.experimental import pallas as pl
from jax.experimental.pallas import tpu as pltpu
from jax.sharding import PartitionSpec as P

base_freq = 0.035
freq_step = 1.1
courant_max = 0.9
gravity = 9.81
input_rate = 0.05
damping_rate = 0.8
energy_ref = 0.5

F32 = jnp.float32
FREQS = 36
DIRS = 36
CELLS = 4
LANES = 128
ROWS = DIRS * CELLS
BLOCKS = (0, 8, 16, 24, 28)
GROUP = 4
HALO = DIRS + DIRS // 2
NEAR_SPLIT = 16
FAR = DIRS // 2
PACK = 6
CHUNKS = (8, 8, 12, 8)
GROUPS = FREQS // PACK
EDGE_ROWS = 2 * (FREQS // PACK) * 8
VMEM = 32 * 1024 * 1024
FIRST_VMEM = 63000000

freqs = base_freq * freq_step ** np.arange(FREQS, dtype=np.float64)
spacing = 2.0 * math.pi / DIRS
theta = (np.arange(DIRS) + 0.5) * spacing
phi = (np.arange(DIRS) + 1.0) * spacing
ratio = base_freq / freqs
SCALARS = np.stack(
    [
        courant_max * ratio,
        np.sqrt(ratio),
        input_rate * freqs / freqs[-1],
        2.0 * math.pi * freqs / gravity,
        freqs / freqs[-1],
    ]
).astype(np.float32)
ANGLES = np.broadcast_to(
    np.stack(
        [np.abs(np.cos(theta)), np.abs(np.sin(theta)), np.cos(theta), np.sin(theta), np.sin(phi), np.cos(phi)]
    )[:, :, None],
    (6, DIRS, LANES),
).astype(np.float32)


def stencil(a):
    one_m = 1.0 - a * a
    beyond = a * one_m * (-1.0 / 6.0)
    half = a * (0.5 - 0.5 * a)
    down = half + beyond
    up = a - half - 2.0 * beyond
    return beyond, up - beyond, 1.0 + down - up, -down


def packed_weights():
    out = np.zeros((5, FREQS // PACK, 8, LANES), np.float64)
    for k in range(FREQS):
        for b, j0 in enumerate(BLOCKS):
            c = courant_max * ratio[k] * np.cos(theta[j0 : j0 + 8])
            far, up, own, down = stencil(np.abs(c))
            zero = np.zeros(8)
            pos = c > 0
            five = [
                np.where(pos, far, zero),
                np.where(pos, up, down),
                own,
                np.where(pos, down, up),
                np.where(pos, zero, far),
            ]
            lane = 4 * ((k % PACK) * len(BLOCKS) + b)
            for d in range(5):
                out[d, k // PACK, :, lane : lane + 4] = five[d][:, None]
    return out.astype(np.float32)


PACKED = packed_weights()


def any_spec():
    return pl.BlockSpec(memory_space=pl.ANY)


def vmem_spec():
    return pl.BlockSpec(memory_space=pltpu.VMEM)


def smem_spec():
    return pl.BlockSpec(memory_space=pltpu.SMEM)


def halo_rows(x, start, right, left, low, high):
    def body(i, _):
        for kk in range(GROUP):
            k = start + i * GROUP + kk
            for ref, near, far in ((right, 3, 2), (left, 0, 1)):
                if far == 2:
                    runs = ((16, 0, 8), (24, 8, 1), (25, 27, 8), (33, 35, 1))
                else:
                    runs = ((16, 9, 8), (24, 17, 8), (32, 25, 2))
                for cell, rows in (
                    (near, ((0, 0, 8), (8, 8, 8), (34, 16, 8), (42, 24, 8), (50, 32, 4))),
                    (far, runs),
                ):
                    for row, j, n in rows:
                        ref[halo_at(i, kk, row, n), :] = x[k, pl.ds(cell + 4 * j, n, stride=4), :]
        return 0

    lax.fori_loop(low // GROUP, high // GROUP, body, 0)


def halo_at(i, kk, row, n):
    return pl.ds(pl.multiple_of(i * (GROUP * HALO), 8) + HALO * kk + row, n)


def lane_ids():
    return lax.broadcasted_iota(jnp.int32, (8, LANES), 1)


def first_body(count, x_hbm, hour, wind_hbm, cells_hbm, right, left, packed, x, wind, cells, sem, small):
    copies = []
    for n in range(count // GROUP):
        span = pl.ds(n * GROUP, GROUP)
        copies.append(pltpu.make_async_copy(x_hbm.at[span], x.at[span], sem.at[n]))
        copies[-1].start()
    few = [
        pltpu.make_async_copy(wind_hbm, wind, small.at[0]),
        pltpu.make_async_copy(cells_hbm, cells, small.at[1]),
    ]
    for copy in few:
        copy.start()
    for copy in few:
        copy.wait()
    late = hour[0]
    now = (1.0 - late) * wind[pl.ds(0, 2), :] + late * wind[pl.ds(2, 2), :]
    width = cells.shape[1]
    index = jnp.concatenate([cells[:, :LANES], cells[:, width - LANES :]] * 4, axis=0)
    table = jnp.concatenate([now[:1]] * 2 + [now[1:]] * 2 + [now[:1]] * 4, axis=0)
    listed = jnp.take_along_axis(table, index, axis=1)
    for ref, row in ((packed, 0), (right, count * HALO), (left, count * HALO)):
        ref[pl.ds(row, 8), :] = listed
    for n in range(count // GROUP):
        copies[n].wait()
        halo_rows(x, 0, right, left, n * GROUP, (n + 1) * GROUP)


def message(count, extra=0):
    return pltpu.VMEM((count * HALO + extra, LANES), F32)


def first_halos(x, count, hour, wind, cells):
    return pl.pallas_call(
        lambda *refs: first_body(count, *refs),
        out_shape=(message(count, 8), message(count, 8), jax.ShapeDtypeStruct((8, LANES), F32)),
        in_specs=[any_spec(), smem_spec(), any_spec(), any_spec()],
        out_specs=(vmem_spec(),) * 3,
        scratch_shapes=[
            pltpu.VMEM((count, *x.shape[1:]), F32),
            pltpu.VMEM(wind.shape, F32),
            pltpu.VMEM(cells.shape, cells.dtype),
            pltpu.SemaphoreType.DMA((count // GROUP,)),
            pltpu.SemaphoreType.DMA((2,)),
        ],
        compiler_params=pltpu.CompilerParams(vmem_limit_bytes=FIRST_VMEM),
        cost_estimate=pl.CostEstimate(flops=0, bytes_accessed=2000000, transcendentals=0),
        name="first_halos",
    )(x, hour, wind, cells)


def edge_body(x, sea, after, q):
    lane = lane_ids()
    block = lane // 4

    def body(g, _):
        for cell in range(CELLS):
            acc = jnp.zeros((8, LANES), F32)
            for r in range(PACK):
                for b, j0 in enumerate(BLOCKS):
                    at = r * len(BLOCKS) + b
                    rows = x[g * PACK + r, pl.ds(cell + 4 * j0, 8, stride=4), :]
                    acc = jnp.where(block == at, pltpu.roll(rows, (4 * at + 2) % LANES, 1), acc)
            q[cell, g] = acc
        return 0

    lax.fori_loop(0, GROUPS, body, 0)
    for cell in range(CELLS):
        mask = jnp.zeros((8, LANES), F32)
        for n, at in enumerate((LANES - 2, LANES - 1, 0, 1)):
            mask = jnp.where(lane % 4 == n, sea[pl.ds(cell, 1), pl.ds(at, 1)].astype(F32), mask)
        q[cell, GROUPS] = mask


def pack_edges(x, sea, after):
    return pl.pallas_call(
        edge_body,
        out_shape=jax.ShapeDtypeStruct((CELLS, GROUPS + 1, 8, LANES), F32),
        in_specs=[vmem_spec()] * 3,
        out_specs=vmem_spec(),
        compiler_params=pltpu.CompilerParams(vmem_limit_bytes=VMEM),
        cost_estimate=pl.CostEstimate(flops=0, bytes_accessed=4000000, transcendentals=0),
        name="pack_edges",
    )(x, sea, after)


def middle_body(spans, x, south, north, after_east, after_west, *refs):
    outs, merged = refs[:-1], refs[-1]
    row = spans[0][1] * HALO
    pick = lane_ids() % 4 < 2
    for c in range(CELLS):
        side, slot = (outs[1], c) if c < 2 else (outs[0], c - 2)
        for g in range(GROUPS + 1):
            both = jnp.where(pick, south[c, g], north[c, g])
            merged[c, g] = both
            if g < GROUPS:
                side[pl.ds(row + (slot * GROUPS + g) * 8, 8), :] = both
    for n, (start, count) in enumerate(spans):
        halo_rows(x, start, outs[2 * n], outs[2 * n + 1], 0, count)


def middle_halos(x, spans, south, north, after):
    extra = [EDGE_ROWS] + [0] * (len(spans) - 1)
    return pl.pallas_call(
        lambda *refs: middle_body(spans, *refs),
        out_shape=tuple(message(count, more) for (_, count), more in zip(spans, extra) for _ in range(2))
        + (jax.ShapeDtypeStruct((CELLS, GROUPS + 1, 8, LANES), F32),),
        in_specs=[vmem_spec()] * 5,
        out_specs=(vmem_spec(),) * (2 * len(spans) + 1),
        compiler_params=pltpu.CompilerParams(vmem_limit_bytes=VMEM),
        cost_estimate=pl.CostEstimate(flops=0, bytes_accessed=6000000, transcendentals=0),
        name="middle_halos",
    )(x, south, north, *after)


def last_halos(x, start, count, *after):
    return pl.pallas_call(
        lambda x, east, west, winds, right, left: halo_rows(x, start, right, left, 0, count),
        out_shape=(message(count), message(count)),
        in_specs=[vmem_spec()] * 4,
        out_specs=(vmem_spec(),) * 2,
        compiler_params=pltpu.CompilerParams(vmem_limit_bytes=VMEM),
        cost_estimate=pl.CostEstimate(flops=0, bytes_accessed=1000000, transcendentals=0),
        name="last_halos",
    )(x, *after)


def ghost_body(count, merged, west, east, weights, ghosts):
    def body(g, _):
        rows = [
            pl.ds(pl.multiple_of(count * HALO + (n * GROUPS + g) * 8, 8), 8) for n in range(2)
        ]
        ext = [west[rows[0], :], west[rows[1], :]] + [merged[c, g] for c in range(CELLS)]
        ext += [east[rows[0], :], east[rows[1], :]]
        for c in range(CELLS):
            total = weights[0, g] * ext[c]
            for d in range(1, 5):
                total = total + weights[d, g] * ext[c + d]
            total = total * merged[c, GROUPS]
            for r in range(PACK):
                for b in range(len(BLOCKS)):
                    shift = LANES - (4 * (r * len(BLOCKS) + b) + 2)
                    ghosts[g * PACK + r, c, b] = pltpu.roll(total, shift, 1)
        return 0

    lax.fori_loop(0, GROUPS, body, 0)


def move_ghosts(count, merged, west, east):
    return pl.pallas_call(
        lambda *refs: ghost_body(count, *refs),
        out_shape=jax.ShapeDtypeStruct((FREQS, CELLS, len(BLOCKS), 8, LANES), F32),
        in_specs=[vmem_spec()] * 4,
        out_specs=vmem_spec(),
        compiler_params=pltpu.CompilerParams(vmem_limit_bytes=VMEM),
        cost_estimate=pl.CostEstimate(flops=0, bytes_accessed=2000000, transcendentals=0),
        name="move_ghosts",
    )(merged, west, east, PACKED)


def wind_body(cap, sources, slots, weights, ang, sea, refr, *rest):
    picked = [[jnp.zeros((8, LANES), F32) for _ in range(2)] for _ in range(2)]
    pieces, (wind, sea8, turn, proj, table) = rest[:-5], rest[-5:]
    at = 0
    for piece in pieces:
        table[pl.ds(at, piece.shape[0]), :] = piece[...]
        at += piece.shape[0]
    width = cap * sources
    me = lax.axis_index("lon")
    mine = cap * me
    for half in range(2):
        index = slots[pl.ds(8 * half, 8), :]
        for s in range(sources):
            place = index - cap * s
            here = (place >= 0) & (place < cap)
            place = jnp.clip(place, 0, cap - 1) + mine
            low = place < LANES
            place = jnp.where(low, place, place - (width - LANES))
            for c in range(2):
                row = [
                    jnp.broadcast_to(table[pl.ds(8 * (s ^ me) + 2 * c + n, 1), :], (8, LANES)) for n in range(2)
                ]
                value = [jnp.take_along_axis(r, place, axis=1) for r in row]
                value = jnp.where(low, value[0], value[1])
                picked[half][c] = jnp.where(here, value, picked[half][c])
    for c in range(2):
        total = weights[pl.ds(0, 8), :] * picked[0][c]
        total = total + weights[pl.ds(8, 8), :] * picked[1][c]
        wind[c] = total[:CELLS] + total[CELLS:]
    for cell in range(CELLS):
        row = pl.ds(cell, 1)
        sea8[cell] = jnp.broadcast_to(sea[row, :], (8, LANES)).astype(F32)
        for j0 in BLOCKS:
            j = pl.ds(j0, 8)
            turn[cell, j, :] = refr[0, row, :] * ang[4, j, :] - refr[1, row, :] * ang[5, j, :]
            proj[cell, j, :] = wind[0, row, :] * ang[2, j, :] + wind[1, row, :] * ang[3, j, :]


def surface(cap, sources, pieces, slots, weights, sea, refr):
    return pl.pallas_call(
        lambda *refs: wind_body(cap, sources, *refs),
        out_shape=(
            jax.ShapeDtypeStruct((2, CELLS, LANES), F32),
            jax.ShapeDtypeStruct((CELLS, 8, LANES), F32),
            jax.ShapeDtypeStruct((CELLS, DIRS, LANES), F32),
            jax.ShapeDtypeStruct((CELLS, DIRS, LANES), F32),
        ),
        in_specs=[vmem_spec()] * (5 + len(pieces)),
        out_specs=(vmem_spec(),) * 4,
        scratch_shapes=[pltpu.VMEM((8 * sources, LANES), F32)],
        compiler_params=pltpu.CompilerParams(vmem_limit_bytes=VMEM),
        cost_estimate=pl.CostEstimate(flops=0, bytes_accessed=2000000, transcendentals=0),
        name="surface_wind",
    )(slots, weights, ANGLES, sea, refr, *pieces)


def chunk_pass(
    first, count, scal, ang, x, from_west, from_east, ghosts, sea8, turn, proj, zs, gs, out, out_first
):
    lane = lane_ids()
    sub = lax.broadcasted_iota(jnp.int32, (8, LANES), 0)
    near_rows = (0, 8, 34, 42, 46)

    def one(i, kk, sums):
        k = first + i * GROUP + kk
        cour = scal[0, k]
        bend = scal[1, k]
        rate = scal[2, k]
        slow = scal[3, k]
        for b, j0 in enumerate(BLOCKS):
            w0, w1, w2, w3 = stencil(cour * ang[0, pl.ds(j0, 8), :])
            v0, v1, v2, v3 = stencil(cour * ang[1, pl.ds(j0, 8), :])
            cells = [x[k, pl.ds(c + 4 * j0, 8, stride=4), :] for c in range(CELLS)]
            west = from_west[halo_at(i, kk, near_rows[b], 8), :]
            east = from_east[halo_at(i, kk, near_rows[b], 8), :]
            plus = [west, *cells, east]
            minus = plus[::-1]
            if b == 0:
                far, seq = from_west[halo_at(i, kk, 16, 8), :], plus
            elif b == 2:
                far, seq = from_east[halo_at(i, kk, 23, 8), :], minus
            elif b == 4:
                far, seq = from_west[halo_at(i, kk, 26, 8), :], plus
            else:
                if b == 1:
                    pos = sub < 1
                    far_p, far_m = from_west[halo_at(i, kk, 24, 8), :], from_east[halo_at(i, kk, 15, 8), :]
                else:
                    pos = sub >= 3
                    far_p, far_m = from_west[halo_at(i, kk, 22, 8), :], from_east[halo_at(i, kk, 31, 8), :]
                far = jnp.where(pos, far_p, far_m)
                seq = [jnp.where(pos, p, m) for p, m in zip(plus, minus)]
            seq = [far, *seq]
            moved = [
                w0 * seq[c] + w1 * seq[c + 1] + w2 * seq[c + 2] + w3 * seq[c + 3] for c in range(CELLS)
            ]
            if b == 2:
                moved = moved[::-1]
            elif b in (1, 3):
                moved = [jnp.where(pos, p, m) for p, m in zip(moved, moved[::-1])]
            for c in range(CELLS):
                z = moved[c] * sea8[c]
                ghost = ghosts[k, c, b]
                s1 = pltpu.roll(jnp.where(lane == LANES - 1, ghost, z), 1, 1)
                n1 = pltpu.roll(jnp.where(lane == 0, ghost, z), LANES - 1, 1)
                if b <= 2:
                    s2 = pltpu.roll(jnp.where(lane >= LANES - 2, ghost, z), 2, 1)
                if b >= 2:
                    n2 = pltpu.roll(jnp.where(lane < 2, ghost, z), LANES - 2, 1)
                if b < 2:
                    up, down, far = s1, n1, s2
                elif b > 2:
                    up, down, far = n1, s1, n2
                else:
                    p = sub < 2
                    up, down = jnp.where(p, s1, n1), jnp.where(p, n1, s1)
                    far = jnp.where(p, s2, n2)
                z = (v0 * far + v1 * up + v2 * z + v3 * down) * sea8[c]
                zs[kk, c, pl.ds(8 + j0, 8), :] = z
        out_sums = []
        for c in range(CELLS):
            zs[kk, c, pl.ds(8 + DIRS, 1), :] = zs[kk, c, pl.ds(8, 1), :]
            for b, j0 in enumerate(BLOCKS):
                own = zs[kk, c, pl.ds(8 + j0, 8), :]
                nxt = zs[kk, c, pl.ds(9 + j0, 8), :]
                s = bend * turn[c, pl.ds(j0, 8), :]
                gs[kk, c, pl.ds(8 + j0, 8), :] = jnp.maximum(s, 0.0) * own + jnp.minimum(s, 0.0) * nxt
            gs[kk, c, pl.ds(7, 1), :] = gs[kk, c, pl.ds(7 + DIRS, 1), :]
            total = sums[c]
            for b, j0 in enumerate(BLOCKS):
                own = zs[kk, c, pl.ds(8 + j0, 8), :]
                flux = gs[kk, c, pl.ds(8 + j0, 8), :]
                prev = gs[kk, c, pl.ds(7 + j0, 8), :]
                refracted = own - (flux - prev)
                total = total + (jnp.where(sub >= 4, refracted, 0.0) if b == 4 else refracted)
                growth = rate * jnp.maximum(proj[c, pl.ds(j0, 8), :] * slow - 1.0, 0.0)
                out[out_first + i * GROUP + kk, pl.ds(c + 4 * j0, 8, stride=4), :] = refracted * jnp.exp(growth)
            out_sums.append(total)
        return tuple(out_sums)

    def body(i, sums):
        for kk in range(GROUP):
            sums = one(i, kk, sums)
        return sums

    zero = jnp.zeros((8, LANES), F32)
    return lax.fori_loop(0, count // GROUP, body, (zero,) * CELLS)


def main_body(
    first, count, scal, ang, x, west, east, ghosts, sea8, turn, proj, out, energy, zs, gs
):
    sums = chunk_pass(first, count, scal, ang, x, west, east, ghosts, sea8, turn, proj, zs, gs, out, 0)
    for c in range(CELLS):
        energy[c] = sums[c]


def pass_scratch():
    return [pltpu.VMEM((GROUP, CELLS, 56, LANES), F32), pltpu.VMEM((GROUP, CELLS, 56, LANES), F32)]


def main_chunk(first, count, x, west, east, ghosts, tables):
    return pl.pallas_call(
        lambda *refs: main_body(first, count, *refs),
        out_shape=(
            jax.ShapeDtypeStruct((count, ROWS, LANES), F32),
            jax.ShapeDtypeStruct((CELLS, 8, LANES), F32),
        ),
        in_specs=[smem_spec()] + [vmem_spec()] * 8,
        out_specs=(vmem_spec(), vmem_spec()),
        scratch_shapes=pass_scratch(),
        compiler_params=pltpu.CompilerParams(vmem_limit_bytes=VMEM),
        cost_estimate=pl.CostEstimate(flops=0, bytes_accessed=1000000, transcendentals=0),
        name="chunk",
    )(SCALARS, ANGLES, x, west, east, ghosts, *tables)


def tail_body(sizes, scal, ang, x, west, east, ghosts, sea8, turn, proj, *rest):
    done = len(sizes) - 1
    parts, energies = rest[:done], rest[done : 2 * done]
    out_hbm, obuf, zs, gs, out_sem = rest[2 * done :]
    count = sizes[-1]
    first = FREQS - count
    sums = chunk_pass(
        first, count, scal, ang, x, west, east, ghosts, sea8, turn, proj, zs, gs, obuf, first
    )
    sub = lax.broadcasted_iota(jnp.int32, (8, LANES), 0)
    pattern = jnp.zeros((8, LANES), F32)
    for c in range(CELLS):
        total = sums[c]
        for energy in energies:
            total = total + energy[c]
        mean = jnp.sum(total, axis=0, keepdims=True) * (1.0 / (FREQS * DIRS))
        level = mean * (1.0 / energy_ref)
        pattern = jnp.where(sub % CELLS == c, damping_rate * (level * level), pattern)
    stores, at = [], 0
    for n, size in enumerate(sizes):
        def body(i, _, at=at, n=n):
            scale = jnp.exp(-(scal[4, at + i] * pattern))
            source, k = (parts[n], i) if n < done else (obuf, at + i)
            for r in range(0, ROWS, 8):
                obuf[at + i, pl.ds(r, 8), :] = source[k, pl.ds(r, 8), :] * scale
            return 0

        lax.fori_loop(0, size, body, 0)
        span = pl.ds(at, size)
        stores.append(pltpu.make_async_copy(obuf.at[span], out_hbm.at[span], out_sem.at[n]))
        stores[-1].start()
        at += size
    for store in stores:
        store.wait()


def tail_chunk(sizes, x, west, east, ghosts, tables, parts, energies):
    done = len(sizes) - 1
    return pl.pallas_call(
        lambda *refs: tail_body(sizes, *refs),
        out_shape=jax.ShapeDtypeStruct((FREQS, ROWS, LANES), F32),
        in_specs=[smem_spec()] + [vmem_spec()] * (8 + 2 * done),
        out_specs=any_spec(),
        scratch_shapes=[
            pltpu.VMEM((FREQS, ROWS, LANES), F32),
            *pass_scratch(),
            pltpu.SemaphoreType.DMA((done + 1,)),
        ],
        compiler_params=pltpu.CompilerParams(vmem_limit_bytes=VMEM),
        cost_estimate=pl.CostEstimate(flops=0, bytes_accessed=6000000, transcendentals=0),
        name="last_chunk",
    )(SCALARS, ANGLES, x, west, east, ghosts, *tables, *parts, *energies)


def ring(axis, wrap):
    size = lax.axis_size(axis)
    up = [(i, (i + 1) % size) for i in range(size if wrap else size - 1)]
    return up, [(j, i) for i, j in up]


def local(
    spectrum, sea_mask, refraction, atm_wind, hour_fraction, send_cells, recv_slots, recv_weights
):
    east_way, west_way = ring("lon", True)
    north_way, south_way = ring("lat", False)
    x = spectrum.reshape(FREQS, ROWS, LANES)
    tiles = lax.axis_size("lon")
    cap = send_cells.shape[1] // tiles
    firsts = [sum(CHUNKS[:n]) for n in range(len(CHUNKS))]

    def exchange(to_east, to_west):
        return lax.ppermute(to_east, "lon", east_way), lax.ppermute(to_west, "lon", west_way)

    *sends, packed = first_halos(
        x, CHUNKS[0], hour_fraction, atm_wind.reshape(4, LANES), send_cells
    )
    halos = [exchange(*sends)]
    q = pack_edges(x, sea_mask, packed)
    south = lax.ppermute(q, "lat", north_way)
    north = lax.ppermute(q, "lat", south_way)
    *sends, merged = middle_halos(x, tuple(zip(firsts, CHUNKS))[1:3], south, north, halos[0])
    halos += [exchange(*sends[:2]), exchange(*sends[2:])]
    west, east = (side[-8:] for side in halos[0])
    lists = [jnp.concatenate([packed, jnp.where(lax.axis_index("lon") % 2 == 0, east, west)])]
    step = 2
    while step < tiles:
        held = lists[0] if len(lists) == 1 else jnp.concatenate(lists)
        lists.append(lax.ppermute(held, "lon", [(i, i ^ step) for i in range(tiles)]))
        step *= 2
    surface_wind, *tables = surface(
        cap,
        tiles,
        lists,
        recv_slots.reshape(4 * CELLS, LANES),
        recv_weights.reshape(4 * CELLS, LANES),
        sea_mask,
        refraction,
    )
    halos.append(exchange(*last_halos(x, firsts[3], CHUNKS[3], *halos[1], tables[0])))
    ghosts = move_ghosts(CHUNKS[1], merged, *halos[1])

    parts, energies = [], []
    for n, (first, count) in enumerate(zip(firsts, CHUNKS)):
        west, east = halos[n]
        if n < len(CHUNKS) - 1:
            part, energy = main_chunk(first, count, x, west, east, ghosts, tables)
            parts.append(part)
            energies.append(energy)
        else:
            out = tail_chunk(CHUNKS, x, west, east, ghosts, tables, parts, energies)
    return (out.reshape(spectrum.shape), surface_wind)


def solution(mesh):
    in_specs = (
        P(None, None, "lon", "lat"),
        P("lon", "lat"),
        P(None, "lon", "lat"),
        P(None, None, ("lon", "lat")),
        P(),
        P(("lon", "lat"), None),
        P(None, "lon", "lat"),
        P(None, "lon", "lat"),
    )
    out_specs = (P(None, None, "lon", "lat"), P(None, "lon", "lat"))
    return jax.shard_map(local, mesh=mesh, in_specs=in_specs, out_specs=out_specs, check_vma=False)
```

time: 104 us -> 61.7 us (0.59); the launches traced: 102 us -> 61.5 us
  Pallas kernels: 37.9 us -> 15.9 us
  local copies, waits for them, and re-layouts: 19.5 us -> 0.73 us
  waiting for transfers between devices: 0.03 us -> 15.8 us
  starting transfers between devices: 37.1 us -> 27.4 us
  other arithmetic: 6.03 us -> 0.01 us
    pallas_call x3, Pallas kernels: 28.2 us -> 6.34 us  [main_chunk(): pl.pallas_call(lambda *refs: main_body(first, count, *refs), out_shape=(j...]
    ppermute x12, waiting for transfers between devices: 0.03 us -> 15.8 us  [the longest x4 7.68 us: exchange(): lax.ppermute(to_west, 'lon', west_way)]
    gather x2 -> x0, local copies, waits for them, and re-layouts: 9.21 us -> none  [the longest x1 8.52 us: local(): picked = received[:, recv_slots]]
    all_to_all x1 -> x0, starting transfers between devices: 7.28 us -> none  [local(): lax.all_to_all(packed, 'lon', split_axis=1, concat_axis=1, tiled=True)]
    unnamed x28 -> x20, local copies, waits for them, and re-layouts: 6.19 us -> 0.73 us
    pallas_call x1, Pallas kernels: 6.21 us -> 3.56 us  [tail_chunk(): pl.pallas_call(lambda *refs: tail_body(sizes, *refs), out_shape=jax.Shape...]
    pallas_call x5 -> x6, Pallas kernels: 3.56 us -> 6 us  [the longest x1 1.92 us: pack_edges(): pl.pallas_call(edge_body, out_shape=jax.ShapeDtypeStruct((CELLS, GROUPS +...]
    ppermute x12, starting transfers between devices: 29.8 us -> 27.4 us  [the longest x4 17 us: exchange(): lax.ppermute(to_west, 'lon', west_way)]
  transfers between devices with their start and end apart: 13 -> 12, of which waited for: 0 -> 7; matrix products, arithmetic and copies ran while one was open for 16% -> 0% of each run, Pallas kernels for 31% -> 17%
where the time goes in v2:
time: 61.7 us; the launch traced here: 61.5 us
  starting transfers between devices  27.4 us (44%)
  Pallas kernels  15.9 us (26%)
  waiting for transfers between devices  15.8 us (26%)
  between operations  1.62 us (3%)
  local copies, waits for them, and re-layouts  0.73 us (1%)
    ppermute x4, starting transfers between devices, exchange(): lax.ppermute(to_west, 'lon', west_way)  17 us
    ppermute x4, waiting for transfers between devices, exchange(): lax.ppermute(to_west, 'lon', west_way)  7.68 us
    ppermute x2, waiting for transfers between devices, local(): lax.ppermute(held, 'lon', [(i, i ^ step) for i in range(tiles)])  6.95 us
    pallas_call x3, Pallas kernels, main_chunk(): pl.pallas_call(lambda *refs: main_body(first, count, *refs), out_shape=(j...  6.34 us
    pallas_call x1, Pallas kernels, tail_chunk(): pl.pallas_call(lambda *refs: tail_body(sizes, *refs), out_shape=jax.Shape...  3.56 us
    ppermute x4, starting transfers between devices, exchange(): lax.ppermute(to_east, 'lon', east_way)  3.47 us
    ppermute x1, starting transfers between devices, local(): south = lax.ppermute(q, 'lat', north_way)  3.04 us
    ppermute x2, starting transfers between devices, local(): lax.ppermute(held, 'lon', [(i, i ^ step) for i in range(tiles)])  2.69 us
  transfers between devices with their start and end apart: 12, of which 7 were waited for; matrix products, arithmetic and copies ran while one was open for 0% of the time, Pallas kernels for 17%

profile of v2, /device:TPU:0, one launch (start us, length us, event | category | flops | bytes accessed | tf_op | source)
XLA Modules:
  0.0 61.5 jit_solution(12035906305663741747)
XLA Ops:
  0.6 0.0 copy-start
  0.6 0.0 copy-start.6
  1.4 1.9 %first_halos.1 = (f32[440,128]{1,0:T(8,128)}, f32[440,128]{1,0:T(8,128)}, f32[8,128]{1,0:T(8,128)}) custom-call(f32[36,144,128]{2,1,0:T(8,128)} %bitcast.5, f32[1]{0:T(128)S(6)} %copy.13.refs_1_, f32[4,128]{1,0:T(4,128)} %bitcast.16, s32[1,192]{1,0:T(1,128)} %refs_3_.3), custom_call_target="tpu_custom_call" | custom-call | bytes 2000000 | tf_op jit(solution)/shard_map/first_halos/pallas_call | solution.py:164
  3.4 3.0 %collective-permute-start.2 = (f32[440,128]{1,0:T(8,128)}, f32[440,128]{1,0:T(8,128)S(1)}, u32[]{:S(2)}, u32[]{:S(2)}) collective-permute-start(f32[440,128]{1,0:T(8,128)} %get-tuple-element.23), channel_id=1, source_target_pairs={{0,4},{4,8},{8,12},{12,16},{16,20},{20,24},{24,28},{28,0},{1,5},{5... | collective-permute-start | bytes 675848 | tf_op jit(solution)/shard_map/ppermute | solution.py:539
  6.4 3.1 %collective-permute-start.3 = (f32[440,128]{1,0:T(8,128)}, f32[440,128]{1,0:T(8,128)S(1)}, u32[]{:S(2)}, u32[]{:S(2)}) collective-permute-start(f32[440,128]{1,0:T(8,128)} %get-tuple-element.24), channel_id=1, source_target_pairs={{4,0},{8,4},{12,8},{16,12},{20,16},{24,20},{28,24},{0,28},{5,1},{9... | collective-permute-start | bytes 675848 | tf_op jit(solution)/shard_map/ppermute | solution.py:539
  9.5 0.0 copy-done
  9.5 0.0 copy-done.6
  9.5 0.0 copy-start.4
  9.5 0.7 %copy-done.4 = f32[8,128]{1,0:T(8,128)S(1)} copy-done((f32[8,128]{1,0:T(8,128)S(1)}, f32[8,128]{1,0:T(8,128)}, u32[]{:S(2)}) %copy-start.4) | copy-done | bytes 4120
  10.2 0.0 copy-start.5
  10.2 0.0 copy-start.1
  10.2 0.0 copy-start.7
  10.2 0.0 copy-start.8
  10.2 0.0 copy-start.9
  10.2 1.9 %pack_edges.1 = f32[4,7,8,128]{3,2,1,0:T(8,128)} custom-call(f32[36,144,128]{2,1,0:T(8,128)S(1)} %bitcast.6, s32[4,128]{1,0:T(4,128)S(1)} %copy-done.6, f32[8,128]{1,0:T(8,128)S(1)} %copy-done.4), custom_call_target="tpu_custom_call" | custom-call | bytes 4000000 | tf_op jit(solution)/shard_map/pack_edges/pallas_call | solution.py:206
  12.1 1.3 %collective-permute-start.1 = (f32[4,7,8,128]{3,2,1,0:T(8,128)}, f32[4,7,8,128]{3,2,1,0:T(8,128)S(1)}, u32[]{:S(2)}, u32[]{:S(2)}) collective-permute-start(f32[4,7,8,128]{3,2,1,0:T(8,128)} %pack_edges.1), channel_id=1, source_target_pairs={{1,0},{2,1},{3,2},{5,4},{6,5},{7,6},{9,8},{10,9},{11,10},{13,12},{... | collective-permute-start | bytes 344072 | tf_op jit(solution)/shard_map/ppermute | solution.py:547
  13.4 3.0 %collective-permute-start = (f32[4,7,8,128]{3,2,1,0:T(8,128)}, f32[4,7,8,128]{3,2,1,0:T(8,128)S(1)}, u32[]{:S(2)}, u32[]{:S(2)}) collective-permute-start(f32[4,7,8,128]{3,2,1,0:T(8,128)} %pack_edges.1), channel_id=1, source_target_pairs={{0,1},{1,2},{2,3},{4,5},{5,6},{6,7},{8,9},{9,10},{10,11},{12,13},{... | collective-permute-start | bytes 344072 | tf_op jit(solution)/shard_map/ppermute | solution.py:546
  16.5 0.0 copy-start.2
  16.5 0.0 collective-permute-done.1.refs_2_
  16.5 1.1 %collective-permute-done.refs_1_ = f32[4,7,8,128]{3,2,1,0:T(8,128)S(1)} collective-permute-done((f32[4,7,8,128]{3,2,1,0:T(8,128)}, f32[4,7,8,128]{3,2,1,0:T(8,128)S(1)}, u32[]{:S(2)}, u32[]{:S(2)}) %collective-permute-start) | collective-permute-done | bytes 114720 | tf_op jit(solution)/shard_map/ppermute | solution.py:546
  17.6 0.0 collective-permute-done.2.refs_3_
  17.6 0.8 %collective-permute-done.3.refs_4_ = f32[440,128]{1,0:T(8,128)S(1)} collective-permute-done((f32[440,128]{1,0:T(8,128)}, f32[440,128]{1,0:T(8,128)S(1)}, u32[]{:S(2)}, u32[]{:S(2)}) %collective-permute-start.3) | collective-permute-done | bytes 225312 | tf_op jit(solution)/shard_map/ppermute | solution.py:539
  18.4 0.1 middle_halos.1
  18.5 0.3 collective-permute-start.4
  18.9 4.4 %collective-permute-start.5 = (f32[528,128]{1,0:T(8,128)S(1)}, f32[528,128]{1,0:T(8,128)S(1)}, u32[]{:S(2)}, u32[]{:S(2)}) collective-permute-start(f32[528,128]{1,0:T(8,128)S(1)} %get-tuple-element.26), channel_id=1, source_target_pairs={{4,0},{8,4},{12,8},{16,12},{20,16},{24,20},{28,24},{0,28},{5,1},{9... | collective-permute-start | bytes 811016 | tf_op jit(solution)/shard_map/ppermute | solution.py:539
  23.3 0.0 copy-done.5
  23.3 0.1 collective-permute-start.6
  23.4 0.1 collective-permute-start.10
  23.5 4.7 %collective-permute-start.11 = (f32[648,128]{1,0:T(8,128)S(1)}, f32[648,128]{1,0:T(8,128)S(1)}, u32[]{:S(2)}, u32[]{:S(2)}) collective-permute-start(f32[648,128]{1,0:T(8,128)S(1)} %get-tuple-element.36), channel_id=1, source_target_pairs={{4,0},{8,4},{12,8},{16,12},{20,16},{24,20},{28,24},{0,28},{5,1},{9... | collective-permute-start | bytes 995336 | tf_op jit(solution)/shard_map/ppermute | solution.py:539
  28.2 2.1 %collective-permute-done.6.refs_6_ = f32[16,128]{1,0:T(8,128)S(1)} collective-permute-done((f32[16,128]{1,0:T(8,128)S(1)}, f32[16,128]{1,0:T(8,128)S(1)}, u32[]{:S(2)}, u32[]{:S(2)}) %collective-permute-start.6) | collective-permute-done | bytes 8224 | tf_op jit(solution)/shard_map/ppermute | solution.py:555
  30.3 2.6 %collective-permute-start.7 = (f32[32,128]{1,0:T(8,128)S(1)}, f32[32,128]{1,0:T(8,128)S(1)}, u32[]{:S(2)}, u32[]{:S(2)}) collective-permute-start(f32[32,128]{1,0:T(8,128)S(1)} %pad_maximum_fusion), channel_id=1, source_target_pairs={{0,16},{4,20},{8,24},{12,28},{16,0},{20,4},{24,8},{28,12},{1,17},{... | collective-permute-start | bytes 49160 | tf_op jit(solution)/shard_map/ppermute | solution.py:555
  32.9 4.9 %collective-permute-done.7.refs_7_ = f32[32,128]{1,0:T(8,128)S(1)} collective-permute-done((f32[32,128]{1,0:T(8,128)S(1)}, f32[32,128]{1,0:T(8,128)S(1)}, u32[]{:S(2)}, u32[]{:S(2)}) %collective-permute-start.7) | collective-permute-done | bytes 16416 | tf_op jit(solution)/shard_map/ppermute | solution.py:555
  37.8 0.0 copy-done.1
  37.8 0.0 copy-done.7
  37.8 0.0 copy-done.8
  37.8 0.0 copy-done.9
  37.8 0.8 %surface_wind.1 = (f32[2,4,128]{2,1,0:T(4,128)}, f32[4,8,128]{2,1,0:T(8,128)S(1)}, f32[4,36,128]{2,1,0:T(8,128)S(1)}, f32[4,36,128]{2,1,0:T(8,128)S(1)}) custom-call(s32[16,128]{1,0:T(8,128)S(1)} %bitcast.13, f32[16,128]{1,0:T(8,128)S(1)} %bitcast.14, f32[6,36,128]{2,1,0:T(8,128)S(1)} %copy-done.1, s32[4,128]{1,0:T(4,128)S(1)} %copy-done.6, ...), custom_call_target="tpu_custom_call" | custom-call | bytes 2000000 | tf_op jit(solution)/shard_map/surface_wind/pallas_call | solution.py:330
  38.6 0.0 collective-permute-done.4.east.refs_1_.refs_3_
  38.6 3.0 %collective-permute-done.5.west.refs_2_.refs_4_ = f32[528,128]{1,0:T(8,128)S(1)} collective-permute-done((f32[528,128]{1,0:T(8,128)S(1)}, f32[528,128]{1,0:T(8,128)S(1)}, u32[]{:S(2)}, u32[]{:S(2)}) %collective-permute-start.5) | collective-permute-done | bytes 270368 | tf_op jit(solution)/shard_map/ppermute | solution.py:539
  41.6 0.0 copy-start.3
  41.6 0.1 collective-permute-start.8
  41.7 4.7 %collective-permute-start.9 = (f32[432,128]{1,0:T(8,128)S(1)}, f32[432,128]{1,0:T(8,128)S(1)}, u32[]{:S(2)}, u32[]{:S(2)}) collective-permute-start(f32[432,128]{1,0:T(8,128)S(1)} %get-tuple-element.29), channel_id=1, source_target_pairs={{4,0},{8,4},{12,8},{16,12},{20,16},{24,20},{28,24},{0,28},{5,1},{9... | collective-permute-start | bytes 663560 | tf_op jit(solution)/shard_map/ppermute | solution.py:539
  46.4 0.0 copy-done.2
  46.4 1.2 %move_ghosts.1.refs_5_ = f32[36,4,5,8,128]{4,3,2,1,0:T(8,128)S(1)} custom-call(f32[4,7,8,128]{3,2,1,0:T(8,128)S(1)} %get-tuple-element.30.refs_0_, f32[528,128]{1,0:T(8,128)S(1)} %collective-permute-done.4.east.refs_1_.refs_3_, f32[528,128]{1,0:T(8,128)S(1)} %collective-permute-done.5.west.refs_2_.refs_4_, f32[5,6,8,128]{3,2,1,0:T(8,128)S(1)} %copy-done.2), custom_call_target="tpu_custom_call" | custom-call | bytes 2000000 | tf_op jit(solution)/shard_map/move_ghosts/pallas_call | solution.py:280
  47.6 0.0 copy-done.3
  47.6 1.9 %chunk.4 = (f32[8,144,128]{2,1,0:T(8,128)S(1)}, f32[4,8,128]{2,1,0:T(8,128)S(1)}) custom-call(f32[5,36]{1,0:T(8,128)S(1)} %copy-done.3, f32[6,36,128]{2,1,0:T(8,128)S(1)} %copy-done.1, f32[36,144,128]{2,1,0:T(8,128)S(1)} %bitcast.9, f32[528,128]{1,0:T(8,128)S(1)} %collective-permute-done.4.east.refs_1_.refs_3_, ...), custom_call_target="tpu_custom_call" | custom-call | bytes 1000000 | tf_op jit(solution)/shard_map/chunk/pallas_call | solution.py:453
  49.5 1.9 %chunk.3 = (f32[8,144,128]{2,1,0:T(8,128)S(1)}, f32[4,8,128]{2,1,0:T(8,128)S(1)}) custom-call(f32[5,36]{1,0:T(8,128)S(1)} %copy-done.3, f32[6,36,128]{2,1,0:T(8,128)S(1)} %copy-done.1, f32[36,144,128]{2,1,0:T(8,128)S(1)} %bitcast.10, f32[440,128]{1,0:T(8,128)S(1)} %collective-permute-done.2.refs_3_, f32[440,128]{1,0:T(8,128)S(1)} %collective-permute-done.3.refs_4_, ...), custom_call_target="tpu_custom_call" | custom-call | bytes 1000000 | tf_op jit(solution)/shard_map/chunk/pallas_call | solution.py:453
  51.4 0.0 collective-permute-done.10.refs_3_
  51.4 2.0 %collective-permute-done.11.refs_4_ = f32[648,128]{1,0:T(8,128)S(1)} collective-permute-done((f32[648,128]{1,0:T(8,128)S(1)}, f32[648,128]{1,0:T(8,128)S(1)}, u32[]{:S(2)}, u32[]{:S(2)}) %collective-permute-start.11) | collective-permute-done | bytes 331808 | tf_op jit(solution)/shard_map/ppermute | solution.py:539
  53.4 2.5 %chunk.5 = (f32[12,144,128]{2,1,0:T(8,128)S(1)}, f32[4,8,128]{2,1,0:T(8,128)S(1)}) custom-call(f32[5,36]{1,0:T(8,128)S(1)} %copy-done.3, f32[6,36,128]{2,1,0:T(8,128)S(1)} %copy-done.1, f32[36,144,128]{2,1,0:T(8,128)S(1)} %bitcast.11, f32[648,128]{1,0:T(8,128)S(1)} %collective-permute-done.10.refs_3_, f32[648,128]{1,0:T(8,128)S(1)} %collective-permute-done.11.refs_4_, ...), custom_call_target="tpu_custom_call" | custom-call | bytes 1000000 | tf_op jit(solution)/shard_map/chunk/pallas_call | solution.py:453
  55.9 0.0 collective-permute-done.8.refs_3_
  55.9 2.0 %collective-permute-done.9.refs_4_ = f32[432,128]{1,0:T(8,128)S(1)} collective-permute-done((f32[432,128]{1,0:T(8,128)S(1)}, f32[432,128]{1,0:T(8,128)S(1)}, u32[]{:S(2)}, u32[]{:S(2)}) %collective-permute-start.9) | collective-permute-done | bytes 221216 | tf_op jit(solution)/shard_map/ppermute | solution.py:539
  57.9 3.6 %last_chunk.1 = f32[36,144,128]{2,1,0:T(8,128)} custom-call(f32[5,36]{1,0:T(8,128)S(1)} %copy-done.3, f32[6,36,128]{2,1,0:T(8,128)S(1)} %copy-done.1, f32[36,144,128]{2,1,0:T(8,128)S(1)} %bitcast.12, f32[432,128]{1,0:T(8,128)S(1)} %collective-permute-done.8.refs_3_, f32[432,128]{1,0:T(8,128)S(1)} %collective-permute-done.9.refs_4_, ...), custom_call_target="tpu_custom_call" | custom-call | bytes 6000000 | tf_op jit(solution)/shard_map/last_chunk/pallas_call | solution.py:506
  (4 shorter events, 0.1 us)
Async XLA Ops:
  0.6 8.9 %copy-start = (f32[36,36,4,128]{3,2,1,0:T(4,128)S(1)}, f32[36,36,4,128]{3,2,1,0:T(4,128)}, u32[]{:S(2)}) copy-start(f32[36,36,4,128]{3,2,1,0:T(4,128)} %param.11) | copy-start | bytes 7962628
  0.6 8.8 %copy-start.6 = (s32[4,128]{1,0:T(4,128)S(1)}, s32[4,128]{1,0:T(4,128)}, u32[]{:S(2)}) copy-start(s32[4,128]{1,0:T(4,128)} %refs_3_.4) | copy-start | bytes 6148
  3.4 14.2 %collective-permute-start.2 = (f32[440,128]{1,0:T(8,128)}, f32[440,128]{1,0:T(8,128)S(1)}, u32[]{:S(2)}, u32[]{:S(2)}) collective-permute-start(f32[440,128]{1,0:T(8,128)} %get-tuple-element.23), channel_id=1, source_target_pairs={{0,4},{4,8},{8,12},{12,16},{16,20},{20,24},{24,28},{28,0},{1,5},{5... | collective-permute-start | bytes 675848 | tf_op jit(solution)/shard_map/ppermute | solution.py:539
  6.4 12.0 %collective-permute-start.3 = (f32[440,128]{1,0:T(8,128)}, f32[440,128]{1,0:T(8,128)S(1)}, u32[]{:S(2)}, u32[]{:S(2)}) collective-permute-start(f32[440,128]{1,0:T(8,128)} %get-tuple-element.24), channel_id=1, source_target_pairs={{4,0},{8,4},{12,8},{16,12},{20,16},{24,20},{28,24},{0,28},{5,1},{9... | collective-permute-start | bytes 675848 | tf_op jit(solution)/shard_map/ppermute | solution.py:539
  9.5 0.7 %copy-start.4 = (f32[8,128]{1,0:T(8,128)S(1)}, f32[8,128]{1,0:T(8,128)}, u32[]{:S(2)}) copy-start(f32[8,128]{1,0:T(8,128)} %get-tuple-element.22.after) | copy-start | bytes 12292
  10.2 13.1 %copy-start.5 = (f32[8,128]{1,0:T(8,128)S(1)}, f32[8,128]{1,0:T(8,128)}, u32[]{:S(2)}) copy-start(f32[8,128]{1,0:T(8,128)} %get-tuple-element.22.after) | copy-start | bytes 12292
  10.2 27.6 %copy-start.1 = (f32[6,36,128]{2,1,0:T(8,128)S(1)}, f32[6,36,128]{2,1,0:T(8,128)}, u32[]{:S(2)}) copy-start(f32[6,36,128]{2,1,0:T(8,128)} %constant.26.clone.refs_2_.refs_1_) | copy-start | bytes 331780
  10.2 27.6 %copy-start.7 = (s32[4,4,128]{2,1,0:T(4,128)S(1)}, s32[4,4,128]{2,1,0:T(4,128)}, u32[]{:S(2)}) copy-start(s32[4,4,128]{2,1,0:T(4,128)} %param.17) | copy-start | bytes 24580
  10.2 27.6 %copy-start.8 = (f32[4,4,128]{2,1,0:T(4,128)S(1)}, f32[4,4,128]{2,1,0:T(4,128)}, u32[]{:S(2)}) copy-start(f32[4,4,128]{2,1,0:T(4,128)} %param.18) | copy-start | bytes 24580
  10.2 27.6 %copy-start.9 = (f32[2,4,128]{2,1,0:T(4,128)S(1)}, f32[2,4,128]{2,1,0:T(4,128)}, u32[]{:S(2)}) copy-start(f32[2,4,128]{2,1,0:T(4,128)} %refs_4_.1) | copy-start | bytes 12292
  12.1 4.4 %collective-permute-start.1 = (f32[4,7,8,128]{3,2,1,0:T(8,128)}, f32[4,7,8,128]{3,2,1,0:T(8,128)S(1)}, u32[]{:S(2)}, u32[]{:S(2)}) collective-permute-start(f32[4,7,8,128]{3,2,1,0:T(8,128)} %pack_edges.1), channel_id=1, source_target_pairs={{1,0},{2,1},{3,2},{5,4},{6,5},{7,6},{9,8},{10,9},{11,10},{13,12},{... | collective-permute-start | bytes 344072 | tf_op jit(solution)/shard_map/ppermute | solution.py:547
  13.4 4.2 %collective-permute-start = (f32[4,7,8,128]{3,2,1,0:T(8,128)}, f32[4,7,8,128]{3,2,1,0:T(8,128)S(1)}, u32[]{:S(2)}, u32[]{:S(2)}) collective-permute-start(f32[4,7,8,128]{3,2,1,0:T(8,128)} %pack_edges.1), channel_id=1, source_target_pairs={{0,1},{1,2},{2,3},{4,5},{5,6},{6,7},{8,9},{9,10},{10,11},{12,13},{... | collective-permute-start | bytes 344072 | tf_op jit(solution)/shard_map/ppermute | solution.py:546
  16.5 29.9 %copy-start.2 = (f32[5,6,8,128]{3,2,1,0:T(8,128)S(1)}, f32[5,6,8,128]{3,2,1,0:T(8,128)}, u32[]{:S(2)}) copy-start(f32[5,6,8,128]{3,2,1,0:T(8,128)} %constant.27.clone.refs_3_) | copy-start | bytes 368644
  18.5 20.0 %collective-permute-start.4 = (f32[528,128]{1,0:T(8,128)S(1)}, f32[528,128]{1,0:T(8,128)S(1)}, u32[]{:S(2)}, u32[]{:S(2)}) collective-permute-start(f32[528,128]{1,0:T(8,128)S(1)} %get-tuple-element.25), channel_id=1, source_target_pairs={{0,4},{4,8},{8,12},{12,16},{16,20},{20,24},{24,28},{28,0},{1,5},{5... | collective-permute-start | bytes 811016 | tf_op jit(solution)/shard_map/ppermute | solution.py:539
  18.9 22.7 %collective-permute-start.5 = (f32[528,128]{1,0:T(8,128)S(1)}, f32[528,128]{1,0:T(8,128)S(1)}, u32[]{:S(2)}, u32[]{:S(2)}) collective-permute-start(f32[528,128]{1,0:T(8,128)S(1)} %get-tuple-element.26), channel_id=1, source_target_pairs={{4,0},{8,4},{12,8},{16,12},{20,16},{24,20},{28,24},{0,28},{5,1},{9... | collective-permute-start | bytes 811016 | tf_op jit(solution)/shard_map/ppermute | solution.py:539
  23.3 6.9 %collective-permute-start.6 = (f32[16,128]{1,0:T(8,128)S(1)}, f32[16,128]{1,0:T(8,128)S(1)}, u32[]{:S(2)}, u32[]{:S(2)}) collective-permute-start(f32[16,128]{1,0:T(8,128)S(1)} %pad_maximum_fusion.1.refs_5_), channel_id=1, source_target_pairs={{0,8},{4,12},{8,0},{12,4},{16,24},{20,28},{24,16},{28,20},{1,9},{5... | collective-permute-start | bytes 24584 | tf_op jit(solution)/shard_map/ppermute | solution.py:555
  23.4 28.0 %collective-permute-start.10 = (f32[648,128]{1,0:T(8,128)S(1)}, f32[648,128]{1,0:T(8,128)S(1)}, u32[]{:S(2)}, u32[]{:S(2)}) collective-permute-start(f32[648,128]{1,0:T(8,128)S(1)} %get-tuple-element.35), channel_id=1, source_target_pairs={{0,4},{4,8},{8,12},{12,16},{16,20},{20,24},{24,28},{28,0},{1,5},{5... | collective-permute-start | bytes 995336 | tf_op jit(solution)/shard_map/ppermute | solution.py:539
  23.5 29.9 %collective-permute-start.11 = (f32[648,128]{1,0:T(8,128)S(1)}, f32[648,128]{1,0:T(8,128)S(1)}, u32[]{:S(2)}, u32[]{:S(2)}) collective-permute-start(f32[648,128]{1,0:T(8,128)S(1)} %get-tuple-element.36), channel_id=1, source_target_pairs={{4,0},{8,4},{12,8},{16,12},{20,16},{24,20},{28,24},{0,28},{5,1},{9... | collective-permute-start | bytes 995336 | tf_op jit(solution)/shard_map/ppermute | solution.py:539
  30.3 7.5 %collective-permute-start.7 = (f32[32,128]{1,0:T(8,128)S(1)}, f32[32,128]{1,0:T(8,128)S(1)}, u32[]{:S(2)}, u32[]{:S(2)}) collective-permute-start(f32[32,128]{1,0:T(8,128)S(1)} %pad_maximum_fusion), channel_id=1, source_target_pairs={{0,16},{4,20},{8,24},{12,28},{16,0},{20,4},{24,8},{28,12},{1,17},{... | collective-permute-start | bytes 49160 | tf_op jit(solution)/shard_map/ppermute | solution.py:555
  41.6 6.0 %copy-start.3 = (f32[5,36]{1,0:T(8,128)S(1)}, f32[5,36]{1,0:T(8,128)}, u32[]{:S(2)}) copy-start(f32[5,36]{1,0:T(8,128)} %constant.28.clone.refs_0_) | copy-start | bytes 2164
  41.6 14.3 %collective-permute-start.8 = (f32[432,128]{1,0:T(8,128)S(1)}, f32[432,128]{1,0:T(8,128)S(1)}, u32[]{:S(2)}, u32[]{:S(2)}) collective-permute-start(f32[432,128]{1,0:T(8,128)S(1)} %get-tuple-element.28), channel_id=1, source_target_pairs={{0,4},{4,8},{8,12},{12,16},{16,20},{20,24},{24,28},{28,0},{1,5},{5... | collective-permute-start | bytes 663560 | tf_op jit(solution)/shard_map/ppermute | solution.py:539
  41.7 16.2 %collective-permute-start.9 = (f32[432,128]{1,0:T(8,128)S(1)}, f32[432,128]{1,0:T(8,128)S(1)}, u32[]{:S(2)}, u32[]{:S(2)}) collective-permute-start(f32[432,128]{1,0:T(8,128)S(1)} %get-tuple-element.29), channel_id=1, source_target_pairs={{4,0},{8,4},{12,8},{16,12},{20,16},{24,20},{28,24},{0,28},{5,1},{9... | collective-permute-start | bytes 663560 | tf_op jit(solution)/shard_map/ppermute | solution.py:539

commit v3 on v2

--- a/solution.py
+++ b/solution.py
@@ -28,8 +28,9 @@
 NEAR_SPLIT = 16
 FAR = DIRS // 2
 PACK = 6
-CHUNKS = (8, 8, 12, 8)
+CHUNKS = (12, 8, 12, 4)
 GROUPS = FREQS // PACK
+PIECE = 4
 EDGE_ROWS = 2 * (FREQS // PACK) * 8
 VMEM = 32 * 1024 * 1024
 FIRST_VMEM = 63000000
@@ -48,6 +49,7 @@
         freqs / freqs[-1],
     ]
 ).astype(np.float32)
+SCALARS = np.ascontiguousarray(np.broadcast_to(SCALARS[:, :, None], (5, FREQS, LANES)))
 ANGLES = np.broadcast_to(
     np.stack(
         [np.abs(np.cos(theta)), np.abs(np.sin(theta)), np.cos(theta), np.sin(theta), np.sin(phi), np.cos(phi)]
@@ -129,7 +131,9 @@
     return lax.broadcasted_iota(jnp.int32, (8, LANES), 1)
 
 
-def first_body(count, x_hbm, hour, wind_hbm, cells_hbm, right, left, packed, x, wind, cells, sem, small):
+def first_body(
+    count, x_hbm, hour_hbm, wind_hbm, cells_hbm, right, left, packed, x, hour, wind, cells, sem, small
+):
     copies = []
     for n in range(count // GROUP):
         span = pl.ds(n * GROUP, GROUP)
@@ -138,12 +142,13 @@
     few = [
         pltpu.make_async_copy(wind_hbm, wind, small.at[0]),
         pltpu.make_async_copy(cells_hbm, cells, small.at[1]),
+        pltpu.make_async_copy(hour_hbm, hour, small.at[2]),
     ]
     for copy in few:
         copy.start()
     for copy in few:
         copy.wait()
-    late = hour[0]
+    late = hour[...]
     now = (1.0 - late) * wind[pl.ds(0, 2), :] + late * wind[pl.ds(2, 2), :]
     width = cells.shape[1]
     index = jnp.concatenate([cells[:, :LANES], cells[:, width - LANES :]] * 4, axis=0)
@@ -164,14 +169,15 @@
     return pl.pallas_call(
         lambda *refs: first_body(count, *refs),
         out_shape=(message(count, 8), message(count, 8), jax.ShapeDtypeStruct((8, LANES), F32)),
-        in_specs=[any_spec(), smem_spec(), any_spec(), any_spec()],
+        in_specs=[any_spec()] * 4,
         out_specs=(vmem_spec(),) * 3,
         scratch_shapes=[
             pltpu.VMEM((count, *x.shape[1:]), F32),
+            pltpu.VMEM(hour.shape, F32),
             pltpu.VMEM(wind.shape, F32),
             pltpu.VMEM(cells.shape, cells.dtype),
             pltpu.SemaphoreType.DMA((count // GROUP,)),
-            pltpu.SemaphoreType.DMA((2,)),
+            pltpu.SemaphoreType.DMA((3,)),
         ],
         compiler_params=pltpu.CompilerParams(vmem_limit_bytes=FIRST_VMEM),
         cost_estimate=pl.CostEstimate(flops=0, bytes_accessed=2000000, transcendentals=0),
@@ -214,44 +220,44 @@
     )(x, sea, after)
 
 
-def middle_body(spans, x, south, north, after_east, after_west, *refs):
-    outs, merged = refs[:-1], refs[-1]
-    row = spans[0][1] * HALO
+def second_body(start, count, x, south, north, right, left, merged):
+    row = count * HALO
     pick = lane_ids() % 4 < 2
     for c in range(CELLS):
-        side, slot = (outs[1], c) if c < 2 else (outs[0], c - 2)
+        side, slot = (left, c) if c < 2 else (right, c - 2)
         for g in range(GROUPS + 1):
             both = jnp.where(pick, south[c, g], north[c, g])
             merged[c, g] = both
             if g < GROUPS:
                 side[pl.ds(row + (slot * GROUPS + g) * 8, 8), :] = both
-    for n, (start, count) in enumerate(spans):
-        halo_rows(x, start, outs[2 * n], outs[2 * n + 1], 0, count)
-
-
-def middle_halos(x, spans, south, north, after):
-    extra = [EDGE_ROWS] + [0] * (len(spans) - 1)
-    return pl.pallas_call(
-        lambda *refs: middle_body(spans, *refs),
-        out_shape=tuple(message(count, more) for (_, count), more in zip(spans, extra) for _ in range(2))
-        + (jax.ShapeDtypeStruct((CELLS, GROUPS + 1, 8, LANES), F32),),
-        in_specs=[vmem_spec()] * 5,
-        out_specs=(vmem_spec(),) * (2 * len(spans) + 1),
+    halo_rows(x, start, right, left, 0, count)
+
+
+def second_halos(x, start, count, south, north):
+    return pl.pallas_call(
+        lambda *refs: second_body(start, count, *refs),
+        out_shape=(
+            message(count, EDGE_ROWS),
+            message(count, EDGE_ROWS),
+            jax.ShapeDtypeStruct((CELLS, GROUPS + 1, 8, LANES), F32),
+        ),
+        in_specs=[vmem_spec()] * 3,
+        out_specs=(vmem_spec(),) * 3,
         compiler_params=pltpu.CompilerParams(vmem_limit_bytes=VMEM),
-        cost_estimate=pl.CostEstimate(flops=0, bytes_accessed=6000000, transcendentals=0),
-        name="middle_halos",
-    )(x, south, north, *after)
-
-
-def last_halos(x, start, count, *after):
-    return pl.pallas_call(
-        lambda x, east, west, winds, right, left: halo_rows(x, start, right, left, 0, count),
+        cost_estimate=pl.CostEstimate(flops=0, bytes_accessed=2000000, transcendentals=0),
+        name="second_halos",
+    )(x, south, north)
+
+
+def later_halos(x, start, count, *after):
+    return pl.pallas_call(
+        lambda x, *refs: halo_rows(x, start, *refs[-2:], 0, count),
         out_shape=(message(count), message(count)),
-        in_specs=[vmem_spec()] * 4,
+        in_specs=[vmem_spec()] * (1 + len(after)),
         out_specs=(vmem_spec(),) * 2,
         compiler_params=pltpu.CompilerParams(vmem_limit_bytes=VMEM),
         cost_estimate=pl.CostEstimate(flops=0, bytes_accessed=1000000, transcendentals=0),
-        name="last_halos",
+        name="later_halos",
     )(x, *after)
 
 
@@ -353,10 +359,7 @@
 
     def one(i, kk, sums):
         k = first + i * GROUP + kk
-        cour = scal[0, k]
-        bend = scal[1, k]
-        rate = scal[2, k]
-        slow = scal[3, k]
+        cour, bend, rate, slow = (scal[n, pl.ds(k, 1), :] for n in range(4))
         for b, j0 in enumerate(BLOCKS):
             w0, w1, w2, w3 = stencil(cour * ang[0, pl.ds(j0, 8), :])
             v0, v1, v2, v3 = stencil(cour * ang[1, pl.ds(j0, 8), :])
@@ -456,7 +459,7 @@
             jax.ShapeDtypeStruct((count, ROWS, LANES), F32),
             jax.ShapeDtypeStruct((CELLS, 8, LANES), F32),
         ),
-        in_specs=[smem_spec()] + [vmem_spec()] * 8,
+        in_specs=[vmem_spec()] * 9,
         out_specs=(vmem_spec(), vmem_spec()),
         scratch_shapes=pass_scratch(),
         compiler_params=pltpu.CompilerParams(vmem_limit_bytes=VMEM),
@@ -485,17 +488,22 @@
         pattern = jnp.where(sub % CELLS == c, damping_rate * (level * level), pattern)
     stores, at = [], 0
     for n, size in enumerate(sizes):
-        def body(i, _, at=at, n=n):
-            scale = jnp.exp(-(scal[4, at + i] * pattern))
-            source, k = (parts[n], i) if n < done else (obuf, at + i)
-            for r in range(0, ROWS, 8):
-                obuf[at + i, pl.ds(r, 8), :] = source[k, pl.ds(r, 8), :] * scale
-            return 0
-
-        lax.fori_loop(0, size, body, 0)
-        span = pl.ds(at, size)
-        stores.append(pltpu.make_async_copy(obuf.at[span], out_hbm.at[span], out_sem.at[n]))
-        stores[-1].start()
+        for low in range(0, size, PIECE):
+            high = min(low + PIECE, size)
+
+            def body(i, _, at=at, n=n):
+                scale = jnp.exp(-(scal[4, pl.ds(at + i, 1), :] * pattern))
+                source, k = (parts[n], i) if n < done else (obuf, at + i)
+                for r in range(0, ROWS, 8):
+                    obuf[at + i, pl.ds(r, 8), :] = source[k, pl.ds(r, 8), :] * scale
+                return 0
+
+            lax.fori_loop(low, high, body, 0)
+            span = pl.ds(at + low, high - low)
+            stores.append(
+                pltpu.make_async_copy(obuf.at[span], out_hbm.at[span], out_sem.at[len(stores)])
+            )
+            stores[-1].start()
         at += size
     for store in stores:
         store.wait()
@@ -506,12 +514,12 @@
     return pl.pallas_call(
         lambda *refs: tail_body(sizes, *refs),
         out_shape=jax.ShapeDtypeStruct((FREQS, ROWS, LANES), F32),
-        in_specs=[smem_spec()] + [vmem_spec()] * (8 + 2 * done),
+        in_specs=[vmem_spec()] * (9 + 2 * done),
         out_specs=any_spec(),
         scratch_shapes=[
             pltpu.VMEM((FREQS, ROWS, LANES), F32),
             *pass_scratch(),
-            pltpu.SemaphoreType.DMA((done + 1,)),
+            pltpu.SemaphoreType.DMA((FREQS // PIECE,)),
         ],
         compiler_params=pltpu.CompilerParams(vmem_limit_bytes=VMEM),
         cost_estimate=pl.CostEstimate(flops=0, bytes_accessed=6000000, transcendentals=0),
@@ -539,14 +547,15 @@
         return lax.ppermute(to_east, "lon", east_way), lax.ppermute(to_west, "lon", west_way)
 
     *sends, packed = first_halos(
-        x, CHUNKS[0], hour_fraction, atm_wind.reshape(4, LANES), send_cells
+        x, CHUNKS[0], hour_fraction.reshape(1, 1), atm_wind.reshape(4, LANES), send_cells
     )
     halos = [exchange(*sends)]
     q = pack_edges(x, sea_mask, packed)
     south = lax.ppermute(q, "lat", north_way)
     north = lax.ppermute(q, "lat", south_way)
-    *sends, merged = middle_halos(x, tuple(zip(firsts, CHUNKS))[1:3], south, north, halos[0])
-    halos += [exchange(*sends[:2]), exchange(*sends[2:])]
+    *sends, merged = second_halos(x, firsts[1], CHUNKS[1], south, north)
+    halos.append(exchange(*sends))
+    halos.append(exchange(*later_halos(x, firsts[2], CHUNKS[2], *halos[0])))
     west, east = (side[-8:] for side in halos[0])
     lists = [jnp.concatenate([packed, jnp.where(lax.axis_index("lon") % 2 == 0, east, west)])]
     step = 2
@@ -563,7 +572,7 @@
         sea_mask,
         refraction,
     )
-    halos.append(exchange(*last_halos(x, firsts[3], CHUNKS[3], *halos[1], tables[0])))
+    halos.append(exchange(*later_halos(x, firsts[3], CHUNKS[3], *halos[1], tables[0])))
     ghosts = move_ghosts(CHUNKS[1], merged, *halos[1])
 
     parts, energies = [], []

time: 61.7 us -> 59.2 us (0.959)
  waiting for transfers between devices: 15.8 us -> 14.1 us
  Pallas kernels: 15.9 us -> 14.5 us
    ppermute x4, waiting for transfers between devices: 7.68 us -> 0.01 us  [exchange(): lax.ppermute(to_west, 'lon', west_way)]
    ppermute x4, waiting for transfers between devices: 0.01 us -> 4.29 us  [exchange(): lax.ppermute(to_east, 'lon', east_way)]
    ppermute x2, waiting for transfers between devices: 6.95 us -> 9.14 us  [local(): lax.ppermute(held, 'lon', [(i, i ^ step) for i in range(tiles)])]
    pallas_call x1, Pallas kernels: 3.56 us -> 2.3 us  [tail_chunk(): pl.pallas_call(lambda *refs: tail_body(sizes, *refs), out_shape=jax.Shape...]
    pallas_call x3, Pallas kernels: 6.34 us -> 5.18 us  [main_chunk(): pl.pallas_call(lambda *refs: main_body(first, count, *refs), out_shape=(j...]
    pallas_call x2 -> x3, Pallas kernels: 0.19 us -> 1.06 us  [the longest x1 0.96 us: second_halos(): pl.pallas_call(lambda *refs: second_body(start, count, *refs), out_shape=...]
    ppermute x1, starting transfers between devices: 3.04 us -> 3.69 us  [local(): south = lax.ppermute(q, 'lat', north_way)]
  transfers between devices with their start and end apart: 12 -> 12, of which waited for: 7 -> 4; matrix products, arithmetic and copies ran while one was open for 0% -> 0% of each run, Pallas kernels for 17% -> 17%
where the time goes in v3:
time: 59.2 us; the launch traced here: 59 us
  starting transfers between devices  28 us (47%)
  Pallas kernels  14.5 us (24%)
  waiting for transfers between devices  14.1 us (24%)
  between operations  1.62 us (3%)
  local copies, waits for them, and re-layouts  0.72 us (1%)
    ppermute x4, starting transfers between devices, exchange(): lax.ppermute(to_west, 'lon', west_way)  16.7 us
    ppermute x2, waiting for transfers between devices, local(): lax.ppermute(held, 'lon', [(i, i ^ step) for i in range(tiles)])  9.14 us
    pallas_call x3, Pallas kernels, main_chunk(): pl.pallas_call(lambda *refs: main_body(first, count, *refs), out_shape=(j...  5.18 us
    ppermute x4, waiting for transfers between devices, exchange(): lax.ppermute(to_east, 'lon', east_way)  4.29 us
    ppermute x4, starting transfers between devices, exchange(): lax.ppermute(to_east, 'lon', east_way)  3.71 us
    ppermute x1, starting transfers between devices, local(): south = lax.ppermute(q, 'lat', north_way)  3.69 us
    ppermute x2, starting transfers between devices, local(): lax.ppermute(held, 'lon', [(i, i ^ step) for i in range(tiles)])  2.64 us
    pallas_call x1, Pallas kernels, tail_chunk(): pl.pallas_call(lambda *refs: tail_body(sizes, *refs), out_shape=jax.Shape...  2.3 us
  transfers between devices with their start and end apart: 12, of which 4 were waited for; matrix products, arithmetic and copies ran while one was open for 0% of the time, Pallas kernels for 17%

profile of v3, /device:TPU:0, one launch (start us, length us, event | category | flops | bytes accessed | tf_op | source)
XLA Modules:
  0.0 59.0 jit_solution(3628199419662197382)
XLA Ops:
  0.6 0.0 copy-start
  0.6 0.0 copy-start.6
  1.4 2.1 %first_halos.1 = (f32[656,128]{1,0:T(8,128)}, f32[656,128]{1,0:T(8,128)}, f32[8,128]{1,0:T(8,128)}) custom-call(f32[36,144,128]{2,1,0:T(8,128)} %bitcast.7, f32[1,1]{1,0:T(1,128)} %bitcast.6.refs_1_, f32[4,128]{1,0:T(4,128)} %bitcast.19, s32[1,192]{1,0:T(1,128)} %refs_3_.3), custom_call_target="tpu_custom_call" | custom-call | bytes 2000000 | tf_op jit(solution)/shard_map/first_halos/pallas_call | solution.py:169
  3.5 6.1 %collective-permute-start.4 = (f32[656,128]{1,0:T(8,128)}, f32[656,128]{1,0:T(8,128)S(1)}, u32[]{:S(2)}, u32[]{:S(2)}) collective-permute-start(f32[656,128]{1,0:T(8,128)} %get-tuple-element.25), channel_id=1, source_target_pairs={{4,0},{8,4},{12,8},{16,12},{20,16},{24,20},{28,24},{0,28},{5,1},{9... | collective-permute-start | bytes 1007624 | tf_op jit(solution)/shard_map/ppermute | solution.py:547
  9.6 0.0 collective-permute-start.5
  9.6 0.0 copy-done
  9.6 0.0 copy-done.6
  9.6 0.0 copy-start.4
  9.6 0.7 %copy-done.4 = f32[8,128]{1,0:T(8,128)S(1)} copy-done((f32[8,128]{1,0:T(8,128)S(1)}, f32[8,128]{1,0:T(8,128)}, u32[]{:S(2)}) %copy-start.4) | copy-done | bytes 4120
  10.3 1.9 %pack_edges.1 = f32[4,7,8,128]{3,2,1,0:T(8,128)} custom-call(f32[36,144,128]{2,1,0:T(8,128)S(1)} %bitcast.8, s32[4,128]{1,0:T(4,128)S(1)} %copy-done.6, f32[8,128]{1,0:T(8,128)S(1)} %copy-done.4), custom_call_target="tpu_custom_call" | custom-call | bytes 4000000 | tf_op jit(solution)/shard_map/pack_edges/pallas_call | solution.py:212
  12.2 1.3 %collective-permute-start.1 = (f32[4,7,8,128]{3,2,1,0:T(8,128)}, f32[4,7,8,128]{3,2,1,0:T(8,128)S(1)}, u32[]{:S(2)}, u32[]{:S(2)}) collective-permute-start(f32[4,7,8,128]{3,2,1,0:T(8,128)} %pack_edges.1), channel_id=1, source_target_pairs={{1,0},{2,1},{3,2},{5,4},{6,5},{7,6},{9,8},{10,9},{11,10},{13,12},{... | collective-permute-start | bytes 344072 | tf_op jit(solution)/shard_map/ppermute | solution.py:555
  13.5 3.7 %collective-permute-start = (f32[4,7,8,128]{3,2,1,0:T(8,128)}, f32[4,7,8,128]{3,2,1,0:T(8,128)}, u32[]{:S(2)}, u32[]{:S(2)}) collective-permute-start(f32[4,7,8,128]{3,2,1,0:T(8,128)} %pack_edges.1), channel_id=1, source_target_pairs={{0,1},{1,2},{2,3},{4,5},{5,6},{6,7},{8,9},{9,10},{10,11},{12,13},{... | collective-permute-start | bytes 344072 | tf_op jit(solution)/shard_map/ppermute | solution.py:554
  17.2 0.0 copy-start.5
  17.2 0.0 copy-start.1
  17.2 0.0 copy-start.7
  17.2 0.0 copy-start.8
  17.2 0.0 copy-start.9
  17.2 0.0 collective-permute-done.1.refs_2_
  17.2 0.6 %collective-permute-done.refs_1_ = f32[4,7,8,128]{3,2,1,0:T(8,128)} collective-permute-done((f32[4,7,8,128]{3,2,1,0:T(8,128)}, f32[4,7,8,128]{3,2,1,0:T(8,128)}, u32[]{:S(2)}, u32[]{:S(2)}) %collective-permute-start) | collective-permute-done | bytes 114720 | tf_op jit(solution)/shard_map/ppermute | solution.py:554
  17.8 1.0 %second_halos.1 = (f32[528,128]{1,0:T(8,128)S(1)}, f32[528,128]{1,0:T(8,128)S(1)}, f32[4,7,8,128]{3,2,1,0:T(8,128)S(1)}) custom-call(f32[36,144,128]{2,1,0:T(8,128)S(1)} %bitcast.9, f32[4,7,8,128]{3,2,1,0:T(8,128)} %collective-permute-done.refs_1_, f32[4,7,8,128]{3,2,1,0:T(8,128)S(1)} %collective-permute-done.1.refs_2_), custom_call_target="tpu_custom_call" | custom-call | bytes 2000000 | tf_op jit(solution)/shard_map/second_halos/pallas_call | solution.py:237
  18.8 0.1 collective-permute-start.2
  18.9 0.0 copy-start.3
  18.9 4.8 %collective-permute-start.3 = (f32[528,128]{1,0:T(8,128)S(1)}, f32[528,128]{1,0:T(8,128)S(1)}, u32[]{:S(2)}, u32[]{:S(2)}) collective-permute-start(f32[528,128]{1,0:T(8,128)S(1)} %get-tuple-element.24), channel_id=1, source_target_pairs={{4,0},{8,4},{12,8},{16,12},{20,16},{24,20},{28,24},{0,28},{5,1},{9... | collective-permute-start | bytes 811016 | tf_op jit(solution)/shard_map/ppermute | solution.py:547
  23.7 0.0 collective-permute-done.4.refs_4_.refs_1_
  23.7 4.3 %collective-permute-done.5.refs_3_.refs_0_ = f32[656,128]{1,0:T(8,128)S(1)} collective-permute-done((f32[656,128]{1,0:T(8,128)}, f32[656,128]{1,0:T(8,128)S(1)}, u32[]{:S(2)}, u32[]{:S(2)}) %collective-permute-start.5) | collective-permute-done | bytes 335904 | tf_op jit(solution)/shard_map/ppermute | solution.py:547
  27.9 0.1 later_halos.3
  28.0 2.5 %collective-permute-start.10 = (f32[648,128]{1,0:T(8,128)S(1)}, f32[648,128]{1,0:T(8,128)S(1)}, u32[]{:S(2)}, u32[]{:S(2)}) collective-permute-start(f32[648,128]{1,0:T(8,128)S(1)} %get-tuple-element.35), channel_id=1, source_target_pairs={{0,4},{4,8},{8,12},{12,16},{16,20},{20,24},{24,28},{28,0},{1,5},{5... | collective-permute-start | bytes 995336 | tf_op jit(solution)/shard_map/ppermute | solution.py:547
  30.5 2.3 %collective-permute-start.11 = (f32[648,128]{1,0:T(8,128)S(1)}, f32[648,128]{1,0:T(8,128)S(1)}, u32[]{:S(2)}, u32[]{:S(2)}) collective-permute-start(f32[648,128]{1,0:T(8,128)S(1)} %get-tuple-element.36), channel_id=1, source_target_pairs={{4,0},{8,4},{12,8},{16,12},{20,16},{24,20},{28,24},{0,28},{5,1},{9... | collective-permute-start | bytes 995336 | tf_op jit(solution)/shard_map/ppermute | solution.py:547
  32.8 0.0 copy-done.5
  32.8 0.9 %collective-permute-start.6 = (f32[16,128]{1,0:T(8,128)S(1)}, f32[16,128]{1,0:T(8,128)S(1)}, u32[]{:S(2)}, u32[]{:S(2)}) collective-permute-start(f32[16,128]{1,0:T(8,128)S(1)} %pad_maximum_fusion.1.refs_5_), channel_id=1, source_target_pairs={{0,8},{4,12},{8,0},{12,4},{16,24},{20,28},{24,16},{28,20},{1,9},{5... | collective-permute-start | bytes 24584 | tf_op jit(solution)/shard_map/ppermute | solution.py:564
  33.7 6.2 %collective-permute-done.6.refs_6_ = f32[16,128]{1,0:T(8,128)S(1)} collective-permute-done((f32[16,128]{1,0:T(8,128)S(1)}, f32[16,128]{1,0:T(8,128)S(1)}, u32[]{:S(2)}, u32[]{:S(2)}) %collective-permute-start.6) | collective-permute-done | bytes 8224 | tf_op jit(solution)/shard_map/ppermute | solution.py:564
  40.0 1.7 %collective-permute-start.7 = (f32[32,128]{1,0:T(8,128)S(1)}, f32[32,128]{1,0:T(8,128)S(1)}, u32[]{:S(2)}, u32[]{:S(2)}) collective-permute-start(f32[32,128]{1,0:T(8,128)S(1)} %pad_maximum_fusion), channel_id=1, source_target_pairs={{0,16},{4,20},{8,24},{12,28},{16,0},{20,4},{24,8},{28,12},{1,17},{... | collective-permute-start | bytes 49160 | tf_op jit(solution)/shard_map/ppermute | solution.py:564
  41.7 2.9 %collective-permute-done.7.refs_7_ = f32[32,128]{1,0:T(8,128)S(1)} collective-permute-done((f32[32,128]{1,0:T(8,128)S(1)}, f32[32,128]{1,0:T(8,128)S(1)}, u32[]{:S(2)}, u32[]{:S(2)}) %collective-permute-start.7) | collective-permute-done | bytes 16416 | tf_op jit(solution)/shard_map/ppermute | solution.py:564
  44.6 0.0 copy-done.1
  44.6 0.0 copy-done.7
  44.6 0.0 copy-done.8
  44.6 0.0 copy-done.9
  44.6 0.8 %surface_wind.1 = (f32[2,4,128]{2,1,0:T(4,128)}, f32[4,8,128]{2,1,0:T(8,128)S(1)}, f32[4,36,128]{2,1,0:T(8,128)S(1)}, f32[4,36,128]{2,1,0:T(8,128)S(1)}) custom-call(s32[16,128]{1,0:T(8,128)S(1)} %bitcast.16, f32[16,128]{1,0:T(8,128)S(1)} %bitcast.17, f32[6,36,128]{2,1,0:T(8,128)S(1)} %copy-done.1, s32[4,128]{1,0:T(4,128)S(1)} %copy-done.6, ...), custom_call_target="tpu_custom_call" | custom-call | bytes 2000000 | tf_op jit(solution)/shard_map/surface_wind/pallas_call | solution.py:336
  45.4 0.0 collective-permute-done.2.refs_0_.refs_1_.refs_3_
  45.4 0.0 collective-permute-done.3.refs_1_.refs_2_.refs_4_
  45.5 0.0 copy-start.2
  45.5 1.2 %collective-permute-start.8 = (f32[216,128]{1,0:T(8,128)S(1)}, f32[216,128]{1,0:T(8,128)S(1)}, u32[]{:S(2)}, u32[]{:S(2)}) collective-permute-start(f32[216,128]{1,0:T(8,128)S(1)} %get-tuple-element.28), channel_id=1, source_target_pairs={{0,4},{4,8},{8,12},{12,16},{16,20},{20,24},{24,28},{28,0},{1,5},{5... | collective-permute-start | bytes 331784 | tf_op jit(solution)/shard_map/ppermute | solution.py:547
  46.6 3.6 %collective-permute-start.9 = (f32[216,128]{1,0:T(8,128)S(1)}, f32[216,128]{1,0:T(8,128)S(1)}, u32[]{:S(2)}, u32[]{:S(2)}) collective-permute-start(f32[216,128]{1,0:T(8,128)S(1)} %get-tuple-element.29), channel_id=1, source_target_pairs={{4,0},{8,4},{12,8},{16,12},{20,16},{24,20},{28,24},{0,28},{5,1},{9... | collective-permute-start | bytes 331784 | tf_op jit(solution)/shard_map/ppermute | solution.py:547
  50.2 0.0 copy-done.3
  50.2 1.2 %move_ghosts.1.refs_5_ = f32[36,4,5,8,128]{4,3,2,1,0:T(8,128)S(1)} custom-call(f32[4,7,8,128]{3,2,1,0:T(8,128)S(1)} %get-tuple-element.30.refs_0_, f32[528,128]{1,0:T(8,128)S(1)} %collective-permute-done.2.refs_0_.refs_1_.refs_3_, f32[528,128]{1,0:T(8,128)S(1)} %collective-permute-done.3.refs_1_.refs_2_.refs_4_, f32[5,6,8,128]{3,2,1,0:T(8,128)S(1)} %copy-done.3), custom_call_target="tpu_custom_call" | custom-call | bytes 2000000 | tf_op jit(solution)/shard_map/move_ghosts/pallas_call | solution.py:286
  51.4 0.0 copy-done.2
  51.5 1.3 %chunk.4 = (f32[8,144,128]{2,1,0:T(8,128)S(1)}, f32[4,8,128]{2,1,0:T(8,128)S(1)}) custom-call(f32[5,36,128]{2,1,0:T(8,128)S(1)} %copy-done.2, f32[6,36,128]{2,1,0:T(8,128)S(1)} %copy-done.1, f32[36,144,128]{2,1,0:T(8,128)S(1)} %bitcast.12, f32[528,128]{1,0:T(8,128)S(1)} %collective-permute-done.2.refs_0_.refs_1_.refs_3_, ...), custom_call_target="tpu_custom_call" | custom-call | bytes 1000000 | tf_op jit(solution)/shard_map/chunk/pallas_call | solution.py:456
  52.8 1.9 %chunk.3 = (f32[12,144,128]{2,1,0:T(8,128)S(1)}, f32[4,8,128]{2,1,0:T(8,128)S(1)}) custom-call(f32[5,36,128]{2,1,0:T(8,128)S(1)} %copy-done.2, f32[6,36,128]{2,1,0:T(8,128)S(1)} %copy-done.1, f32[36,144,128]{2,1,0:T(8,128)S(1)} %bitcast.13, f32[656,128]{1,0:T(8,128)S(1)} %collective-permute-done.5.refs_3_.refs_0_, ...), custom_call_target="tpu_custom_call" | custom-call | bytes 1000000 | tf_op jit(solution)/shard_map/chunk/pallas_call | solution.py:456
  54.7 0.0 collective-permute-done.10.refs_3_
  54.7 0.0 collective-permute-done.11.refs_4_
  54.7 1.9 %chunk.5 = (f32[12,144,128]{2,1,0:T(8,128)S(1)}, f32[4,8,128]{2,1,0:T(8,128)S(1)}) custom-call(f32[5,36,128]{2,1,0:T(8,128)S(1)} %copy-done.2, f32[6,36,128]{2,1,0:T(8,128)S(1)} %copy-done.1, f32[36,144,128]{2,1,0:T(8,128)S(1)} %bitcast.14, f32[648,128]{1,0:T(8,128)S(1)} %collective-permute-done.10.refs_3_, f32[648,128]{1,0:T(8,128)S(1)} %collective-permute-done.11.refs_4_, ...), custom_call_target="tpu_custom_call" | custom-call | bytes 1000000 | tf_op jit(solution)/shard_map/chunk/pallas_call | solution.py:456
  56.7 0.0 collective-permute-done.8.refs_3_
  56.7 0.0 collective-permute-done.9.refs_4_
  56.7 2.3 %last_chunk.1 = f32[36,144,128]{2,1,0:T(8,128)} custom-call(f32[5,36,128]{2,1,0:T(8,128)S(1)} %copy-done.2, f32[6,36,128]{2,1,0:T(8,128)S(1)} %copy-done.1, f32[36,144,128]{2,1,0:T(8,128)S(1)} %bitcast.15, f32[216,128]{1,0:T(8,128)S(1)} %collective-permute-done.8.refs_3_, f32[216,128]{1,0:T(8,128)S(1)} %collective-permute-done.9.refs_4_, ...), custom_call_target="tpu_custom_call" | custom-call | bytes 6000000 | tf_op jit(solution)/shard_map/last_chunk/pallas_call | solution.py:514
  (4 shorter events, 0.0 us)
Async XLA Ops:
  0.6 9.0 %copy-start = (f32[36,36,4,128]{3,2,1,0:T(4,128)S(1)}, f32[36,36,4,128]{3,2,1,0:T(4,128)}, u32[]{:S(2)}) copy-start(f32[36,36,4,128]{3,2,1,0:T(4,128)} %param.11) | copy-start | bytes 7962628
  0.6 9.0 %copy-start.6 = (s32[4,128]{1,0:T(4,128)S(1)}, s32[4,128]{1,0:T(4,128)}, u32[]{:S(2)}) copy-start(s32[4,128]{1,0:T(4,128)} %refs_3_.4) | copy-start | bytes 6148
  3.5 20.1 %collective-permute-start.4 = (f32[656,128]{1,0:T(8,128)}, f32[656,128]{1,0:T(8,128)S(1)}, u32[]{:S(2)}, u32[]{:S(2)}) collective-permute-start(f32[656,128]{1,0:T(8,128)} %get-tuple-element.25), channel_id=1, source_target_pairs={{4,0},{8,4},{12,8},{16,12},{20,16},{24,20},{28,24},{0,28},{5,1},{9... | collective-permute-start | bytes 1007624 | tf_op jit(solution)/shard_map/ppermute | solution.py:547
  9.6 18.3 %collective-permute-start.5 = (f32[656,128]{1,0:T(8,128)}, f32[656,128]{1,0:T(8,128)S(1)}, u32[]{:S(2)}, u32[]{:S(2)}) collective-permute-start(f32[656,128]{1,0:T(8,128)} %get-tuple-element.26), channel_id=1, source_target_pairs={{0,4},{4,8},{8,12},{12,16},{16,20},{20,24},{24,28},{28,0},{1,5},{5... | collective-permute-start | bytes 1007624 | tf_op jit(solution)/shard_map/ppermute | solution.py:547
  9.6 0.7 %copy-start.4 = (f32[8,128]{1,0:T(8,128)S(1)}, f32[8,128]{1,0:T(8,128)}, u32[]{:S(2)}) copy-start(f32[8,128]{1,0:T(8,128)} %get-tuple-element.22.after) | copy-start | bytes 12292
  12.2 5.0 %collective-permute-start.1 = (f32[4,7,8,128]{3,2,1,0:T(8,128)}, f32[4,7,8,128]{3,2,1,0:T(8,128)S(1)}, u32[]{:S(2)}, u32[]{:S(2)}) collective-permute-start(f32[4,7,8,128]{3,2,1,0:T(8,128)} %pack_edges.1), channel_id=1, source_target_pairs={{1,0},{2,1},{3,2},{5,4},{6,5},{7,6},{9,8},{10,9},{11,10},{13,12},{... | collective-permute-start | bytes 344072 | tf_op jit(solution)/shard_map/ppermute | solution.py:555
  13.5 4.3 %collective-permute-start = (f32[4,7,8,128]{3,2,1,0:T(8,128)}, f32[4,7,8,128]{3,2,1,0:T(8,128)}, u32[]{:S(2)}, u32[]{:S(2)}) collective-permute-start(f32[4,7,8,128]{3,2,1,0:T(8,128)} %pack_edges.1), channel_id=1, source_target_pairs={{0,1},{1,2},{2,3},{4,5},{5,6},{6,7},{8,9},{9,10},{10,11},{12,13},{... | collective-permute-start | bytes 344072 | tf_op jit(solution)/shard_map/ppermute | solution.py:554
  17.2 15.6 %copy-start.5 = (f32[8,128]{1,0:T(8,128)S(1)}, f32[8,128]{1,0:T(8,128)}, u32[]{:S(2)}) copy-start(f32[8,128]{1,0:T(8,128)} %get-tuple-element.22.after) | copy-start | bytes 12292
  17.2 27.4 %copy-start.1 = (f32[6,36,128]{2,1,0:T(8,128)S(1)}, f32[6,36,128]{2,1,0:T(8,128)}, u32[]{:S(2)}) copy-start(f32[6,36,128]{2,1,0:T(8,128)} %constant.26.clone.refs_2_.refs_1_) | copy-start | bytes 331780
  17.2 27.4 %copy-start.7 = (s32[4,4,128]{2,1,0:T(4,128)S(1)}, s32[4,4,128]{2,1,0:T(4,128)}, u32[]{:S(2)}) copy-start(s32[4,4,128]{2,1,0:T(4,128)} %param.17) | copy-start | bytes 24580
  17.2 27.4 %copy-start.8 = (f32[4,4,128]{2,1,0:T(4,128)S(1)}, f32[4,4,128]{2,1,0:T(4,128)}, u32[]{:S(2)}) copy-start(f32[4,4,128]{2,1,0:T(4,128)} %param.18) | copy-start | bytes 24580
  17.2 27.4 %copy-start.9 = (f32[2,4,128]{2,1,0:T(4,128)S(1)}, f32[2,4,128]{2,1,0:T(4,128)}, u32[]{:S(2)}) copy-start(f32[2,4,128]{2,1,0:T(4,128)} %refs_4_.1) | copy-start | bytes 12292
  18.8 26.6 %collective-permute-start.2 = (f32[528,128]{1,0:T(8,128)S(1)}, f32[528,128]{1,0:T(8,128)S(1)}, u32[]{:S(2)}, u32[]{:S(2)}) collective-permute-start(f32[528,128]{1,0:T(8,128)S(1)} %get-tuple-element.23), channel_id=1, source_target_pairs={{0,4},{4,8},{8,12},{12,16},{16,20},{20,24},{24,28},{28,0},{1,5},{5... | collective-permute-start | bytes 811016 | tf_op jit(solution)/shard_map/ppermute | solution.py:547
  18.9 31.4 %copy-start.3 = (f32[5,6,8,128]{3,2,1,0:T(8,128)S(1)}, f32[5,6,8,128]{3,2,1,0:T(8,128)}, u32[]{:S(2)}) copy-start(f32[5,6,8,128]{3,2,1,0:T(8,128)} %constant.27.clone.refs_3_) | copy-start | bytes 368644
  18.9 26.5 %collective-permute-start.3 = (f32[528,128]{1,0:T(8,128)S(1)}, f32[528,128]{1,0:T(8,128)S(1)}, u32[]{:S(2)}, u32[]{:S(2)}) collective-permute-start(f32[528,128]{1,0:T(8,128)S(1)} %get-tuple-element.24), channel_id=1, source_target_pairs={{4,0},{8,4},{12,8},{16,12},{20,16},{24,20},{28,24},{0,28},{5,1},{9... | collective-permute-start | bytes 811016 | tf_op jit(solution)/shard_map/ppermute | solution.py:547
  28.0 26.7 %collective-permute-start.10 = (f32[648,128]{1,0:T(8,128)S(1)}, f32[648,128]{1,0:T(8,128)S(1)}, u32[]{:S(2)}, u32[]{:S(2)}) collective-permute-start(f32[648,128]{1,0:T(8,128)S(1)} %get-tuple-element.35), channel_id=1, source_target_pairs={{0,4},{4,8},{8,12},{12,16},{16,20},{20,24},{24,28},{28,0},{1,5},{5... | collective-permute-start | bytes 995336 | tf_op jit(solution)/shard_map/ppermute | solution.py:547
  30.5 24.2 %collective-permute-start.11 = (f32[648,128]{1,0:T(8,128)S(1)}, f32[648,128]{1,0:T(8,128)S(1)}, u32[]{:S(2)}, u32[]{:S(2)}) collective-permute-start(f32[648,128]{1,0:T(8,128)S(1)} %get-tuple-element.36), channel_id=1, source_target_pairs={{4,0},{8,4},{12,8},{16,12},{20,16},{24,20},{28,24},{0,28},{5,1},{9... | collective-permute-start | bytes 995336 | tf_op jit(solution)/shard_map/ppermute | solution.py:547
  32.8 7.1 %collective-permute-start.6 = (f32[16,128]{1,0:T(8,128)S(1)}, f32[16,128]{1,0:T(8,128)S(1)}, u32[]{:S(2)}, u32[]{:S(2)}) collective-permute-start(f32[16,128]{1,0:T(8,128)S(1)} %pad_maximum_fusion.1.refs_5_), channel_id=1, source_target_pairs={{0,8},{4,12},{8,0},{12,4},{16,24},{20,28},{24,16},{28,20},{1,9},{5... | collective-permute-start | bytes 24584 | tf_op jit(solution)/shard_map/ppermute | solution.py:564
  40.0 4.6 %collective-permute-start.7 = (f32[32,128]{1,0:T(8,128)S(1)}, f32[32,128]{1,0:T(8,128)S(1)}, u32[]{:S(2)}, u32[]{:S(2)}) collective-permute-start(f32[32,128]{1,0:T(8,128)S(1)} %pad_maximum_fusion), channel_id=1, source_target_pairs={{0,16},{4,20},{8,24},{12,28},{16,0},{20,4},{24,8},{28,12},{1,17},{... | collective-permute-start | bytes 49160 | tf_op jit(solution)/shard_map/ppermute | solution.py:564
  45.5 6.0 %copy-start.2 = (f32[5,36,128]{2,1,0:T(8,128)S(1)}, f32[5,36,128]{2,1,0:T(8,128)}, u32[]{:S(2)}) copy-start(f32[5,36,128]{2,1,0:T(8,128)} %constant.28.clone.refs_0_) | copy-start | bytes 276484
  45.5 11.2 %collective-permute-start.8 = (f32[216,128]{1,0:T(8,128)S(1)}, f32[216,128]{1,0:T(8,128)S(1)}, u32[]{:S(2)}, u32[]{:S(2)}) collective-permute-start(f32[216,128]{1,0:T(8,128)S(1)} %get-tuple-element.28), channel_id=1, source_target_pairs={{0,4},{4,8},{8,12},{12,16},{16,20},{20,24},{24,28},{28,0},{1,5},{5... | collective-permute-start | bytes 331784 | tf_op jit(solution)/shard_map/ppermute | solution.py:547
  46.6 10.1 %collective-permute-start.9 = (f32[216,128]{1,0:T(8,128)S(1)}, f32[216,128]{1,0:T(8,128)S(1)}, u32[]{:S(2)}, u32[]{:S(2)}) collective-permute-start(f32[216,128]{1,0:T(8,128)S(1)} %get-tuple-element.29), channel_id=1, source_target_pairs={{4,0},{8,4},{12,8},{16,12},{20,16},{24,20},{28,24},{0,28},{5,1},{9... | collective-permute-start | bytes 331784 | tf_op jit(solution)/shard_map/ppermute | solution.py:547

commit v4 on v3

--- a/solution.py
+++ b/solution.py
@@ -103,21 +103,24 @@
     return pl.BlockSpec(memory_space=pltpu.SMEM)
 
 
-def halo_rows(x, start, right, left, low, high):
+def is_even():
+    return jnp.full((8, LANES), lax.axis_index("lon") % 2) == 0
+
+
+def halo_rows(x, start, one, two, low, high):
+    even = is_even()
+
     def body(i, _):
         for kk in range(GROUP):
             k = start + i * GROUP + kk
-            for ref, near, far in ((right, 3, 2), (left, 0, 1)):
-                if far == 2:
-                    runs = ((16, 0, 8), (24, 8, 1), (25, 27, 8), (33, 35, 1))
-                else:
-                    runs = ((16, 9, 8), (24, 17, 8), (32, 25, 2))
-                for cell, rows in (
-                    (near, ((0, 0, 8), (8, 8, 8), (34, 16, 8), (42, 24, 8), (50, 32, 4))),
-                    (far, runs),
-                ):
-                    for row, j, n in rows:
-                        ref[halo_at(i, kk, row, n), :] = x[k, pl.ds(cell + 4 * j, n, stride=4), :]
+            near = ((0, 0, 0, 8), (8, 8, 8, 8), (34, 16, 16, 8), (42, 24, 24, 8), (50, 32, 32, 4))
+            far = ((16, 0, 9, 8), (24, 8, 17, 1), (25, 27, 18, 8), (33, 35, 26, 1))
+            for cell_e, cell_w, runs in ((3, 0, near), (2, 1, far)):
+                for row, j_e, j_w, n in runs:
+                    east = x[k, pl.ds(cell_e + 4 * j_e, n, stride=4), :]
+                    west = x[k, pl.ds(cell_w + 4 * j_w, n, stride=4), :]
+                    one[halo_at(i, kk, row, n), :] = jnp.where(even[:n], east, west)
+                    two[halo_at(i, kk, row, n), :] = jnp.where(even[:n], west, east)
         return 0
 
     lax.fori_loop(low // GROUP, high // GROUP, body, 0)
@@ -132,7 +135,7 @@
 
 
 def first_body(
-    count, x_hbm, hour_hbm, wind_hbm, cells_hbm, right, left, packed, x, hour, wind, cells, sem, small
+    count, x_hbm, hour_hbm, wind_hbm, cells_hbm, one, two, packed, x, hour, wind, cells, sem, small
 ):
     copies = []
     for n in range(count // GROUP):
@@ -154,11 +157,11 @@
     index = jnp.concatenate([cells[:, :LANES], cells[:, width - LANES :]] * 4, axis=0)
     table = jnp.concatenate([now[:1]] * 2 + [now[1:]] * 2 + [now[:1]] * 4, axis=0)
     listed = jnp.take_along_axis(table, index, axis=1)
-    for ref, row in ((packed, 0), (right, count * HALO), (left, count * HALO)):
-        ref[pl.ds(row, 8), :] = listed
+    packed[...] = listed
+    one[pl.ds(count * HALO, 8), :] = listed
     for n in range(count // GROUP):
         copies[n].wait()
-        halo_rows(x, 0, right, left, n * GROUP, (n + 1) * GROUP)
+        halo_rows(x, 0, one, two, n * GROUP, (n + 1) * GROUP)
 
 
 def message(count, extra=0):
@@ -168,7 +171,7 @@
 def first_halos(x, count, hour, wind, cells):
     return pl.pallas_call(
         lambda *refs: first_body(count, *refs),
-        out_shape=(message(count, 8), message(count, 8), jax.ShapeDtypeStruct((8, LANES), F32)),
+        out_shape=(message(count, 8), message(count), jax.ShapeDtypeStruct((8, LANES), F32)),
         in_specs=[any_spec()] * 4,
         out_specs=(vmem_spec(),) * 3,
         scratch_shapes=[
@@ -220,17 +223,24 @@
     )(x, sea, after)
 
 
-def second_body(start, count, x, south, north, right, left, merged):
-    row = count * HALO
+def second_body(start, count, x, south, north, one, two, merged):
     pick = lane_ids() % 4 < 2
+    even = is_even()
+
+    def body(g, _):
+        both = [jnp.where(pick, south[c, g], north[c, g]) for c in range(CELLS)]
+        for c in range(CELLS):
+            merged[c, g] = both[c]
+        for n in range(2):
+            row = pl.ds(pl.multiple_of(count * HALO + (n * GROUPS + g) * 8, 8), 8)
+            one[row, :] = jnp.where(even, both[2 + n], both[n])
+            two[row, :] = jnp.where(even, both[n], both[2 + n])
+        return 0
+
+    lax.fori_loop(0, GROUPS, body, 0)
     for c in range(CELLS):
-        side, slot = (left, c) if c < 2 else (right, c - 2)
-        for g in range(GROUPS + 1):
-            both = jnp.where(pick, south[c, g], north[c, g])
-            merged[c, g] = both
-            if g < GROUPS:
-                side[pl.ds(row + (slot * GROUPS + g) * 8, 8), :] = both
-    halo_rows(x, start, right, left, 0, count)
+        merged[c, GROUPS] = jnp.where(pick, south[c, GROUPS], north[c, GROUPS])
+    halo_rows(x, start, one, two, 0, count)
 
 
 def second_halos(x, start, count, south, north):
@@ -261,13 +271,16 @@
     )(x, *after)
 
 
-def ghost_body(count, merged, west, east, weights, ghosts):
+def ghost_body(count, merged, one, two, weights, ghosts):
+    even = is_even()
+
     def body(g, _):
         rows = [
             pl.ds(pl.multiple_of(count * HALO + (n * GROUPS + g) * 8, 8), 8) for n in range(2)
         ]
-        ext = [west[rows[0], :], west[rows[1], :]] + [merged[c, g] for c in range(CELLS)]
-        ext += [east[rows[0], :], east[rows[1], :]]
+        west = [jnp.where(even, two[row, :], one[row, :]) for row in rows]
+        east = [jnp.where(even, one[row, :], two[row, :]) for row in rows]
+        ext = west + [merged[c, g] for c in range(CELLS)] + east
         for c in range(CELLS):
             total = weights[0, g] * ext[c]
             for d in range(1, 5):
@@ -282,7 +295,7 @@
     lax.fori_loop(0, GROUPS, body, 0)
 
 
-def move_ghosts(count, merged, west, east):
+def move_ghosts(count, merged, one, two):
     return pl.pallas_call(
         lambda *refs: ghost_body(count, *refs),
         out_shape=jax.ShapeDtypeStruct((FREQS, CELLS, len(BLOCKS), 8, LANES), F32),
@@ -291,7 +304,7 @@
         compiler_params=pltpu.CompilerParams(vmem_limit_bytes=VMEM),
         cost_estimate=pl.CostEstimate(flops=0, bytes_accessed=2000000, transcendentals=0),
         name="move_ghosts",
-    )(merged, west, east, PACKED)
+    )(merged, one, two, PACKED)
 
 
 def wind_body(cap, sources, slots, weights, ang, sea, refr, *rest):
@@ -351,11 +364,18 @@
 
 
 def chunk_pass(
-    first, count, scal, ang, x, from_west, from_east, ghosts, sea8, turn, proj, zs, gs, out, out_first
+    first, count, scal, ang, x, one_ref, two_ref, ghosts, sea8, turn, proj, zs, gs, out, out_first
 ):
     lane = lane_ids()
     sub = lax.broadcasted_iota(jnp.int32, (8, LANES), 0)
     near_rows = (0, 8, 34, 42, 46)
+    even = is_even()
+
+    def from_west(rows):
+        return jnp.where(even, two_ref[rows, :], one_ref[rows, :])
+
+    def from_east(rows):
+        return jnp.where(even, one_ref[rows, :], two_ref[rows, :])
 
     def one(i, kk, sums):
         k = first + i * GROUP + kk
@@ -364,23 +384,23 @@
             w0, w1, w2, w3 = stencil(cour * ang[0, pl.ds(j0, 8), :])
             v0, v1, v2, v3 = stencil(cour * ang[1, pl.ds(j0, 8), :])
             cells = [x[k, pl.ds(c + 4 * j0, 8, stride=4), :] for c in range(CELLS)]
-            west = from_west[halo_at(i, kk, near_rows[b], 8), :]
-            east = from_east[halo_at(i, kk, near_rows[b], 8), :]
+            west = from_west(halo_at(i, kk, near_rows[b], 8))
+            east = from_east(halo_at(i, kk, near_rows[b], 8))
             plus = [west, *cells, east]
             minus = plus[::-1]
             if b == 0:
-                far, seq = from_west[halo_at(i, kk, 16, 8), :], plus
+                far, seq = from_west(halo_at(i, kk, 16, 8)), plus
             elif b == 2:
-                far, seq = from_east[halo_at(i, kk, 23, 8), :], minus
+                far, seq = from_east(halo_at(i, kk, 23, 8)), minus
             elif b == 4:
-                far, seq = from_west[halo_at(i, kk, 26, 8), :], plus
+                far, seq = from_west(halo_at(i, kk, 26, 8)), plus
             else:
                 if b == 1:
                     pos = sub < 1
-                    far_p, far_m = from_west[halo_at(i, kk, 24, 8), :], from_east[halo_at(i, kk, 15, 8), :]
+                    far_p, far_m = from_west(halo_at(i, kk, 24, 8)), from_east(halo_at(i, kk, 15, 8))
                 else:
                     pos = sub >= 3
-                    far_p, far_m = from_west[halo_at(i, kk, 22, 8), :], from_east[halo_at(i, kk, 31, 8), :]
+                    far_p, far_m = from_west(halo_at(i, kk, 22, 8)), from_east(halo_at(i, kk, 31, 8))
                 far = jnp.where(pos, far_p, far_m)
                 seq = [jnp.where(pos, p, m) for p, m in zip(plus, minus)]
             seq = [far, *seq]
@@ -527,24 +547,24 @@
     )(SCALARS, ANGLES, x, west, east, ghosts, *tables, *parts, *energies)
 
 
-def ring(axis, wrap):
-    size = lax.axis_size(axis)
-    up = [(i, (i + 1) % size) for i in range(size if wrap else size - 1)]
+def line(axis):
+    up = [(i, i + 1) for i in range(lax.axis_size(axis) - 1)]
     return up, [(j, i) for i, j in up]
 
 
 def local(
     spectrum, sea_mask, refraction, atm_wind, hour_fraction, send_cells, recv_slots, recv_weights
 ):
-    east_way, west_way = ring("lon", True)
-    north_way, south_way = ring("lat", False)
+    north_way, south_way = line("lat")
     x = spectrum.reshape(FREQS, ROWS, LANES)
     tiles = lax.axis_size("lon")
+    swap_one = [(i, i ^ 1) for i in range(tiles)]
+    swap_two = [(i, (i + 1 if i % 2 else i - 1) % tiles) for i in range(tiles)]
     cap = send_cells.shape[1] // tiles
     firsts = [sum(CHUNKS[:n]) for n in range(len(CHUNKS))]
 
-    def exchange(to_east, to_west):
-        return lax.ppermute(to_east, "lon", east_way), lax.ppermute(to_west, "lon", west_way)
+    def exchange(one, two):
+        return lax.ppermute(one, "lon", swap_one), lax.ppermute(two, "lon", swap_two)
 
     *sends, packed = first_halos(
         x, CHUNKS[0], hour_fraction.reshape(1, 1), atm_wind.reshape(4, LANES), send_cells
@@ -556,8 +576,9 @@
     *sends, merged = second_halos(x, firsts[1], CHUNKS[1], south, north)
     halos.append(exchange(*sends))
     halos.append(exchange(*later_halos(x, firsts[2], CHUNKS[2], *halos[0])))
-    west, east = (side[-8:] for side in halos[0])
-    lists = [jnp.concatenate([packed, jnp.where(lax.axis_index("lon") % 2 == 0, east, west)])]
+    ghosts = move_ghosts(CHUNKS[1], merged, *halos[1])
+
+    lists = [jnp.concatenate([packed, halos[0][0][-8:]])]
     step = 2
     while step < tiles:
         held = lists[0] if len(lists) == 1 else jnp.concatenate(lists)
@@ -573,7 +594,6 @@
         refraction,
     )
     halos.append(exchange(*later_halos(x, firsts[3], CHUNKS[3], *halos[1], tables[0])))
-    ghosts = move_ghosts(CHUNKS[1], merged, *halos[1])
 
     parts, energies = [], []
     for n, (first, count) in enumerate(zip(firsts, CHUNKS)):

time: 59.2 us -> 57 us (0.963)
  waiting for transfers between devices: 14.1 us -> 11.5 us
  starting transfers between devices: 28 us -> 29.9 us
  Pallas kernels: 14.5 us -> 13 us
    ppermute x8, starting transfers between devices: 20.4 us -> 24.3 us  [the longest x4 17.3 us: exchange(): lax.ppermute(two, 'lon', swap_two)]
    ppermute x8, waiting for transfers between devices: 4.3 us -> 1.94 us  [the longest x4 1.93 us: exchange(): lax.ppermute(one, 'lon', swap_one)]
    ppermute x2, starting transfers between devices: 2.64 us -> 1.15 us  [local(): lax.ppermute(held, 'lon', [(i, i ^ step) for i in range(tiles)])]
    pallas_call x1, Pallas kernels: 0.96 us -> 0.09 us  [second_halos(): pl.pallas_call(lambda *refs: second_body(start, count, *refs), out_shape=...]
    ppermute x1, starting transfers between devices: 3.69 us -> 3.04 us  [local(): south = lax.ppermute(q, 'lat', north_way)]
    pallas_call x1, Pallas kernels: 1.92 us -> 1.28 us  [pack_edges(): pl.pallas_call(edge_body, out_shape=jax.ShapeDtypeStruct((CELLS, GROUPS +...]
  transfers between devices with their start and end apart: 12 -> 12, of which waited for: 4 -> 4; matrix products, arithmetic and copies ran while one was open for 0% -> 0% of each run, Pallas kernels for 17% -> 16%
where the time goes in v4:
time: 57 us; the launch traced here: 56.8 us
  starting transfers between devices  29.9 us (52%)
  Pallas kernels  13 us (23%)
  waiting for transfers between devices  11.5 us (20%)
  between operations  1.65 us (3%)
  local copies, waits for them, and re-layouts  0.74 us (1%)
    ppermute x4, starting transfers between devices, exchange(): lax.ppermute(two, 'lon', swap_two)  17.3 us
    ppermute x2, waiting for transfers between devices, local(): lax.ppermute(held, 'lon', [(i, i ^ step) for i in range(tiles)])  8.63 us
    ppermute x4, starting transfers between devices, exchange(): lax.ppermute(one, 'lon', swap_one)  6.94 us
    pallas_call x3, Pallas kernels, main_chunk(): pl.pallas_call(lambda *refs: main_body(first, count, *refs), out_shape=(j...  5.37 us
    ppermute x1, starting transfers between devices, local(): south = lax.ppermute(q, 'lat', north_way)  3.04 us
    pallas_call x1, Pallas kernels, tail_chunk(): pl.pallas_call(lambda *refs: tail_body(sizes, *refs), out_shape=jax.Shape...  2.31 us
    ppermute x4, waiting for transfers between devices, exchange(): lax.ppermute(one, 'lon', swap_one)  1.93 us
    pallas_call x1, Pallas kernels, first_halos(): pl.pallas_call(lambda *refs: first_body(count, *refs), out_shape=(message...  1.83 us
  transfers between devices with their start and end apart: 12, of which 4 were waited for; matrix products, arithmetic and copies ran while one was open for 0% of the time, Pallas kernels for 16%

profile of v4, /device:TPU:0, one launch (start us, length us, event | category | flops | bytes accessed | tf_op | source)
XLA Modules:
  0.0 56.8 jit_solution(3093926970553113442)
XLA Ops:
  0.6 0.0 copy-start
  0.6 0.0 copy-start.5
  1.4 1.8 %first_halos.1 = (f32[656,128]{1,0:T(8,128)S(1)}, f32[648,128]{1,0:T(8,128)S(1)}, f32[8,128]{1,0:T(8,128)}) custom-call(f32[36,144,128]{2,1,0:T(8,128)} %bitcast.7, f32[1,1]{1,0:T(1,128)} %bitcast.6.refs_1_, f32[4,128]{1,0:T(4,128)} %bitcast.19, s32[1,192]{1,0:T(1,128)} %refs_3_.3), custom_call_target="tpu_custom_call" | custom-call | bytes 2000000 | tf_op jit(solution)/shard_map/first_halos/pallas_call | solution.py:172
  3.3 3.0 %collective-permute-start.4 = (f32[656,128]{1,0:T(8,128)S(1)}, f32[656,128]{1,0:T(8,128)S(1)}, u32[]{:S(2)}, u32[]{:S(2)}) collective-permute-start(f32[656,128]{1,0:T(8,128)S(1)} %get-tuple-element.25), channel_id=1, source_target_pairs={{0,4},{4,0},{8,12},{12,8},{16,20},{20,16},{24,28},{28,24},{1,5},{5... | collective-permute-start | bytes 1007624 | tf_op jit(solution)/shard_map/ppermute | solution.py:567
  6.3 3.5 %collective-permute-start.9 = (f32[648,128]{1,0:T(8,128)S(1)}, f32[648,128]{1,0:T(8,128)S(1)}, u32[]{:S(2)}, u32[]{:S(2)}) collective-permute-start(f32[648,128]{1,0:T(8,128)S(1)} %get-tuple-element.32), channel_id=1, source_target_pairs={{0,28},{4,8},{8,4},{12,16},{16,12},{20,24},{24,20},{28,0},{1,29},{... | collective-permute-start | bytes 995336 | tf_op jit(solution)/shard_map/ppermute | solution.py:567
  9.9 0.0 copy-done
  9.9 0.0 copy-done.5
  9.9 0.0 copy-start.4
  9.9 0.7 %copy-done.4 = f32[8,128]{1,0:T(8,128)S(1)} copy-done((f32[8,128]{1,0:T(8,128)S(1)}, f32[8,128]{1,0:T(8,128)}, u32[]{:S(2)}) %copy-start.4) | copy-done | bytes 4120
  10.6 1.3 %pack_edges.1 = f32[4,7,8,128]{3,2,1,0:T(8,128)S(1)} custom-call(f32[36,144,128]{2,1,0:T(8,128)S(1)} %bitcast.8, s32[4,128]{1,0:T(4,128)S(1)} %copy-done.5, f32[8,128]{1,0:T(8,128)S(1)} %copy-done.4), custom_call_target="tpu_custom_call" | custom-call | bytes 4000000 | tf_op jit(solution)/shard_map/pack_edges/pallas_call | solution.py:215
  11.8 0.0 copy-start.1
  11.9 0.0 copy-start.6
  11.9 0.0 copy-start.7
  11.9 0.0 copy-start.8
  11.9 1.4 %collective-permute-start.1 = (f32[4,7,8,128]{3,2,1,0:T(8,128)S(1)}, f32[4,7,8,128]{3,2,1,0:T(8,128)S(1)}, u32[]{:S(2)}, u32[]{:S(2)}) collective-permute-start(f32[4,7,8,128]{3,2,1,0:T(8,128)S(1)} %pack_edges.1), channel_id=1, source_target_pairs={{1,0},{2,1},{3,2},{5,4},{6,5},{7,6},{9,8},{10,9},{11,10},{13,12},{... | collective-permute-start | bytes 344072 | tf_op jit(solution)/shard_map/ppermute | solution.py:575
  13.3 3.0 %collective-permute-start = (f32[4,7,8,128]{3,2,1,0:T(8,128)S(1)}, f32[4,7,8,128]{3,2,1,0:T(8,128)S(1)}, u32[]{:S(2)}, u32[]{:S(2)}) collective-permute-start(f32[4,7,8,128]{3,2,1,0:T(8,128)S(1)} %pack_edges.1), channel_id=1, source_target_pairs={{0,1},{1,2},{2,3},{4,5},{5,6},{6,7},{8,9},{9,10},{10,11},{12,13},{... | collective-permute-start | bytes 344072 | tf_op jit(solution)/shard_map/ppermute | solution.py:574
  16.4 0.0 collective-permute-done.1.refs_2_
  16.4 0.9 %collective-permute-done.refs_1_ = f32[4,7,8,128]{3,2,1,0:T(8,128)S(1)} collective-permute-done((f32[4,7,8,128]{3,2,1,0:T(8,128)S(1)}, f32[4,7,8,128]{3,2,1,0:T(8,128)S(1)}, u32[]{:S(2)}, u32[]{:S(2)}) %collective-permute-start) | collective-permute-done | bytes 114720 | tf_op jit(solution)/shard_map/ppermute | solution.py:574
  17.3 0.1 second_halos.1
  17.4 0.1 collective-permute-start.2
  17.5 0.0 copy-start.3
  17.5 1.9 %collective-permute-start.3 = (f32[528,128]{1,0:T(8,128)S(1)}, f32[528,128]{1,0:T(8,128)S(1)}, u32[]{:S(2)}, u32[]{:S(2)}) collective-permute-start(f32[528,128]{1,0:T(8,128)S(1)} %get-tuple-element.24), channel_id=1, source_target_pairs={{0,28},{4,8},{8,4},{12,16},{16,12},{20,24},{24,20},{28,0},{1,29},{... | collective-permute-start | bytes 811016 | tf_op jit(solution)/shard_map/ppermute | solution.py:567
  19.4 0.0 collective-permute-done.9.refs_4_.refs_1_
  19.4 1.9 %collective-permute-done.4.refs_3_.refs_0_ = f32[656,128]{1,0:T(8,128)S(1)} collective-permute-done((f32[656,128]{1,0:T(8,128)S(1)}, f32[656,128]{1,0:T(8,128)S(1)}, u32[]{:S(2)}, u32[]{:S(2)}) %collective-permute-start.4) | collective-permute-done | bytes 335904 | tf_op jit(solution)/shard_map/ppermute | solution.py:567
  21.3 0.1 later_halos.3
  21.4 2.5 %collective-permute-start.10 = (f32[648,128]{1,0:T(8,128)S(1)}, f32[648,128]{1,0:T(8,128)S(1)}, u32[]{:S(2)}, u32[]{:S(2)}) collective-permute-start(f32[648,128]{1,0:T(8,128)S(1)} %get-tuple-element.35), channel_id=1, source_target_pairs={{0,4},{4,0},{8,12},{12,8},{16,20},{20,16},{24,28},{28,24},{1,5},{5... | collective-permute-start | bytes 995336 | tf_op jit(solution)/shard_map/ppermute | solution.py:567
  23.9 9.8 %collective-permute-start.11 = (f32[648,128]{1,0:T(8,128)S(1)}, f32[648,128]{1,0:T(8,128)S(1)}, u32[]{:S(2)}, u32[]{:S(2)}) collective-permute-start(f32[648,128]{1,0:T(8,128)S(1)} %get-tuple-element.36), channel_id=1, source_target_pairs={{0,28},{4,8},{8,4},{12,16},{16,12},{20,24},{24,20},{28,0},{1,29},{... | collective-permute-start | bytes 995336 | tf_op jit(solution)/shard_map/ppermute | solution.py:567
  33.7 0.0 collective-permute-start.5
  33.7 5.1 %collective-permute-done.5.refs_6_ = f32[16,128]{1,0:T(8,128)S(1)} collective-permute-done((f32[16,128]{1,0:T(8,128)S(1)}, f32[16,128]{1,0:T(8,128)S(1)}, u32[]{:S(2)}, u32[]{:S(2)}) %collective-permute-start.5) | collective-permute-done | bytes 8224 | tf_op jit(solution)/shard_map/ppermute | solution.py:585
  38.8 1.2 %collective-permute-start.6 = (f32[32,128]{1,0:T(8,128)S(1)}, f32[32,128]{1,0:T(8,128)S(1)}, u32[]{:S(2)}, u32[]{:S(2)}) collective-permute-start(f32[32,128]{1,0:T(8,128)S(1)} %pad_maximum_fusion), channel_id=1, source_target_pairs={{0,16},{4,20},{8,24},{12,28},{16,0},{20,4},{24,8},{28,12},{1,17},{... | collective-permute-start | bytes 49160 | tf_op jit(solution)/shard_map/ppermute | solution.py:585
  40.0 3.5 %collective-permute-done.6.refs_7_ = f32[32,128]{1,0:T(8,128)S(1)} collective-permute-done((f32[32,128]{1,0:T(8,128)S(1)}, f32[32,128]{1,0:T(8,128)S(1)}, u32[]{:S(2)}, u32[]{:S(2)}) %collective-permute-start.6) | collective-permute-done | bytes 16416 | tf_op jit(solution)/shard_map/ppermute | solution.py:585
  43.5 0.0 copy-done.1
  43.5 0.0 copy-done.6
  43.5 0.0 copy-done.7
  43.5 0.0 copy-done.8
  43.5 0.8 %surface_wind.1 = (f32[2,4,128]{2,1,0:T(4,128)}, f32[4,8,128]{2,1,0:T(8,128)S(1)}, f32[4,36,128]{2,1,0:T(8,128)S(1)}, f32[4,36,128]{2,1,0:T(8,128)S(1)}) custom-call(s32[16,128]{1,0:T(8,128)S(1)} %bitcast.16, f32[16,128]{1,0:T(8,128)S(1)} %bitcast.17, f32[6,36,128]{2,1,0:T(8,128)S(1)} %copy-done.1, s32[4,128]{1,0:T(4,128)S(1)} %copy-done.5, ...), custom_call_target="tpu_custom_call" | custom-call | bytes 2000000 | tf_op jit(solution)/shard_map/surface_wind/pallas_call | solution.py:349
  44.3 0.0 collective-permute-done.2.refs_0_.refs_1_.refs_3_
  44.3 0.0 collective-permute-done.3.refs_1_.refs_2_.refs_4_
  44.3 0.0 copy-start.2
  44.4 1.3 %collective-permute-start.7 = (f32[216,128]{1,0:T(8,128)S(1)}, f32[216,128]{1,0:T(8,128)S(1)}, u32[]{:S(2)}, u32[]{:S(2)}) collective-permute-start(f32[216,128]{1,0:T(8,128)S(1)} %get-tuple-element.27), channel_id=1, source_target_pairs={{0,4},{4,0},{8,12},{12,8},{16,20},{20,16},{24,28},{28,24},{1,5},{5... | collective-permute-start | bytes 331784 | tf_op jit(solution)/shard_map/ppermute | solution.py:567
  45.7 2.1 %collective-permute-start.8 = (f32[216,128]{1,0:T(8,128)S(1)}, f32[216,128]{1,0:T(8,128)S(1)}, u32[]{:S(2)}, u32[]{:S(2)}) collective-permute-start(f32[216,128]{1,0:T(8,128)S(1)} %get-tuple-element.28), channel_id=1, source_target_pairs={{0,28},{4,8},{8,4},{12,16},{16,12},{20,24},{24,20},{28,0},{1,29},{... | collective-permute-start | bytes 331784 | tf_op jit(solution)/shard_map/ppermute | solution.py:567
  47.8 0.0 copy-done.3
  47.8 1.2 %move_ghosts.1.refs_5_ = f32[36,4,5,8,128]{4,3,2,1,0:T(8,128)S(1)} custom-call(f32[4,7,8,128]{3,2,1,0:T(8,128)S(1)} %get-tuple-element.29.refs_0_, f32[528,128]{1,0:T(8,128)S(1)} %collective-permute-done.2.refs_0_.refs_1_.refs_3_, f32[528,128]{1,0:T(8,128)S(1)} %collective-permute-done.3.refs_1_.refs_2_.refs_4_, f32[5,6,8,128]{3,2,1,0:T(8,128)S(1)} %copy-done.3), custom_call_target="tpu_custom_call" | custom-call | bytes 2000000 | tf_op jit(solution)/shard_map/move_ghosts/pallas_call | solution.py:299
  49.0 0.0 copy-done.2
  49.0 1.3 %chunk.4 = (f32[8,144,128]{2,1,0:T(8,128)S(1)}, f32[4,8,128]{2,1,0:T(8,128)S(1)}) custom-call(f32[5,36,128]{2,1,0:T(8,128)S(1)} %copy-done.2, f32[6,36,128]{2,1,0:T(8,128)S(1)} %copy-done.1, f32[36,144,128]{2,1,0:T(8,128)S(1)} %bitcast.12, f32[528,128]{1,0:T(8,128)S(1)} %collective-permute-done.2.refs_0_.refs_1_.refs_3_, ...), custom_call_target="tpu_custom_call" | custom-call | bytes 1000000 | tf_op jit(solution)/shard_map/chunk/pallas_call | solution.py:476
  50.4 2.0 %chunk.3 = (f32[12,144,128]{2,1,0:T(8,128)S(1)}, f32[4,8,128]{2,1,0:T(8,128)S(1)}) custom-call(f32[5,36,128]{2,1,0:T(8,128)S(1)} %copy-done.2, f32[6,36,128]{2,1,0:T(8,128)S(1)} %copy-done.1, f32[36,144,128]{2,1,0:T(8,128)S(1)} %bitcast.13, f32[656,128]{1,0:T(8,128)S(1)} %collective-permute-done.4.refs_3_.refs_0_, ...), custom_call_target="tpu_custom_call" | custom-call | bytes 1000000 | tf_op jit(solution)/shard_map/chunk/pallas_call | solution.py:476
  52.4 0.0 collective-permute-done.10.refs_3_
  52.4 0.0 collective-permute-done.11.refs_4_
  52.4 2.0 %chunk.5 = (f32[12,144,128]{2,1,0:T(8,128)S(1)}, f32[4,8,128]{2,1,0:T(8,128)S(1)}) custom-call(f32[5,36,128]{2,1,0:T(8,128)S(1)} %copy-done.2, f32[6,36,128]{2,1,0:T(8,128)S(1)} %copy-done.1, f32[36,144,128]{2,1,0:T(8,128)S(1)} %bitcast.14, f32[648,128]{1,0:T(8,128)S(1)} %collective-permute-done.10.refs_3_, f32[648,128]{1,0:T(8,128)S(1)} %collective-permute-done.11.refs_4_, ...), custom_call_target="tpu_custom_call" | custom-call | bytes 1000000 | tf_op jit(solution)/shard_map/chunk/pallas_call | solution.py:476
  54.4 0.0 collective-permute-done.7.refs_3_
  54.5 0.0 collective-permute-done.8.refs_4_
  54.5 2.3 %last_chunk.1 = f32[36,144,128]{2,1,0:T(8,128)} custom-call(f32[5,36,128]{2,1,0:T(8,128)S(1)} %copy-done.2, f32[6,36,128]{2,1,0:T(8,128)S(1)} %copy-done.1, f32[36,144,128]{2,1,0:T(8,128)S(1)} %bitcast.15, f32[216,128]{1,0:T(8,128)S(1)} %collective-permute-done.7.refs_3_, f32[216,128]{1,0:T(8,128)S(1)} %collective-permute-done.8.refs_4_, ...), custom_call_target="tpu_custom_call" | custom-call | bytes 6000000 | tf_op jit(solution)/shard_map/last_chunk/pallas_call | solution.py:534
  (4 shorter events, 0.0 us)
Async XLA Ops:
  0.6 9.2 %copy-start = (f32[36,36,4,128]{3,2,1,0:T(4,128)S(1)}, f32[36,36,4,128]{3,2,1,0:T(4,128)}, u32[]{:S(2)}) copy-start(f32[36,36,4,128]{3,2,1,0:T(4,128)} %param.11) | copy-start | bytes 7962628
  0.6 9.2 %copy-start.5 = (s32[4,128]{1,0:T(4,128)S(1)}, s32[4,128]{1,0:T(4,128)}, u32[]{:S(2)}) copy-start(s32[4,128]{1,0:T(4,128)} %refs_3_.4) | copy-start | bytes 6148
  3.3 18.0 %collective-permute-start.4 = (f32[656,128]{1,0:T(8,128)S(1)}, f32[656,128]{1,0:T(8,128)S(1)}, u32[]{:S(2)}, u32[]{:S(2)}) collective-permute-start(f32[656,128]{1,0:T(8,128)S(1)} %get-tuple-element.25), channel_id=1, source_target_pairs={{0,4},{4,0},{8,12},{12,8},{16,20},{20,16},{24,28},{28,24},{1,5},{5... | collective-permute-start | bytes 1007624 | tf_op jit(solution)/shard_map/ppermute | solution.py:567
  6.3 13.1 %collective-permute-start.9 = (f32[648,128]{1,0:T(8,128)S(1)}, f32[648,128]{1,0:T(8,128)S(1)}, u32[]{:S(2)}, u32[]{:S(2)}) collective-permute-start(f32[648,128]{1,0:T(8,128)S(1)} %get-tuple-element.32), channel_id=1, source_target_pairs={{0,28},{4,8},{8,4},{12,16},{16,12},{20,24},{24,20},{28,0},{1,29},{... | collective-permute-start | bytes 995336 | tf_op jit(solution)/shard_map/ppermute | solution.py:567
  9.9 0.7 %copy-start.4 = (f32[8,128]{1,0:T(8,128)S(1)}, f32[8,128]{1,0:T(8,128)}, u32[]{:S(2)}) copy-start(f32[8,128]{1,0:T(8,128)} %get-tuple-element.22.after) | copy-start | bytes 12292
  11.8 31.6 %copy-start.1 = (f32[6,36,128]{2,1,0:T(8,128)S(1)}, f32[6,36,128]{2,1,0:T(8,128)}, u32[]{:S(2)}) copy-start(f32[6,36,128]{2,1,0:T(8,128)} %constant.7.clone.refs_2_.refs_1_) | copy-start | bytes 331780
  11.9 31.6 %copy-start.6 = (s32[4,4,128]{2,1,0:T(4,128)S(1)}, s32[4,4,128]{2,1,0:T(4,128)}, u32[]{:S(2)}) copy-start(s32[4,4,128]{2,1,0:T(4,128)} %param.17) | copy-start | bytes 24580
  11.9 31.6 %copy-start.7 = (f32[4,4,128]{2,1,0:T(4,128)S(1)}, f32[4,4,128]{2,1,0:T(4,128)}, u32[]{:S(2)}) copy-start(f32[4,4,128]{2,1,0:T(4,128)} %param.18) | copy-start | bytes 24580
  11.9 31.6 %copy-start.8 = (f32[2,4,128]{2,1,0:T(4,128)S(1)}, f32[2,4,128]{2,1,0:T(4,128)}, u32[]{:S(2)}) copy-start(f32[2,4,128]{2,1,0:T(4,128)} %refs_4_.1) | copy-start | bytes 12292
  11.9 4.5 %collective-permute-start.1 = (f32[4,7,8,128]{3,2,1,0:T(8,128)S(1)}, f32[4,7,8,128]{3,2,1,0:T(8,128)S(1)}, u32[]{:S(2)}, u32[]{:S(2)}) collective-permute-start(f32[4,7,8,128]{3,2,1,0:T(8,128)S(1)} %pack_edges.1), channel_id=1, source_target_pairs={{1,0},{2,1},{3,2},{5,4},{6,5},{7,6},{9,8},{10,9},{11,10},{13,12},{... | collective-permute-start | bytes 344072 | tf_op jit(solution)/shard_map/ppermute | solution.py:575
  13.3 4.0 %collective-permute-start = (f32[4,7,8,128]{3,2,1,0:T(8,128)S(1)}, f32[4,7,8,128]{3,2,1,0:T(8,128)S(1)}, u32[]{:S(2)}, u32[]{:S(2)}) collective-permute-start(f32[4,7,8,128]{3,2,1,0:T(8,128)S(1)} %pack_edges.1), channel_id=1, source_target_pairs={{0,1},{1,2},{2,3},{4,5},{5,6},{6,7},{8,9},{9,10},{10,11},{12,13},{... | collective-permute-start | bytes 344072 | tf_op jit(solution)/shard_map/ppermute | solution.py:574
  17.4 26.9 %collective-permute-start.2 = (f32[528,128]{1,0:T(8,128)S(1)}, f32[528,128]{1,0:T(8,128)S(1)}, u32[]{:S(2)}, u32[]{:S(2)}) collective-permute-start(f32[528,128]{1,0:T(8,128)S(1)} %get-tuple-element.23), channel_id=1, source_target_pairs={{0,4},{4,0},{8,12},{12,8},{16,20},{20,16},{24,28},{28,24},{1,5},{5... | collective-permute-start | bytes 811016 | tf_op jit(solution)/shard_map/ppermute | solution.py:567
  17.5 30.3 %copy-start.3 = (f32[5,6,8,128]{3,2,1,0:T(8,128)S(1)}, f32[5,6,8,128]{3,2,1,0:T(8,128)}, u32[]{:S(2)}) copy-start(f32[5,6,8,128]{3,2,1,0:T(8,128)} %constant.6.clone.refs_3_) | copy-start | bytes 368644
  17.5 26.8 %collective-permute-start.3 = (f32[528,128]{1,0:T(8,128)S(1)}, f32[528,128]{1,0:T(8,128)S(1)}, u32[]{:S(2)}, u32[]{:S(2)}) collective-permute-start(f32[528,128]{1,0:T(8,128)S(1)} %get-tuple-element.24), channel_id=1, source_target_pairs={{0,28},{4,8},{8,4},{12,16},{16,12},{20,24},{24,20},{28,0},{1,29},{... | collective-permute-start | bytes 811016 | tf_op jit(solution)/shard_map/ppermute | solution.py:567
  21.4 31.0 %collective-permute-start.10 = (f32[648,128]{1,0:T(8,128)S(1)}, f32[648,128]{1,0:T(8,128)S(1)}, u32[]{:S(2)}, u32[]{:S(2)}) collective-permute-start(f32[648,128]{1,0:T(8,128)S(1)} %get-tuple-element.35), channel_id=1, source_target_pairs={{0,4},{4,0},{8,12},{12,8},{16,20},{20,16},{24,28},{28,24},{1,5},{5... | collective-permute-start | bytes 995336 | tf_op jit(solution)/shard_map/ppermute | solution.py:567
  23.9 28.5 %collective-permute-start.11 = (f32[648,128]{1,0:T(8,128)S(1)}, f32[648,128]{1,0:T(8,128)S(1)}, u32[]{:S(2)}, u32[]{:S(2)}) collective-permute-start(f32[648,128]{1,0:T(8,128)S(1)} %get-tuple-element.36), channel_id=1, source_target_pairs={{0,28},{4,8},{8,4},{12,16},{16,12},{20,24},{24,20},{28,0},{1,29},{... | collective-permute-start | bytes 995336 | tf_op jit(solution)/shard_map/ppermute | solution.py:567
  33.7 5.1 %collective-permute-start.5 = (f32[16,128]{1,0:T(8,128)S(1)}, f32[16,128]{1,0:T(8,128)S(1)}, u32[]{:S(2)}, u32[]{:S(2)}) collective-permute-start(f32[16,128]{1,0:T(8,128)S(1)} %pad_maximum_fusion.1.refs_5_), channel_id=1, source_target_pairs={{0,8},{4,12},{8,0},{12,4},{16,24},{20,28},{24,16},{28,20},{1,9},{5... | collective-permute-start | bytes 24584 | tf_op jit(solution)/shard_map/ppermute | solution.py:585
  38.8 4.6 %collective-permute-start.6 = (f32[32,128]{1,0:T(8,128)S(1)}, f32[32,128]{1,0:T(8,128)S(1)}, u32[]{:S(2)}, u32[]{:S(2)}) collective-permute-start(f32[32,128]{1,0:T(8,128)S(1)} %pad_maximum_fusion), channel_id=1, source_target_pairs={{0,16},{4,20},{8,24},{12,28},{16,0},{20,4},{24,8},{28,12},{1,17},{... | collective-permute-start | bytes 49160 | tf_op jit(solution)/shard_map/ppermute | solution.py:585
  44.3 4.7 %copy-start.2 = (f32[5,36,128]{2,1,0:T(8,128)S(1)}, f32[5,36,128]{2,1,0:T(8,128)}, u32[]{:S(2)}) copy-start(f32[5,36,128]{2,1,0:T(8,128)} %constant.8.clone.refs_0_) | copy-start | bytes 276484
  44.4 10.1 %collective-permute-start.7 = (f32[216,128]{1,0:T(8,128)S(1)}, f32[216,128]{1,0:T(8,128)S(1)}, u32[]{:S(2)}, u32[]{:S(2)}) collective-permute-start(f32[216,128]{1,0:T(8,128)S(1)} %get-tuple-element.27), channel_id=1, source_target_pairs={{0,4},{4,0},{8,12},{12,8},{16,20},{20,16},{24,28},{28,24},{1,5},{5... | collective-permute-start | bytes 331784 | tf_op jit(solution)/shard_map/ppermute | solution.py:567
  45.7 8.8 %collective-permute-start.8 = (f32[216,128]{1,0:T(8,128)S(1)}, f32[216,128]{1,0:T(8,128)S(1)}, u32[]{:S(2)}, u32[]{:S(2)}) collective-permute-start(f32[216,128]{1,0:T(8,128)S(1)} %get-tuple-element.28), channel_id=1, source_target_pairs={{0,28},{4,8},{8,4},{12,16},{16,12},{20,24},{24,20},{28,0},{1,29},{... | collective-permute-start | bytes 331784 | tf_op jit(solution)/shard_map/ppermute | solution.py:567

commit v5 on v4

--- a/solution.py
+++ b/solution.py
@@ -40,13 +40,15 @@
 theta = (np.arange(DIRS) + 0.5) * spacing
 phi = (np.arange(DIRS) + 1.0) * spacing
 ratio = base_freq / freqs
+log2_e = 1.0 / math.log(2.0)
+rate = input_rate * freqs / freqs[-1] * log2_e
 SCALARS = np.stack(
     [
         courant_max * ratio,
         np.sqrt(ratio),
-        input_rate * freqs / freqs[-1],
-        2.0 * math.pi * freqs / gravity,
-        freqs / freqs[-1],
+        rate * 2.0 * math.pi * freqs / gravity,
+        rate,
+        damping_rate * freqs / freqs[-1] * log2_e,
     ]
 ).astype(np.float32)
 SCALARS = np.ascontiguousarray(np.broadcast_to(SCALARS[:, :, None], (5, FREQS, LANES)))
@@ -134,28 +136,23 @@
     return lax.broadcasted_iota(jnp.int32, (8, LANES), 1)
 
 
-def first_body(
-    count, x_hbm, hour_hbm, wind_hbm, cells_hbm, one, two, packed, x, hour, wind, cells, sem, small
-):
+def first_body(count, x_hbm, wind_hbm, cells_hbm, one, two, packed, x, wind, cells, sem, small):
+    few = [
+        pltpu.make_async_copy(wind_hbm, wind, small.at[0]),
+        pltpu.make_async_copy(cells_hbm, cells, small.at[1]),
+    ]
+    for copy in few:
+        copy.start()
     copies = []
     for n in range(count // GROUP):
         span = pl.ds(n * GROUP, GROUP)
         copies.append(pltpu.make_async_copy(x_hbm.at[span], x.at[span], sem.at[n]))
         copies[-1].start()
-    few = [
-        pltpu.make_async_copy(wind_hbm, wind, small.at[0]),
-        pltpu.make_async_copy(cells_hbm, cells, small.at[1]),
-        pltpu.make_async_copy(hour_hbm, hour, small.at[2]),
-    ]
-    for copy in few:
-        copy.start()
     for copy in few:
         copy.wait()
-    late = hour[...]
-    now = (1.0 - late) * wind[pl.ds(0, 2), :] + late * wind[pl.ds(2, 2), :]
     width = cells.shape[1]
     index = jnp.concatenate([cells[:, :LANES], cells[:, width - LANES :]] * 4, axis=0)
-    table = jnp.concatenate([now[:1]] * 2 + [now[1:]] * 2 + [now[:1]] * 4, axis=0)
+    table = jnp.concatenate([wind[pl.ds(n // 2, 1), :] for n in range(8)], axis=0)
     listed = jnp.take_along_axis(table, index, axis=1)
     packed[...] = listed
     one[pl.ds(count * HALO, 8), :] = listed
@@ -168,24 +165,23 @@
     return pltpu.VMEM((count * HALO + extra, LANES), F32)
 
 
-def first_halos(x, count, hour, wind, cells):
+def first_halos(x, count, wind, cells):
     return pl.pallas_call(
         lambda *refs: first_body(count, *refs),
-        out_shape=(message(count, 8), message(count), jax.ShapeDtypeStruct((8, LANES), F32)),
-        in_specs=[any_spec()] * 4,
+        out_shape=(message(count, 8), message(count), pltpu.VMEM((8, LANES), F32)),
+        in_specs=[any_spec()] * 3,
         out_specs=(vmem_spec(),) * 3,
         scratch_shapes=[
             pltpu.VMEM((count, *x.shape[1:]), F32),
-            pltpu.VMEM(hour.shape, F32),
             pltpu.VMEM(wind.shape, F32),
             pltpu.VMEM(cells.shape, cells.dtype),
             pltpu.SemaphoreType.DMA((count // GROUP,)),
-            pltpu.SemaphoreType.DMA((3,)),
+            pltpu.SemaphoreType.DMA((2,)),
         ],
         compiler_params=pltpu.CompilerParams(vmem_limit_bytes=FIRST_VMEM),
         cost_estimate=pl.CostEstimate(flops=0, bytes_accessed=2000000, transcendentals=0),
         name="first_halos",
-    )(x, hour, wind, cells)
+    )(x, wind, cells)
 
 
 def edge_body(x, sea, after, q):
@@ -214,7 +210,7 @@
 def pack_edges(x, sea, after):
     return pl.pallas_call(
         edge_body,
-        out_shape=jax.ShapeDtypeStruct((CELLS, GROUPS + 1, 8, LANES), F32),
+        out_shape=pltpu.VMEM((CELLS, GROUPS + 1, 8, LANES), F32),
         in_specs=[vmem_spec()] * 3,
         out_specs=vmem_spec(),
         compiler_params=pltpu.CompilerParams(vmem_limit_bytes=VMEM),
@@ -249,7 +245,7 @@
         out_shape=(
             message(count, EDGE_ROWS),
             message(count, EDGE_ROWS),
-            jax.ShapeDtypeStruct((CELLS, GROUPS + 1, 8, LANES), F32),
+            pltpu.VMEM((CELLS, GROUPS + 1, 8, LANES), F32),
         ),
         in_specs=[vmem_spec()] * 3,
         out_specs=(vmem_spec(),) * 3,
@@ -298,7 +294,7 @@
 def move_ghosts(count, merged, one, two):
     return pl.pallas_call(
         lambda *refs: ghost_body(count, *refs),
-        out_shape=jax.ShapeDtypeStruct((FREQS, CELLS, len(BLOCKS), 8, LANES), F32),
+        out_shape=pltpu.VMEM((FREQS, CELLS, len(BLOCKS), 8, LANES), F32),
         in_specs=[vmem_spec()] * 4,
         out_specs=vmem_spec(),
         compiler_params=pltpu.CompilerParams(vmem_limit_bytes=VMEM),
@@ -307,13 +303,14 @@
     )(merged, one, two, PACKED)
 
 
-def wind_body(cap, sources, slots, weights, ang, sea, refr, *rest):
+def wind_body(cap, sources, hour, slots, weights, ang, sea, refr, *rest):
     picked = [[jnp.zeros((8, LANES), F32) for _ in range(2)] for _ in range(2)]
     pieces, (wind, sea8, turn, proj, table) = rest[:-5], rest[-5:]
     at = 0
     for piece in pieces:
         table[pl.ds(at, piece.shape[0]), :] = piece[...]
         at += piece.shape[0]
+    late = hour[...]
     width = cap * sources
     me = lax.axis_index("lon")
     mine = cap * me
@@ -326,9 +323,12 @@
             low = place < LANES
             place = jnp.where(low, place, place - (width - LANES))
             for c in range(2):
+                at = 8 * (s ^ me) + 2 * c
                 row = [
-                    jnp.broadcast_to(table[pl.ds(8 * (s ^ me) + 2 * c + n, 1), :], (8, LANES)) for n in range(2)
+                    (1.0 - late) * table[pl.ds(at + n, 1), :] + late * table[pl.ds(at + 4 + n, 1), :]
+                    for n in range(2)
                 ]
+                row = [jnp.broadcast_to(r, (8, LANES)) for r in row]
                 value = [jnp.take_along_axis(r, place, axis=1) for r in row]
                 value = jnp.where(low, value[0], value[1])
                 picked[half][c] = jnp.where(here, value, picked[half][c])
@@ -345,26 +345,50 @@
             proj[cell, j, :] = wind[0, row, :] * ang[2, j, :] + wind[1, row, :] * ang[3, j, :]
 
 
-def surface(cap, sources, pieces, slots, weights, sea, refr):
+def surface(cap, sources, hour, pieces, slots, weights, sea, refr):
     return pl.pallas_call(
         lambda *refs: wind_body(cap, sources, *refs),
         out_shape=(
             jax.ShapeDtypeStruct((2, CELLS, LANES), F32),
-            jax.ShapeDtypeStruct((CELLS, 8, LANES), F32),
-            jax.ShapeDtypeStruct((CELLS, DIRS, LANES), F32),
-            jax.ShapeDtypeStruct((CELLS, DIRS, LANES), F32),
+            pltpu.VMEM((CELLS, 8, LANES), F32),
+            pltpu.VMEM((CELLS, DIRS, LANES), F32),
+            pltpu.VMEM((CELLS, DIRS, LANES), F32),
         ),
-        in_specs=[vmem_spec()] * (5 + len(pieces)),
+        in_specs=[vmem_spec()] * (6 + len(pieces)),
         out_specs=(vmem_spec(),) * 4,
         scratch_shapes=[pltpu.VMEM((8 * sources, LANES), F32)],
         compiler_params=pltpu.CompilerParams(vmem_limit_bytes=VMEM),
         cost_estimate=pl.CostEstimate(flops=0, bytes_accessed=2000000, transcendentals=0),
         name="surface_wind",
-    )(slots, weights, ANGLES, sea, refr, *pieces)
+    )(hour, slots, weights, ANGLES, sea, refr, *pieces)
+
+
+def weight_body(scal, ang, after, table):
+    def body(k, _):
+        cour = scal[0, pl.ds(k, 1), :]
+        for b, j0 in enumerate(BLOCKS):
+            both = stencil(cour * ang[0, pl.ds(j0, 8), :]) + stencil(cour * ang[1, pl.ds(j0, 8), :])
+            for n, weight in enumerate(both):
+                table[k, b, n] = weight
+        return 0
+
+    lax.fori_loop(0, FREQS, body, 0)
+
+
+def stencil_weights(after):
+    return pl.pallas_call(
+        weight_body,
+        out_shape=pltpu.VMEM((FREQS, len(BLOCKS), 8, 8, LANES), F32),
+        in_specs=[vmem_spec()] * 3,
+        out_specs=vmem_spec(),
+        compiler_params=pltpu.CompilerParams(vmem_limit_bytes=VMEM),
+        cost_estimate=pl.CostEstimate(flops=0, bytes_accessed=2000000, transcendentals=0),
+        name="stencil_weights",
+    )(SCALARS, ANGLES, after)
 
 
 def chunk_pass(
-    first, count, scal, ang, x, one_ref, two_ref, ghosts, sea8, turn, proj, zs, gs, out, out_first
+    first, count, scal, weights, x, one_ref, two_ref, ghosts, sea8, turn, proj, zs, gs, out, out_first
 ):
     lane = lane_ids()
     sub = lax.broadcasted_iota(jnp.int32, (8, LANES), 0)
@@ -379,10 +403,9 @@
 
     def one(i, kk, sums):
         k = first + i * GROUP + kk
-        cour, bend, rate, slow = (scal[n, pl.ds(k, 1), :] for n in range(4))
+        bend, gain, floor = (scal[n, pl.ds(k, 1), :] for n in range(1, 4))
         for b, j0 in enumerate(BLOCKS):
-            w0, w1, w2, w3 = stencil(cour * ang[0, pl.ds(j0, 8), :])
-            v0, v1, v2, v3 = stencil(cour * ang[1, pl.ds(j0, 8), :])
+            w0, w1, w2, w3, v0, v1, v2, v3 = (weights[k, b, n] for n in range(8))
             cells = [x[k, pl.ds(c + 4 * j0, 8, stride=4), :] for c in range(CELLS)]
             west = from_west(halo_at(i, kk, near_rows[b], 8))
             east = from_east(halo_at(i, kk, near_rows[b], 8))
@@ -428,7 +451,7 @@
                     p = sub < 2
                     up, down = jnp.where(p, s1, n1), jnp.where(p, n1, s1)
                     far = jnp.where(p, s2, n2)
-                z = (v0 * far + v1 * up + v2 * z + v3 * down) * sea8[c]
+                z = v0 * far + v1 * up + v2 * z + v3 * down
                 zs[kk, c, pl.ds(8 + j0, 8), :] = z
         out_sums = []
         for c in range(CELLS):
@@ -437,7 +460,7 @@
                 own = zs[kk, c, pl.ds(8 + j0, 8), :]
                 nxt = zs[kk, c, pl.ds(9 + j0, 8), :]
                 s = bend * turn[c, pl.ds(j0, 8), :]
-                gs[kk, c, pl.ds(8 + j0, 8), :] = jnp.maximum(s, 0.0) * own + jnp.minimum(s, 0.0) * nxt
+                gs[kk, c, pl.ds(8 + j0, 8), :] = s * jnp.where(s > 0, own, nxt)
             gs[kk, c, pl.ds(7, 1), :] = gs[kk, c, pl.ds(7 + DIRS, 1), :]
             total = sums[c]
             for b, j0 in enumerate(BLOCKS):
@@ -446,8 +469,8 @@
                 prev = gs[kk, c, pl.ds(7 + j0, 8), :]
                 refracted = own - (flux - prev)
                 total = total + (jnp.where(sub >= 4, refracted, 0.0) if b == 4 else refracted)
-                growth = rate * jnp.maximum(proj[c, pl.ds(j0, 8), :] * slow - 1.0, 0.0)
-                out[out_first + i * GROUP + kk, pl.ds(c + 4 * j0, 8, stride=4), :] = refracted * jnp.exp(growth)
+                growth = jnp.maximum(proj[c, pl.ds(j0, 8), :] * gain - floor, 0.0)
+                out[out_first + i * GROUP + kk, pl.ds(c + 4 * j0, 8, stride=4), :] = refracted * jnp.exp2(growth)
             out_sums.append(total)
         return tuple(out_sums)
 
@@ -461,9 +484,9 @@
 
 
 def main_body(
-    first, count, scal, ang, x, west, east, ghosts, sea8, turn, proj, out, energy, zs, gs
+    first, count, scal, weights, x, west, east, ghosts, sea8, turn, proj, out, energy, zs, gs
 ):
-    sums = chunk_pass(first, count, scal, ang, x, west, east, ghosts, sea8, turn, proj, zs, gs, out, 0)
+    sums = chunk_pass(first, count, scal, weights, x, west, east, ghosts, sea8, turn, proj, zs, gs, out, 0)
     for c in range(CELLS):
         energy[c] = sums[c]
 
@@ -472,12 +495,12 @@
     return [pltpu.VMEM((GROUP, CELLS, 56, LANES), F32), pltpu.VMEM((GROUP, CELLS, 56, LANES), F32)]
 
 
-def main_chunk(first, count, x, west, east, ghosts, tables):
+def main_chunk(first, count, weights, x, west, east, ghosts, tables):
     return pl.pallas_call(
         lambda *refs: main_body(first, count, *refs),
         out_shape=(
-            jax.ShapeDtypeStruct((count, ROWS, LANES), F32),
-            jax.ShapeDtypeStruct((CELLS, 8, LANES), F32),
+            pltpu.VMEM((count, ROWS, LANES), F32),
+            pltpu.VMEM((CELLS, 8, LANES), F32),
         ),
         in_specs=[vmem_spec()] * 9,
         out_specs=(vmem_spec(), vmem_spec()),
@@ -485,34 +508,35 @@
         compiler_params=pltpu.CompilerParams(vmem_limit_bytes=VMEM),
         cost_estimate=pl.CostEstimate(flops=0, bytes_accessed=1000000, transcendentals=0),
         name="chunk",
-    )(SCALARS, ANGLES, x, west, east, ghosts, *tables)
-
-
-def tail_body(sizes, scal, ang, x, west, east, ghosts, sea8, turn, proj, *rest):
+    )(SCALARS, weights, x, west, east, ghosts, *tables)
+
+
+def tail_body(sizes, scal, weights, x, west, east, ghosts, sea8, turn, proj, *rest):
     done = len(sizes) - 1
     parts, energies = rest[:done], rest[done : 2 * done]
     out_hbm, obuf, zs, gs, out_sem = rest[2 * done :]
     count = sizes[-1]
     first = FREQS - count
     sums = chunk_pass(
-        first, count, scal, ang, x, west, east, ghosts, sea8, turn, proj, zs, gs, obuf, first
+        first, count, scal, weights, x, west, east, ghosts, sea8, turn, proj, zs, gs, obuf, first
     )
     sub = lax.broadcasted_iota(jnp.int32, (8, LANES), 0)
-    pattern = jnp.zeros((8, LANES), F32)
+    pattern = mask = jnp.zeros((8, LANES), F32)
     for c in range(CELLS):
         total = sums[c]
         for energy in energies:
             total = total + energy[c]
-        mean = jnp.sum(total, axis=0, keepdims=True) * (1.0 / (FREQS * DIRS))
+        mean = sea8[c] * (jnp.sum(total, axis=0, keepdims=True) * (1.0 / (FREQS * DIRS)))
         level = mean * (1.0 / energy_ref)
-        pattern = jnp.where(sub % CELLS == c, damping_rate * (level * level), pattern)
+        pattern = jnp.where(sub % CELLS == c, level * level, pattern)
+        mask = jnp.where(sub % CELLS == c, sea8[c], mask)
     stores, at = [], 0
     for n, size in enumerate(sizes):
         for low in range(0, size, PIECE):
             high = min(low + PIECE, size)
 
             def body(i, _, at=at, n=n):
-                scale = jnp.exp(-(scal[4, pl.ds(at + i, 1), :] * pattern))
+                scale = jnp.exp2(-(scal[4, pl.ds(at + i, 1), :] * pattern)) * mask
                 source, k = (parts[n], i) if n < done else (obuf, at + i)
                 for r in range(0, ROWS, 8):
                     obuf[at + i, pl.ds(r, 8), :] = source[k, pl.ds(r, 8), :] * scale
@@ -529,7 +553,7 @@
         store.wait()
 
 
-def tail_chunk(sizes, x, west, east, ghosts, tables, parts, energies):
+def tail_chunk(sizes, weights, x, west, east, ghosts, tables, parts, energies):
     done = len(sizes) - 1
     return pl.pallas_call(
         lambda *refs: tail_body(sizes, *refs),
@@ -544,7 +568,7 @@
         compiler_params=pltpu.CompilerParams(vmem_limit_bytes=VMEM),
         cost_estimate=pl.CostEstimate(flops=0, bytes_accessed=6000000, transcendentals=0),
         name="last_chunk",
-    )(SCALARS, ANGLES, x, west, east, ghosts, *tables, *parts, *energies)
+    )(SCALARS, weights, x, west, east, ghosts, *tables, *parts, *energies)
 
 
 def line(axis):
@@ -567,15 +591,16 @@
         return lax.ppermute(one, "lon", swap_one), lax.ppermute(two, "lon", swap_two)
 
     *sends, packed = first_halos(
-        x, CHUNKS[0], hour_fraction.reshape(1, 1), atm_wind.reshape(4, LANES), send_cells
+        x, CHUNKS[0], atm_wind.reshape(4, LANES), send_cells
     )
     halos = [exchange(*sends)]
     q = pack_edges(x, sea_mask, packed)
+    weights = stencil_weights(packed)
     south = lax.ppermute(q, "lat", north_way)
     north = lax.ppermute(q, "lat", south_way)
     *sends, merged = second_halos(x, firsts[1], CHUNKS[1], south, north)
     halos.append(exchange(*sends))
-    halos.append(exchange(*later_halos(x, firsts[2], CHUNKS[2], *halos[0])))
+    halos.append(exchange(*later_halos(x, firsts[2], CHUNKS[2], *halos[0], weights)))
     ghosts = move_ghosts(CHUNKS[1], merged, *halos[1])
 
     lists = [jnp.concatenate([packed, halos[0][0][-8:]])]
@@ -587,6 +612,7 @@
     surface_wind, *tables = surface(
         cap,
         tiles,
+        hour_fraction.reshape(1, 1),
         lists,
         recv_slots.reshape(4 * CELLS, LANES),
         recv_weights.reshape(4 * CELLS, LANES),
@@ -599,11 +625,11 @@
     for n, (first, count) in enumerate(zip(firsts, CHUNKS)):
         west, east = halos[n]
         if n < len(CHUNKS) - 1:
-            part, energy = main_chunk(first, count, x, west, east, ghosts, tables)
+            part, energy = main_chunk(first, count, weights, x, west, east, ghosts, tables)
             parts.append(part)
             energies.append(energy)
         else:
-            out = tail_chunk(CHUNKS, x, west, east, ghosts, tables, parts, energies)
+            out = tail_chunk(CHUNKS, weights, x, west, east, ghosts, tables, parts, energies)
     return (out.reshape(spectrum.shape), surface_wind)
 
 

time: 57 us -> 54.7 us (0.960)
  waiting for transfers between devices: 11.5 us -> 10.2 us
    ppermute x4, starting transfers between devices: 17.3 us -> 11 us  [exchange(): lax.ppermute(two, 'lon', swap_two)]
    ppermute x4, starting transfers between devices: 6.94 us -> 13.1 us  [exchange(): lax.ppermute(one, 'lon', swap_one)]
    ppermute x4, waiting for transfers between devices: 1.93 us -> 1.26 us  [exchange(): lax.ppermute(one, 'lon', swap_one)]
    ppermute x2, waiting for transfers between devices: 8.63 us -> 7.97 us  [local(): lax.ppermute(held, 'lon', [(i, i ^ step) for i in range(tiles)])]
    pallas_call x5 -> x6, Pallas kernels: 7.84 us -> 7.85 us  [the longest x3 4.39 us: main_chunk(): pl.pallas_call(lambda *refs: main_body(first, count, *refs), out_shape=(p...]
where the time goes in v5:
time: 54.7 us; the launch traced here: 54.5 us
  starting transfers between devices  29.6 us (54%)
  Pallas kernels  12.5 us (23%)
  waiting for transfers between devices  10.2 us (19%)
  between operations  1.51 us (3%)
  local copies, waits for them, and re-layouts  0.73 us (1%)
    ppermute x4, starting transfers between devices, exchange(): lax.ppermute(one, 'lon', swap_one)  13.1 us
    ppermute x4, starting transfers between devices, exchange(): lax.ppermute(two, 'lon', swap_two)  11 us
    ppermute x2, waiting for transfers between devices, local(): lax.ppermute(held, 'lon', [(i, i ^ step) for i in range(tiles)])  7.97 us
    pallas_call x3, Pallas kernels, main_chunk(): pl.pallas_call(lambda *refs: main_body(first, count, *refs), out_shape=(p...  4.39 us
    ppermute x1, starting transfers between devices, local(): south = lax.ppermute(q, 'lat', north_way)  3.04 us
    pallas_call x1, Pallas kernels, tail_chunk(): pl.pallas_call(lambda *refs: tail_body(sizes, *refs), out_shape=jax.Shape...  2.16 us
    pallas_call x1, Pallas kernels, first_halos(): pl.pallas_call(lambda *refs: first_body(count, *refs), out_shape=(message...  1.39 us
    ppermute x1, starting transfers between devices, local(): north = lax.ppermute(q, 'lat', south_way)  1.29 us
  transfers between devices with their start and end apart: 12, of which 4 were waited for; matrix products, arithmetic and copies ran while one was open for 0% of the time, Pallas kernels for 16%

profile of v5, /device:TPU:0, one launch (start us, length us, event | category | flops | bytes accessed | tf_op | source)
XLA Modules:
  0.0 54.5 jit_solution(16858767546715016951)
XLA Ops:
  0.6 0.0 copy-start
  0.6 1.4 %first_halos.1 = (f32[656,128]{1,0:T(8,128)S(1)}, f32[648,128]{1,0:T(8,128)S(1)}, f32[8,128]{1,0:T(8,128)S(1)}) custom-call(f32[36,144,128]{2,1,0:T(8,128)} %bitcast.7, f32[4,128]{1,0:T(4,128)} %bitcast.19, s32[1,192]{1,0:T(1,128)} %refs_2_.1), custom_call_target="tpu_custom_call" | custom-call | bytes 2000000 | tf_op jit(solution)/shard_map/first_halos/pallas_call | solution.py:169
  2.0 0.0 copy-start.1
  2.1 0.0 copy-start.2
  2.1 3.0 %collective-permute-start.4 = (f32[656,128]{1,0:T(8,128)S(1)}, f32[656,128]{1,0:T(8,128)S(1)}, u32[]{:S(2)}, u32[]{:S(2)}) collective-permute-start(f32[656,128]{1,0:T(8,128)S(1)} %get-tuple-element.25), channel_id=1, source_target_pairs={{0,4},{4,0},{8,12},{12,8},{16,20},{20,16},{24,28},{28,24},{1,5},{5... | collective-permute-start | bytes 1007624 | tf_op jit(solution)/shard_map/ppermute | solution.py:591
  5.1 3.5 %collective-permute-start.9 = (f32[648,128]{1,0:T(8,128)S(1)}, f32[648,128]{1,0:T(8,128)S(1)}, u32[]{:S(2)}, u32[]{:S(2)}) collective-permute-start(f32[648,128]{1,0:T(8,128)S(1)} %get-tuple-element.32), channel_id=1, source_target_pairs={{0,28},{4,8},{8,4},{12,16},{16,12},{20,24},{24,20},{28,0},{1,29},{... | collective-permute-start | bytes 995336 | tf_op jit(solution)/shard_map/ppermute | solution.py:591
  8.6 0.0 copy-done
  8.6 0.0 copy-start.4
  8.6 0.7 %copy-done.4 = s32[4,128]{1,0:T(4,128)S(1)} copy-done((s32[4,128]{1,0:T(4,128)S(1)}, s32[4,128]{1,0:T(4,128)}, u32[]{:S(2)}) %copy-start.4) | copy-done | bytes 2072
  9.3 1.3 %pack_edges.1 = f32[4,7,8,128]{3,2,1,0:T(8,128)S(1)} custom-call(f32[36,144,128]{2,1,0:T(8,128)S(1)} %bitcast.8, s32[4,128]{1,0:T(4,128)S(1)} %copy-done.4, f32[8,128]{1,0:T(8,128)S(1)} %get-tuple-element.22.after), custom_call_target="tpu_custom_call" | custom-call | bytes 4000000 | tf_op jit(solution)/shard_map/pack_edges/pallas_call | solution.py:211
  10.6 1.3 %collective-permute-start.1 = (f32[4,7,8,128]{3,2,1,0:T(8,128)S(1)}, f32[4,7,8,128]{3,2,1,0:T(8,128)S(1)}, u32[]{:S(2)}, u32[]{:S(2)}) collective-permute-start(f32[4,7,8,128]{3,2,1,0:T(8,128)S(1)} %pack_edges.1), channel_id=1, source_target_pairs={{1,0},{2,1},{3,2},{5,4},{6,5},{7,6},{9,8},{10,9},{11,10},{13,12},{... | collective-permute-start | bytes 344072 | tf_op jit(solution)/shard_map/ppermute | solution.py:600
  11.9 3.0 %collective-permute-start = (f32[4,7,8,128]{3,2,1,0:T(8,128)S(1)}, f32[4,7,8,128]{3,2,1,0:T(8,128)S(1)}, u32[]{:S(2)}, u32[]{:S(2)}) collective-permute-start(f32[4,7,8,128]{3,2,1,0:T(8,128)S(1)} %pack_edges.1), channel_id=1, source_target_pairs={{0,1},{1,2},{2,3},{4,5},{5,6},{6,7},{8,9},{9,10},{10,11},{12,13},{... | collective-permute-start | bytes 344072 | tf_op jit(solution)/shard_map/ppermute | solution.py:599
  15.0 0.0 collective-permute-done.1.refs_2_
  15.0 0.9 %collective-permute-done.refs_1_ = f32[4,7,8,128]{3,2,1,0:T(8,128)S(1)} collective-permute-done((f32[4,7,8,128]{3,2,1,0:T(8,128)S(1)}, f32[4,7,8,128]{3,2,1,0:T(8,128)S(1)}, u32[]{:S(2)}, u32[]{:S(2)}) %collective-permute-start) | collective-permute-done | bytes 114720 | tf_op jit(solution)/shard_map/ppermute | solution.py:599
  15.9 0.1 second_halos.1
  16.0 0.1 collective-permute-start.2
  16.1 1.9 %collective-permute-start.3 = (f32[528,128]{1,0:T(8,128)S(1)}, f32[528,128]{1,0:T(8,128)S(1)}, u32[]{:S(2)}, u32[]{:S(2)}) collective-permute-start(f32[528,128]{1,0:T(8,128)S(1)} %get-tuple-element.24), channel_id=1, source_target_pairs={{0,28},{4,8},{8,4},{12,16},{16,12},{20,24},{24,20},{28,0},{1,29},{... | collective-permute-start | bytes 811016 | tf_op jit(solution)/shard_map/ppermute | solution.py:591
  18.0 0.0 copy-done.1
  18.0 0.0 copy-done.2
  18.0 1.0 %stencil_weights.1.refs_1_.refs_2_ = f32[36,5,8,8,128]{4,3,2,1,0:T(8,128)S(1)} custom-call(f32[5,36,128]{2,1,0:T(8,128)S(1)} %copy-done.1, f32[6,36,128]{2,1,0:T(8,128)S(1)} %copy-done.2, f32[8,128]{1,0:T(8,128)S(1)} %get-tuple-element.22.after), custom_call_target="tpu_custom_call" | custom-call | bytes 2000000 | tf_op jit(solution)/shard_map/stencil_weights/pallas_call | solution.py:379
  19.0 0.0 copy-start.5
  19.0 0.0 copy-start.6
  19.0 0.0 copy-start.7
  19.0 0.0 copy-start.8
  19.0 0.0 collective-permute-done.9.refs_4_.refs_1_
  19.0 1.2 %collective-permute-done.4.refs_3_.refs_0_ = f32[656,128]{1,0:T(8,128)S(1)} collective-permute-done((f32[656,128]{1,0:T(8,128)S(1)}, f32[656,128]{1,0:T(8,128)S(1)}, u32[]{:S(2)}, u32[]{:S(2)}) %collective-permute-start.4) | collective-permute-done | bytes 335904 | tf_op jit(solution)/shard_map/ppermute | solution.py:591
  20.3 0.1 later_halos.3
  20.4 0.0 copy-start.3
  20.4 8.3 %collective-permute-start.10 = (f32[648,128]{1,0:T(8,128)S(1)}, f32[648,128]{1,0:T(8,128)S(1)}, u32[]{:S(2)}, u32[]{:S(2)}) collective-permute-start(f32[648,128]{1,0:T(8,128)S(1)} %get-tuple-element.35), channel_id=1, source_target_pairs={{0,4},{4,0},{8,12},{12,8},{16,20},{20,16},{24,28},{28,24},{1,5},{5... | collective-permute-start | bytes 995336 | tf_op jit(solution)/shard_map/ppermute | solution.py:591
  28.7 3.8 %collective-permute-start.11 = (f32[648,128]{1,0:T(8,128)S(1)}, f32[648,128]{1,0:T(8,128)S(1)}, u32[]{:S(2)}, u32[]{:S(2)}) collective-permute-start(f32[648,128]{1,0:T(8,128)S(1)} %get-tuple-element.36), channel_id=1, source_target_pairs={{0,28},{4,8},{8,4},{12,16},{16,12},{20,24},{24,20},{28,0},{1,29},{... | collective-permute-start | bytes 995336 | tf_op jit(solution)/shard_map/ppermute | solution.py:591
  32.5 0.0 collective-permute-start.5
  32.5 5.1 %collective-permute-done.5.refs_7_ = f32[16,128]{1,0:T(8,128)S(1)} collective-permute-done((f32[16,128]{1,0:T(8,128)S(1)}, f32[16,128]{1,0:T(8,128)S(1)}, u32[]{:S(2)}, u32[]{:S(2)}) %collective-permute-start.5) | collective-permute-done | bytes 8224 | tf_op jit(solution)/shard_map/ppermute | solution.py:610
  37.6 1.2 %collective-permute-start.6 = (f32[32,128]{1,0:T(8,128)S(1)}, f32[32,128]{1,0:T(8,128)S(1)}, u32[]{:S(2)}, u32[]{:S(2)}) collective-permute-start(f32[32,128]{1,0:T(8,128)S(1)} %pad_maximum_fusion), channel_id=1, source_target_pairs={{0,16},{4,20},{8,24},{12,28},{16,0},{20,4},{24,8},{28,12},{1,17},{... | collective-permute-start | bytes 49160 | tf_op jit(solution)/shard_map/ppermute | solution.py:610
  39.4 2.8 %collective-permute-done.6.refs_8_ = f32[32,128]{1,0:T(8,128)S(1)} collective-permute-done((f32[32,128]{1,0:T(8,128)S(1)}, f32[32,128]{1,0:T(8,128)S(1)}, u32[]{:S(2)}, u32[]{:S(2)}) %collective-permute-start.6) | collective-permute-done | bytes 16416 | tf_op jit(solution)/shard_map/ppermute | solution.py:610
  42.3 0.0 copy-done.5
  42.3 0.0 copy-done.6
  42.3 0.0 copy-done.7
  42.3 0.0 copy-done.8
  42.3 0.9 %surface_wind.1 = (f32[2,4,128]{2,1,0:T(4,128)}, f32[4,8,128]{2,1,0:T(8,128)S(1)}, f32[4,36,128]{2,1,0:T(8,128)S(1)}, f32[4,36,128]{2,1,0:T(8,128)S(1)}) custom-call(f32[1,1]{1,0:T(1,128)} %bitcast.6.refs_0_, s32[16,128]{1,0:T(8,128)S(1)} %bitcast.16, f32[16,128]{1,0:T(8,128)S(1)} %bitcast.17, f32[6,36,128]{2,1,0:T(8,128)S(1)} %copy-done.2, ...), custom_call_target="tpu_custom_call" | custom-call | bytes 2000000 | tf_op jit(solution)/shard_map/surface_wind/pallas_call | solution.py:349
  43.2 0.0 collective-permute-done.2.refs_0_.refs_1_.refs_3_
  43.2 0.0 collective-permute-done.3.refs_1_.refs_2_.refs_4_
  43.2 1.7 %collective-permute-start.7 = (f32[216,128]{1,0:T(8,128)S(1)}, f32[216,128]{1,0:T(8,128)S(1)}, u32[]{:S(2)}, u32[]{:S(2)}) collective-permute-start(f32[216,128]{1,0:T(8,128)S(1)} %get-tuple-element.27), channel_id=1, source_target_pairs={{0,4},{4,0},{8,12},{12,8},{16,20},{20,16},{24,28},{28,24},{1,5},{5... | collective-permute-start | bytes 331784 | tf_op jit(solution)/shard_map/ppermute | solution.py:591
  44.9 1.8 %collective-permute-start.8 = (f32[216,128]{1,0:T(8,128)S(1)}, f32[216,128]{1,0:T(8,128)S(1)}, u32[]{:S(2)}, u32[]{:S(2)}) collective-permute-start(f32[216,128]{1,0:T(8,128)S(1)} %get-tuple-element.28), channel_id=1, source_target_pairs={{0,28},{4,8},{8,4},{12,16},{16,12},{20,24},{24,20},{28,0},{1,29},{... | collective-permute-start | bytes 331784 | tf_op jit(solution)/shard_map/ppermute | solution.py:591
  46.7 0.0 copy-done.3
  46.7 1.2 %move_ghosts.1.refs_5_ = f32[36,4,5,8,128]{4,3,2,1,0:T(8,128)S(1)} custom-call(f32[4,7,8,128]{3,2,1,0:T(8,128)S(1)} %get-tuple-element.29.refs_0_, f32[528,128]{1,0:T(8,128)S(1)} %collective-permute-done.2.refs_0_.refs_1_.refs_3_, f32[528,128]{1,0:T(8,128)S(1)} %collective-permute-done.3.refs_1_.refs_2_.refs_4_, f32[5,6,8,128]{3,2,1,0:T(8,128)S(1)} %copy-done.3), custom_call_target="tpu_custom_call" | custom-call | bytes 2000000 | tf_op jit(solution)/shard_map/move_ghosts/pallas_call | solution.py:295
  47.9 1.1 %chunk.4 = (f32[8,144,128]{2,1,0:T(8,128)S(1)}, f32[4,8,128]{2,1,0:T(8,128)S(1)}) custom-call(f32[5,36,128]{2,1,0:T(8,128)S(1)} %copy-done.1, f32[36,5,8,8,128]{4,3,2,1,0:T(8,128)S(1)} %stencil_weights.1.refs_1_.refs_2_, f32[36,144,128]{2,1,0:T(8,128)S(1)} %bitcast.12, f32[528,128]{1,0:T(8,128)S(1)} %collective-permute-done.2.refs_0_.refs_1_.refs_3_, ...), custom_call_target="tpu_custom_call" | custom-call | bytes 1000000 | tf_op jit(solution)/shard_map/chunk/pallas_call | solution.py:499
  49.0 1.6 %chunk.3 = (f32[12,144,128]{2,1,0:T(8,128)S(1)}, f32[4,8,128]{2,1,0:T(8,128)S(1)}) custom-call(f32[5,36,128]{2,1,0:T(8,128)S(1)} %copy-done.1, f32[36,5,8,8,128]{4,3,2,1,0:T(8,128)S(1)} %stencil_weights.1.refs_1_.refs_2_, f32[36,144,128]{2,1,0:T(8,128)S(1)} %bitcast.13, f32[656,128]{1,0:T(8,128)S(1)} %collective-permute-done.4.refs_3_.refs_0_, ...), custom_call_target="tpu_custom_call" | custom-call | bytes 1000000 | tf_op jit(solution)/shard_map/chunk/pallas_call | solution.py:499
  50.6 0.0 collective-permute-done.10.refs_3_
  50.7 0.0 collective-permute-done.11.refs_4_
  50.7 1.6 %chunk.5 = (f32[12,144,128]{2,1,0:T(8,128)S(1)}, f32[4,8,128]{2,1,0:T(8,128)S(1)}) custom-call(f32[5,36,128]{2,1,0:T(8,128)S(1)} %copy-done.1, f32[36,5,8,8,128]{4,3,2,1,0:T(8,128)S(1)} %stencil_weights.1.refs_1_.refs_2_, f32[36,144,128]{2,1,0:T(8,128)S(1)} %bitcast.14, f32[648,128]{1,0:T(8,128)S(1)} %collective-permute-done.10.refs_3_, ...), custom_call_target="tpu_custom_call" | custom-call | bytes 1000000 | tf_op jit(solution)/shard_map/chunk/pallas_call | solution.py:499
  52.3 0.0 collective-permute-done.7.refs_3_
  52.3 0.0 collective-permute-done.8.refs_4_
  52.4 2.2 %last_chunk.1 = f32[36,144,128]{2,1,0:T(8,128)} custom-call(f32[5,36,128]{2,1,0:T(8,128)S(1)} %copy-done.1, f32[36,5,8,8,128]{4,3,2,1,0:T(8,128)S(1)} %stencil_weights.1.refs_1_.refs_2_, f32[36,144,128]{2,1,0:T(8,128)S(1)} %bitcast.15, f32[216,128]{1,0:T(8,128)S(1)} %collective-permute-done.7.refs_3_, f32[216,128]{1,0:T(8,128)S(1)} %collective-permute-done.8.refs_4_, ...), custom_call_target="tpu_custom_call" | custom-call | bytes 6000000 | tf_op jit(solution)/shard_map/last_chunk/pallas_call | solution.py:558
  (4 shorter events, 0.0 us)
Async XLA Ops:
  0.6 8.0 %copy-start = (f32[36,36,4,128]{3,2,1,0:T(4,128)S(1)}, f32[36,36,4,128]{3,2,1,0:T(4,128)}, u32[]{:S(2)}) copy-start(f32[36,36,4,128]{3,2,1,0:T(4,128)} %param.11) | copy-start | bytes 7962628
  2.0 15.9 %copy-start.1 = (f32[5,36,128]{2,1,0:T(8,128)S(1)}, f32[5,36,128]{2,1,0:T(8,128)}, u32[]{:S(2)}) copy-start(f32[5,36,128]{2,1,0:T(8,128)} %constant.6.clone.scal.refs_0_) | copy-start | bytes 276484
  2.1 15.9 %copy-start.2 = (f32[6,36,128]{2,1,0:T(8,128)S(1)}, f32[6,36,128]{2,1,0:T(8,128)}, u32[]{:S(2)}) copy-start(f32[6,36,128]{2,1,0:T(8,128)} %constant.7.clone.ang.refs_3_) | copy-start | bytes 331780
  2.1 18.2 %collective-permute-start.4 = (f32[656,128]{1,0:T(8,128)S(1)}, f32[656,128]{1,0:T(8,128)S(1)}, u32[]{:S(2)}, u32[]{:S(2)}) collective-permute-start(f32[656,128]{1,0:T(8,128)S(1)} %get-tuple-element.25), channel_id=1, source_target_pairs={{0,4},{4,0},{8,12},{12,8},{16,20},{20,16},{24,28},{28,24},{1,5},{5... | collective-permute-start | bytes 1007624 | tf_op jit(solution)/shard_map/ppermute | solution.py:591
  5.1 13.9 %collective-permute-start.9 = (f32[648,128]{1,0:T(8,128)S(1)}, f32[648,128]{1,0:T(8,128)S(1)}, u32[]{:S(2)}, u32[]{:S(2)}) collective-permute-start(f32[648,128]{1,0:T(8,128)S(1)} %get-tuple-element.32), channel_id=1, source_target_pairs={{0,28},{4,8},{8,4},{12,16},{16,12},{20,24},{24,20},{28,0},{1,29},{... | collective-permute-start | bytes 995336 | tf_op jit(solution)/shard_map/ppermute | solution.py:591
  8.6 0.7 %copy-start.4 = (s32[4,128]{1,0:T(4,128)S(1)}, s32[4,128]{1,0:T(4,128)}, u32[]{:S(2)}) copy-start(s32[4,128]{1,0:T(4,128)} %refs_4_.1) | copy-start | bytes 6148
  10.6 4.3 %collective-permute-start.1 = (f32[4,7,8,128]{3,2,1,0:T(8,128)S(1)}, f32[4,7,8,128]{3,2,1,0:T(8,128)S(1)}, u32[]{:S(2)}, u32[]{:S(2)}) collective-permute-start(f32[4,7,8,128]{3,2,1,0:T(8,128)S(1)} %pack_edges.1), channel_id=1, source_target_pairs={{1,0},{2,1},{3,2},{5,4},{6,5},{7,6},{9,8},{10,9},{11,10},{13,12},{... | collective-permute-start | bytes 344072 | tf_op jit(solution)/shard_map/ppermute | solution.py:600
  11.9 4.0 %collective-permute-start = (f32[4,7,8,128]{3,2,1,0:T(8,128)S(1)}, f32[4,7,8,128]{3,2,1,0:T(8,128)S(1)}, u32[]{:S(2)}, u32[]{:S(2)}) collective-permute-start(f32[4,7,8,128]{3,2,1,0:T(8,128)S(1)} %pack_edges.1), channel_id=1, source_target_pairs={{0,1},{1,2},{2,3},{4,5},{5,6},{6,7},{8,9},{9,10},{10,11},{12,13},{... | collective-permute-start | bytes 344072 | tf_op jit(solution)/shard_map/ppermute | solution.py:599
  16.0 27.2 %collective-permute-start.2 = (f32[528,128]{1,0:T(8,128)S(1)}, f32[528,128]{1,0:T(8,128)S(1)}, u32[]{:S(2)}, u32[]{:S(2)}) collective-permute-start(f32[528,128]{1,0:T(8,128)S(1)} %get-tuple-element.23), channel_id=1, source_target_pairs={{0,4},{4,0},{8,12},{12,8},{16,20},{20,16},{24,28},{28,24},{1,5},{5... | collective-permute-start | bytes 811016 | tf_op jit(solution)/shard_map/ppermute | solution.py:591
  16.1 27.1 %collective-permute-start.3 = (f32[528,128]{1,0:T(8,128)S(1)}, f32[528,128]{1,0:T(8,128)S(1)}, u32[]{:S(2)}, u32[]{:S(2)}) collective-permute-start(f32[528,128]{1,0:T(8,128)S(1)} %get-tuple-element.24), channel_id=1, source_target_pairs={{0,28},{4,8},{8,4},{12,16},{16,12},{20,24},{24,20},{28,0},{1,29},{... | collective-permute-start | bytes 811016 | tf_op jit(solution)/shard_map/ppermute | solution.py:591
  19.0 23.3 %copy-start.5 = (s32[4,128]{1,0:T(4,128)S(1)}, s32[4,128]{1,0:T(4,128)}, u32[]{:S(2)}) copy-start(s32[4,128]{1,0:T(4,128)} %refs_4_.1) | copy-start | bytes 6148
  19.0 23.3 %copy-start.6 = (s32[4,4,128]{2,1,0:T(4,128)S(1)}, s32[4,4,128]{2,1,0:T(4,128)}, u32[]{:S(2)}) copy-start(s32[4,4,128]{2,1,0:T(4,128)} %param.17) | copy-start | bytes 24580
  19.0 23.3 %copy-start.7 = (f32[4,4,128]{2,1,0:T(4,128)S(1)}, f32[4,4,128]{2,1,0:T(4,128)}, u32[]{:S(2)}) copy-start(f32[4,4,128]{2,1,0:T(4,128)} %param.18) | copy-start | bytes 24580
  19.0 23.3 %copy-start.8 = (f32[2,4,128]{2,1,0:T(4,128)S(1)}, f32[2,4,128]{2,1,0:T(4,128)}, u32[]{:S(2)}) copy-start(f32[2,4,128]{2,1,0:T(4,128)} %refs_5_.1) | copy-start | bytes 12292
  20.4 26.3 %copy-start.3 = (f32[5,6,8,128]{3,2,1,0:T(8,128)S(1)}, f32[5,6,8,128]{3,2,1,0:T(8,128)}, u32[]{:S(2)}) copy-start(f32[5,6,8,128]{3,2,1,0:T(8,128)} %constant.8.clone.refs_3_) | copy-start | bytes 368644
  20.4 30.3 %collective-permute-start.10 = (f32[648,128]{1,0:T(8,128)S(1)}, f32[648,128]{1,0:T(8,128)S(1)}, u32[]{:S(2)}, u32[]{:S(2)}) collective-permute-start(f32[648,128]{1,0:T(8,128)S(1)} %get-tuple-element.35), channel_id=1, source_target_pairs={{0,4},{4,0},{8,12},{12,8},{16,20},{20,16},{24,28},{28,24},{1,5},{5... | collective-permute-start | bytes 995336 | tf_op jit(solution)/shard_map/ppermute | solution.py:591
  28.7 22.0 %collective-permute-start.11 = (f32[648,128]{1,0:T(8,128)S(1)}, f32[648,128]{1,0:T(8,128)S(1)}, u32[]{:S(2)}, u32[]{:S(2)}) collective-permute-start(f32[648,128]{1,0:T(8,128)S(1)} %get-tuple-element.36), channel_id=1, source_target_pairs={{0,28},{4,8},{8,4},{12,16},{16,12},{20,24},{24,20},{28,0},{1,29},{... | collective-permute-start | bytes 995336 | tf_op jit(solution)/shard_map/ppermute | solution.py:591
  32.5 5.1 %collective-permute-start.5 = (f32[16,128]{1,0:T(8,128)S(1)}, f32[16,128]{1,0:T(8,128)S(1)}, u32[]{:S(2)}, u32[]{:S(2)}) collective-permute-start(f32[16,128]{1,0:T(8,128)S(1)} %pad_maximum_fusion.1.refs_6_), channel_id=1, source_target_pairs={{0,8},{4,12},{8,0},{12,4},{16,24},{20,28},{24,16},{28,20},{1,9},{5... | collective-permute-start | bytes 24584 | tf_op jit(solution)/shard_map/ppermute | solution.py:610
  37.6 4.6 %collective-permute-start.6 = (f32[32,128]{1,0:T(8,128)S(1)}, f32[32,128]{1,0:T(8,128)S(1)}, u32[]{:S(2)}, u32[]{:S(2)}) collective-permute-start(f32[32,128]{1,0:T(8,128)S(1)} %pad_maximum_fusion), channel_id=1, source_target_pairs={{0,16},{4,20},{8,24},{12,28},{16,0},{20,4},{24,8},{28,12},{1,17},{... | collective-permute-start | bytes 49160 | tf_op jit(solution)/shard_map/ppermute | solution.py:610
  43.2 9.1 %collective-permute-start.7 = (f32[216,128]{1,0:T(8,128)S(1)}, f32[216,128]{1,0:T(8,128)S(1)}, u32[]{:S(2)}, u32[]{:S(2)}) collective-permute-start(f32[216,128]{1,0:T(8,128)S(1)} %get-tuple-element.27), channel_id=1, source_target_pairs={{0,4},{4,0},{8,12},{12,8},{16,20},{20,16},{24,28},{28,24},{1,5},{5... | collective-permute-start | bytes 331784 | tf_op jit(solution)/shard_map/ppermute | solution.py:591
  44.9 7.4 %collective-permute-start.8 = (f32[216,128]{1,0:T(8,128)S(1)}, f32[216,128]{1,0:T(8,128)S(1)}, u32[]{:S(2)}, u32[]{:S(2)}) collective-permute-start(f32[216,128]{1,0:T(8,128)S(1)} %get-tuple-element.28), channel_id=1, source_target_pairs={{0,28},{4,8},{8,4},{12,16},{16,12},{20,24},{24,20},{28,0},{1,29},{... | collective-permute-start | bytes 331784 | tf_op jit(solution)/shard_map/ppermute | solution.py:591

commit v6 on v5

--- a/solution.py
+++ b/solution.py
@@ -27,11 +27,13 @@
 HALO = DIRS + DIRS // 2
 NEAR_SPLIT = 16
 FAR = DIRS // 2
-PACK = 6
+PACK = 8
+SPAN = LANES // PACK
+OFFSETS, WIDTHS, EDGES = (0, 3, 6, 10, 13), (3, 3, 4, 3, 3), (0, 0, 0, 1, 1)
 CHUNKS = (12, 8, 12, 4)
-GROUPS = FREQS // PACK
+GROUPS = -(-FREQS // PACK)
 PIECE = 4
-EDGE_ROWS = 2 * (FREQS // PACK) * 8
+EDGE_ROWS = 2 * (-(-FREQS // PACK)) * 8
 VMEM = 32 * 1024 * 1024
 FIRST_VMEM = 63000000
 
@@ -70,7 +72,7 @@
 
 
 def packed_weights():
-    out = np.zeros((5, FREQS // PACK, 8, LANES), np.float64)
+    out = np.zeros((5, GROUPS, 8, LANES), np.float64)
     for k in range(FREQS):
         for b, j0 in enumerate(BLOCKS):
             c = courant_max * ratio[k] * np.cos(theta[j0 : j0 + 8])
@@ -84,9 +86,9 @@
                 np.where(pos, down, up),
                 np.where(pos, zero, far),
             ]
-            lane = 4 * ((k % PACK) * len(BLOCKS) + b)
+            lane = (k % PACK) * SPAN + OFFSETS[b]
             for d in range(5):
-                out[d, k // PACK, :, lane : lane + 4] = five[d][:, None]
+                out[d, k // PACK, :, lane : lane + WIDTHS[b]] = five[d][:, None]
     return out.astype(np.float32)
 
 
@@ -184,26 +186,42 @@
     )(x, wind, cells)
 
 
+def edge_ids():
+    place = lane_ids() % SPAN
+    edge = place
+    for offset, first in zip(OFFSETS[1:], EDGES[1:]):
+        edge = jnp.where(place >= offset, place - (offset - first), edge)
+    return edge
+
+
+def edge_shift(r, b):
+    return (r * SPAN + OFFSETS[b] + 2 - EDGES[b]) % LANES
+
+
 def edge_body(x, sea, after, q):
     lane = lane_ids()
-    block = lane // 4
-
-    def body(g, _):
+    edge = edge_ids()
+
+    def pack(g, count):
         for cell in range(CELLS):
             acc = jnp.zeros((8, LANES), F32)
-            for r in range(PACK):
+            for r in range(count):
                 for b, j0 in enumerate(BLOCKS):
-                    at = r * len(BLOCKS) + b
                     rows = x[g * PACK + r, pl.ds(cell + 4 * j0, 8, stride=4), :]
-                    acc = jnp.where(block == at, pltpu.roll(rows, (4 * at + 2) % LANES, 1), acc)
+                    rows = pltpu.roll(rows, edge_shift(r, b), 1)
+                    acc = jnp.where(lane >= r * SPAN + OFFSETS[b], rows, acc)
             q[cell, g] = acc
+
+    def body(g, _):
+        pack(g, PACK)
         return 0
 
-    lax.fori_loop(0, GROUPS, body, 0)
+    lax.fori_loop(0, FREQS // PACK, body, 0)
+    pack(GROUPS - 1, FREQS - (GROUPS - 1) * PACK)
     for cell in range(CELLS):
         mask = jnp.zeros((8, LANES), F32)
         for n, at in enumerate((LANES - 2, LANES - 1, 0, 1)):
-            mask = jnp.where(lane % 4 == n, sea[pl.ds(cell, 1), pl.ds(at, 1)].astype(F32), mask)
+            mask = jnp.where(edge == n, sea[pl.ds(cell, 1), pl.ds(at, 1)].astype(F32), mask)
         q[cell, GROUPS] = mask
 
 
@@ -220,7 +238,7 @@
 
 
 def second_body(start, count, x, south, north, one, two, merged):
-    pick = lane_ids() % 4 < 2
+    pick = edge_ids() < 2
     even = is_even()
 
     def body(g, _):
@@ -267,10 +285,11 @@
     )(x, *after)
 
 
-def ghost_body(count, merged, one, two, weights, ghosts):
+def ghost_body(count, merged, one, two, weights, ghosts, token):
     even = is_even()
-
-    def body(g, _):
+    token[...] = jnp.zeros_like(token)
+
+    def spread(g, freqs):
         rows = [
             pl.ds(pl.multiple_of(count * HALO + (n * GROUPS + g) * 8, 8), 8) for n in range(2)
         ]
@@ -282,28 +301,34 @@
             for d in range(1, 5):
                 total = total + weights[d, g] * ext[c + d]
             total = total * merged[c, GROUPS]
-            for r in range(PACK):
+            for r in range(freqs):
                 for b in range(len(BLOCKS)):
-                    shift = LANES - (4 * (r * len(BLOCKS) + b) + 2)
-                    ghosts[g * PACK + r, c, b] = pltpu.roll(total, shift, 1)
+                    ghosts[g * PACK + r, c, b] = pltpu.roll(total, (LANES - edge_shift(r, b)) % LANES, 1)
+
+    def body(g, _):
+        spread(g, PACK)
         return 0
 
-    lax.fori_loop(0, GROUPS, body, 0)
+    lax.fori_loop(0, FREQS // PACK, body, 0)
+    spread(GROUPS - 1, FREQS - (GROUPS - 1) * PACK)
 
 
 def move_ghosts(count, merged, one, two):
     return pl.pallas_call(
         lambda *refs: ghost_body(count, *refs),
-        out_shape=pltpu.VMEM((FREQS, CELLS, len(BLOCKS), 8, LANES), F32),
+        out_shape=(
+            pltpu.VMEM((FREQS, CELLS, len(BLOCKS), 8, LANES), F32),
+            pltpu.VMEM((8, LANES), F32),
+        ),
         in_specs=[vmem_spec()] * 4,
-        out_specs=vmem_spec(),
+        out_specs=(vmem_spec(),) * 2,
         compiler_params=pltpu.CompilerParams(vmem_limit_bytes=VMEM),
         cost_estimate=pl.CostEstimate(flops=0, bytes_accessed=2000000, transcendentals=0),
         name="move_ghosts",
     )(merged, one, two, PACKED)
 
 
-def wind_body(cap, sources, hour, slots, weights, ang, sea, refr, *rest):
+def wind_body(cap, sources, after, hour, slots, weights, ang, sea, refr, *rest):
     picked = [[jnp.zeros((8, LANES), F32) for _ in range(2)] for _ in range(2)]
     pieces, (wind, sea8, turn, proj, table) = rest[:-5], rest[-5:]
     at = 0
@@ -345,7 +370,7 @@
             proj[cell, j, :] = wind[0, row, :] * ang[2, j, :] + wind[1, row, :] * ang[3, j, :]
 
 
-def surface(cap, sources, hour, pieces, slots, weights, sea, refr):
+def surface(cap, sources, after, hour, pieces, slots, weights, sea, refr):
     return pl.pallas_call(
         lambda *refs: wind_body(cap, sources, *refs),
         out_shape=(
@@ -354,13 +379,13 @@
             pltpu.VMEM((CELLS, DIRS, LANES), F32),
             pltpu.VMEM((CELLS, DIRS, LANES), F32),
         ),
-        in_specs=[vmem_spec()] * (6 + len(pieces)),
+        in_specs=[vmem_spec()] * (7 + len(pieces)),
         out_specs=(vmem_spec(),) * 4,
         scratch_shapes=[pltpu.VMEM((8 * sources, LANES), F32)],
         compiler_params=pltpu.CompilerParams(vmem_limit_bytes=VMEM),
         cost_estimate=pl.CostEstimate(flops=0, bytes_accessed=2000000, transcendentals=0),
         name="surface_wind",
-    )(hour, slots, weights, ANGLES, sea, refr, *pieces)
+    )(after, hour, slots, weights, ANGLES, sea, refr, *pieces)
 
 
 def weight_body(scal, ang, after, table):
@@ -601,7 +626,6 @@
     *sends, merged = second_halos(x, firsts[1], CHUNKS[1], south, north)
     halos.append(exchange(*sends))
     halos.append(exchange(*later_halos(x, firsts[2], CHUNKS[2], *halos[0], weights)))
-    ghosts = move_ghosts(CHUNKS[1], merged, *halos[1])
 
     lists = [jnp.concatenate([packed, halos[0][0][-8:]])]
     step = 2
@@ -609,9 +633,11 @@
         held = lists[0] if len(lists) == 1 else jnp.concatenate(lists)
         lists.append(lax.ppermute(held, "lon", [(i, i ^ step) for i in range(tiles)]))
         step *= 2
+    ghosts, token = move_ghosts(CHUNKS[1], merged, *halos[1])
     surface_wind, *tables = surface(
         cap,
         tiles,
+        token,
         hour_fraction.reshape(1, 1),
         lists,
         recv_slots.reshape(4 * CELLS, LANES),

time: 54.7 us -> 53.8 us (0.984)
  starting transfers between devices: 29.6 us -> 24.3 us
  waiting for transfers between devices: 10.2 us -> 14.8 us
    ppermute x4, starting transfers between devices: 13.1 us -> 6.24 us  [exchange(): lax.ppermute(one, 'lon', swap_one)]
    ppermute x4, waiting for transfers between devices: 1.26 us -> 7.11 us  [exchange(): lax.ppermute(one, 'lon', swap_one)]
    ppermute x4, starting transfers between devices: 11 us -> 12.6 us  [exchange(): lax.ppermute(two, 'lon', swap_two)]
    ppermute x2, waiting for transfers between devices: 7.97 us -> 6.81 us  [local(): lax.ppermute(held, 'lon', [(i, i ^ step) for i in range(tiles)])]
where the time goes in v6:
time: 53.8 us; the launch traced here: 53.7 us
  starting transfers between devices  24.3 us (45%)
  waiting for transfers between devices  14.8 us (28%)
  Pallas kernels  12.3 us (23%)
  between operations  1.53 us (3%)
  local copies, waits for them, and re-layouts  0.73 us (1%)
    ppermute x4, starting transfers between devices, exchange(): lax.ppermute(two, 'lon', swap_two)  12.6 us
    ppermute x4, waiting for transfers between devices, exchange(): lax.ppermute(one, 'lon', swap_one)  7.11 us
    ppermute x2, waiting for transfers between devices, local(): lax.ppermute(held, 'lon', [(i, i ^ step) for i in range(tiles)])  6.81 us
    ppermute x4, starting transfers between devices, exchange(): lax.ppermute(one, 'lon', swap_one)  6.24 us
    pallas_call x3, Pallas kernels, main_chunk(): pl.pallas_call(lambda *refs: main_body(first, count, *refs), out_shape=(p...  4.39 us
    ppermute x1, starting transfers between devices, local(): south = lax.ppermute(q, 'lat', north_way)  3.04 us
    pallas_call x1, Pallas kernels, tail_chunk(): pl.pallas_call(lambda *refs: tail_body(sizes, *refs), out_shape=jax.Shape...  2.18 us
    pallas_call x1, Pallas kernels, first_halos(): pl.pallas_call(lambda *refs: first_body(count, *refs), out_shape=(message...  1.39 us
  transfers between devices with their start and end apart: 12, of which 4 were waited for; matrix products, arithmetic and copies ran while one was open for 0% of the time, Pallas kernels for 16%

profile of v6, /device:TPU:0, one launch (start us, length us, event | category | flops | bytes accessed | tf_op | source)
XLA Modules:
  0.0 53.7 jit_solution(14118756723012438045)
XLA Ops:
  0.6 0.0 copy-start
  0.6 1.4 %first_halos.1 = (f32[656,128]{1,0:T(8,128)S(1)}, f32[648,128]{1,0:T(8,128)S(1)}, f32[8,128]{1,0:T(8,128)S(1)}) custom-call(f32[36,144,128]{2,1,0:T(8,128)} %bitcast.7, f32[4,128]{1,0:T(4,128)} %bitcast.19, s32[1,192]{1,0:T(1,128)} %refs_2_.1), custom_call_target="tpu_custom_call" | custom-call | bytes 2000000 | tf_op jit(solution)/shard_map/first_halos/pallas_call | solution.py:171
  2.0 0.0 copy-start.1
  2.1 0.0 copy-start.2
  2.1 3.0 %collective-permute-start.4 = (f32[656,128]{1,0:T(8,128)S(1)}, f32[656,128]{1,0:T(8,128)S(1)}, u32[]{:S(2)}, u32[]{:S(2)}) collective-permute-start(f32[656,128]{1,0:T(8,128)S(1)} %get-tuple-element.29), channel_id=1, source_target_pairs={{0,4},{4,0},{8,12},{12,8},{16,20},{20,16},{24,28},{28,24},{1,5},{5... | collective-permute-start | bytes 1007624 | tf_op jit(solution)/shard_map/ppermute | solution.py:616
  5.1 3.5 %collective-permute-start.9 = (f32[648,128]{1,0:T(8,128)S(1)}, f32[648,128]{1,0:T(8,128)S(1)}, u32[]{:S(2)}, u32[]{:S(2)}) collective-permute-start(f32[648,128]{1,0:T(8,128)S(1)} %get-tuple-element.36), channel_id=1, source_target_pairs={{0,28},{4,8},{8,4},{12,16},{16,12},{20,24},{24,20},{28,0},{1,29},{... | collective-permute-start | bytes 995336 | tf_op jit(solution)/shard_map/ppermute | solution.py:616
  8.6 0.0 copy-done
  8.6 0.0 copy-start.4
  8.6 0.7 %copy-done.4 = s32[4,128]{1,0:T(4,128)S(1)} copy-done((s32[4,128]{1,0:T(4,128)S(1)}, s32[4,128]{1,0:T(4,128)}, u32[]{:S(2)}) %copy-start.4) | copy-done | bytes 2072
  9.3 1.1 %pack_edges.1 = f32[4,6,8,128]{3,2,1,0:T(8,128)S(1)} custom-call(f32[36,144,128]{2,1,0:T(8,128)S(1)} %bitcast.8, s32[4,128]{1,0:T(4,128)S(1)} %copy-done.4, f32[8,128]{1,0:T(8,128)S(1)} %get-tuple-element.24.after), custom_call_target="tpu_custom_call" | custom-call | bytes 4000000 | tf_op jit(solution)/shard_map/pack_edges/pallas_call | solution.py:229
  10.4 1.3 %collective-permute-start.1 = (f32[4,6,8,128]{3,2,1,0:T(8,128)S(1)}, f32[4,6,8,128]{3,2,1,0:T(8,128)S(1)}, u32[]{:S(2)}, u32[]{:S(2)}) collective-permute-start(f32[4,6,8,128]{3,2,1,0:T(8,128)S(1)} %pack_edges.1), channel_id=1, source_target_pairs={{1,0},{2,1},{3,2},{5,4},{6,5},{7,6},{9,8},{10,9},{11,10},{13,12},{... | collective-permute-start | bytes 294920 | tf_op jit(solution)/shard_map/ppermute | solution.py:625
  11.8 3.0 %collective-permute-start = (f32[4,6,8,128]{3,2,1,0:T(8,128)S(1)}, f32[4,6,8,128]{3,2,1,0:T(8,128)S(1)}, u32[]{:S(2)}, u32[]{:S(2)}) collective-permute-start(f32[4,6,8,128]{3,2,1,0:T(8,128)S(1)} %pack_edges.1), channel_id=1, source_target_pairs={{0,1},{1,2},{2,3},{4,5},{5,6},{6,7},{8,9},{9,10},{10,11},{12,13},{... | collective-permute-start | bytes 294920 | tf_op jit(solution)/shard_map/ppermute | solution.py:624
  14.8 0.0 collective-permute-done.1.refs_2_
  14.8 0.9 %collective-permute-done.refs_1_ = f32[4,6,8,128]{3,2,1,0:T(8,128)S(1)} collective-permute-done((f32[4,6,8,128]{3,2,1,0:T(8,128)S(1)}, f32[4,6,8,128]{3,2,1,0:T(8,128)S(1)}, u32[]{:S(2)}, u32[]{:S(2)}) %collective-permute-start) | collective-permute-done | bytes 98336 | tf_op jit(solution)/shard_map/ppermute | solution.py:624
  15.7 0.1 second_halos.1
  15.8 0.1 collective-permute-start.2
  15.9 1.9 %collective-permute-start.3 = (f32[512,128]{1,0:T(8,128)S(1)}, f32[512,128]{1,0:T(8,128)S(1)}, u32[]{:S(2)}, u32[]{:S(2)}) collective-permute-start(f32[512,128]{1,0:T(8,128)S(1)} %get-tuple-element.26), channel_id=1, source_target_pairs={{0,28},{4,8},{8,4},{12,16},{16,12},{20,24},{24,20},{28,0},{1,29},{... | collective-permute-start | bytes 786440 | tf_op jit(solution)/shard_map/ppermute | solution.py:616
  17.8 0.0 copy-done.1
  17.8 0.0 copy-done.2
  17.8 1.0 %stencil_weights.1.refs_1_.refs_2_ = f32[36,5,8,8,128]{4,3,2,1,0:T(8,128)S(1)} custom-call(f32[5,36,128]{2,1,0:T(8,128)S(1)} %copy-done.1, f32[6,36,128]{2,1,0:T(8,128)S(1)} %copy-done.2, f32[8,128]{1,0:T(8,128)S(1)} %get-tuple-element.24.after), custom_call_target="tpu_custom_call" | custom-call | bytes 2000000 | tf_op jit(solution)/shard_map/stencil_weights/pallas_call | solution.py:404
  18.8 0.0 copy-start.3
  18.8 0.0 copy-start.5
  18.8 0.0 copy-start.6
  18.8 0.0 copy-start.7
  18.8 0.0 copy-start.8
  18.8 0.0 collective-permute-done.9.refs_4_.refs_1_
  18.9 7.1 %collective-permute-done.4.refs_3_.refs_0_ = f32[656,128]{1,0:T(8,128)S(1)} collective-permute-done((f32[656,128]{1,0:T(8,128)S(1)}, f32[656,128]{1,0:T(8,128)S(1)}, u32[]{:S(2)}, u32[]{:S(2)}) %collective-permute-start.4) | collective-permute-done | bytes 335904 | tf_op jit(solution)/shard_map/ppermute | solution.py:616
  26.0 0.1 later_halos.3
  26.0 2.7 %collective-permute-start.10 = (f32[648,128]{1,0:T(8,128)S(1)}, f32[648,128]{1,0:T(8,128)S(1)}, u32[]{:S(2)}, u32[]{:S(2)}) collective-permute-start(f32[648,128]{1,0:T(8,128)S(1)} %get-tuple-element.39), channel_id=1, source_target_pairs={{0,4},{4,0},{8,12},{12,8},{16,20},{20,16},{24,28},{28,24},{1,5},{5... | collective-permute-start | bytes 995336 | tf_op jit(solution)/shard_map/ppermute | solution.py:616
  28.7 3.6 %collective-permute-start.11 = (f32[648,128]{1,0:T(8,128)S(1)}, f32[648,128]{1,0:T(8,128)S(1)}, u32[]{:S(2)}, u32[]{:S(2)}) collective-permute-start(f32[648,128]{1,0:T(8,128)S(1)} %get-tuple-element.40), channel_id=1, source_target_pairs={{0,28},{4,8},{8,4},{12,16},{16,12},{20,24},{24,20},{28,0},{1,29},{... | collective-permute-start | bytes 995336 | tf_op jit(solution)/shard_map/ppermute | solution.py:616
  32.3 0.0 collective-permute-start.5
  32.3 5.1 %collective-permute-done.5.refs_8_ = f32[16,128]{1,0:T(8,128)S(1)} collective-permute-done((f32[16,128]{1,0:T(8,128)S(1)}, f32[16,128]{1,0:T(8,128)S(1)}, u32[]{:S(2)}, u32[]{:S(2)}) %collective-permute-start.5) | collective-permute-done | bytes 8224 | tf_op jit(solution)/shard_map/ppermute | solution.py:634
  37.5 1.2 %collective-permute-start.6 = (f32[32,128]{1,0:T(8,128)S(1)}, f32[32,128]{1,0:T(8,128)S(1)}, u32[]{:S(2)}, u32[]{:S(2)}) collective-permute-start(f32[32,128]{1,0:T(8,128)S(1)} %pad_maximum_fusion), channel_id=1, source_target_pairs={{0,16},{4,20},{8,24},{12,28},{16,0},{20,4},{24,8},{28,12},{1,17},{... | collective-permute-start | bytes 49160 | tf_op jit(solution)/shard_map/ppermute | solution.py:634
  39.3 0.0 collective-permute-done.2.refs_1_.refs_0_.refs_3_
  39.3 0.0 collective-permute-done.3.refs_2_.refs_1_.refs_4_
  39.3 0.0 copy-done.3
  39.3 1.1 %move_ghosts.1 = (f32[36,4,5,8,128]{4,3,2,1,0:T(8,128)S(1)}, f32[8,128]{1,0:T(8,128)S(1)}) custom-call(f32[4,6,8,128]{3,2,1,0:T(8,128)S(1)} %get-tuple-element.27.refs_0_, f32[512,128]{1,0:T(8,128)S(1)} %collective-permute-done.2.refs_1_.refs_0_.refs_3_, f32[512,128]{1,0:T(8,128)S(1)} %collective-permute-done.3.refs_2_.refs_1_.refs_4_, ...), custom_call_target="tpu_custom_call" | custom-call | bytes 2000000 | tf_op jit(solution)/shard_map/move_ghosts/pallas_call | solution.py:317
  40.4 1.7 %collective-permute-done.6.refs_9_ = f32[32,128]{1,0:T(8,128)S(1)} collective-permute-done((f32[32,128]{1,0:T(8,128)S(1)}, f32[32,128]{1,0:T(8,128)S(1)}, u32[]{:S(2)}, u32[]{:S(2)}) %collective-permute-start.6) | collective-permute-done | bytes 16416 | tf_op jit(solution)/shard_map/ppermute | solution.py:634
  42.1 0.0 copy-done.5
  42.1 0.0 copy-done.6
  42.1 0.0 copy-done.7
  42.1 0.0 copy-done.8
  42.1 0.9 %surface_wind.1 = (f32[2,4,128]{2,1,0:T(4,128)}, f32[4,8,128]{2,1,0:T(8,128)S(1)}, f32[4,36,128]{2,1,0:T(8,128)S(1)}, f32[4,36,128]{2,1,0:T(8,128)S(1)}) custom-call(f32[8,128]{1,0:T(8,128)S(1)} %get-tuple-element.28.refs_0_, f32[1,1]{1,0:T(1,128)} %bitcast.6.refs_1_, s32[16,128]{1,0:T(8,128)S(1)} %bitcast.16, f32[16,128]{1,0:T(8,128)S(1)} %bitcast.17, ...), custom_call_target="tpu_custom_call" | custom-call | bytes 2000000 | tf_op jit(solution)/shard_map/surface_wind/pallas_call | solution.py:374
  43.0 0.4 collective-permute-start.7
  43.5 3.6 %collective-permute-start.8 = (f32[216,128]{1,0:T(8,128)S(1)}, f32[216,128]{1,0:T(8,128)S(1)}, u32[]{:S(2)}, u32[]{:S(2)}) collective-permute-start(f32[216,128]{1,0:T(8,128)S(1)} %get-tuple-element.32), channel_id=1, source_target_pairs={{0,28},{4,8},{8,4},{12,16},{16,12},{20,24},{24,20},{28,0},{1,29},{... | collective-permute-start | bytes 331784 | tf_op jit(solution)/shard_map/ppermute | solution.py:616
  47.0 1.1 %chunk.4 = (f32[8,144,128]{2,1,0:T(8,128)S(1)}, f32[4,8,128]{2,1,0:T(8,128)S(1)}) custom-call(f32[5,36,128]{2,1,0:T(8,128)S(1)} %copy-done.1, f32[36,5,8,8,128]{4,3,2,1,0:T(8,128)S(1)} %stencil_weights.1.refs_1_.refs_2_, f32[36,144,128]{2,1,0:T(8,128)S(1)} %bitcast.12, f32[512,128]{1,0:T(8,128)S(1)} %collective-permute-done.2.refs_1_.refs_0_.refs_3_, ...), custom_call_target="tpu_custom_call" | custom-call | bytes 1000000 | tf_op jit(solution)/shard_map/chunk/pallas_call | solution.py:524
  48.1 1.6 %chunk.3 = (f32[12,144,128]{2,1,0:T(8,128)S(1)}, f32[4,8,128]{2,1,0:T(8,128)S(1)}) custom-call(f32[5,36,128]{2,1,0:T(8,128)S(1)} %copy-done.1, f32[36,5,8,8,128]{4,3,2,1,0:T(8,128)S(1)} %stencil_weights.1.refs_1_.refs_2_, f32[36,144,128]{2,1,0:T(8,128)S(1)} %bitcast.13, f32[656,128]{1,0:T(8,128)S(1)} %collective-permute-done.4.refs_3_.refs_0_, ...), custom_call_target="tpu_custom_call" | custom-call | bytes 1000000 | tf_op jit(solution)/shard_map/chunk/pallas_call | solution.py:524
  49.8 0.0 collective-permute-done.10.refs_3_
  49.8 0.0 collective-permute-done.11.refs_4_
  49.8 1.7 %chunk.5 = (f32[12,144,128]{2,1,0:T(8,128)S(1)}, f32[4,8,128]{2,1,0:T(8,128)S(1)}) custom-call(f32[5,36,128]{2,1,0:T(8,128)S(1)} %copy-done.1, f32[36,5,8,8,128]{4,3,2,1,0:T(8,128)S(1)} %stencil_weights.1.refs_1_.refs_2_, f32[36,144,128]{2,1,0:T(8,128)S(1)} %bitcast.14, f32[648,128]{1,0:T(8,128)S(1)} %collective-permute-done.10.refs_3_, ...), custom_call_target="tpu_custom_call" | custom-call | bytes 1000000 | tf_op jit(solution)/shard_map/chunk/pallas_call | solution.py:524
  51.5 0.0 collective-permute-done.7.refs_3_
  51.5 0.0 collective-permute-done.8.refs_4_
  51.5 2.2 %last_chunk.1 = f32[36,144,128]{2,1,0:T(8,128)} custom-call(f32[5,36,128]{2,1,0:T(8,128)S(1)} %copy-done.1, f32[36,5,8,8,128]{4,3,2,1,0:T(8,128)S(1)} %stencil_weights.1.refs_1_.refs_2_, f32[36,144,128]{2,1,0:T(8,128)S(1)} %bitcast.15, f32[216,128]{1,0:T(8,128)S(1)} %collective-permute-done.7.refs_3_, f32[216,128]{1,0:T(8,128)S(1)} %collective-permute-done.8.refs_4_, ...), custom_call_target="tpu_custom_call" | custom-call | bytes 6000000 | tf_op jit(solution)/shard_map/last_chunk/pallas_call | solution.py:583
  (4 shorter events, 0.0 us)
Async XLA Ops:
  0.6 8.0 %copy-start = (f32[36,36,4,128]{3,2,1,0:T(4,128)S(1)}, f32[36,36,4,128]{3,2,1,0:T(4,128)}, u32[]{:S(2)}) copy-start(f32[36,36,4,128]{3,2,1,0:T(4,128)} %param.11) | copy-start | bytes 7962628
  2.0 15.8 %copy-start.1 = (f32[5,36,128]{2,1,0:T(8,128)S(1)}, f32[5,36,128]{2,1,0:T(8,128)}, u32[]{:S(2)}) copy-start(f32[5,36,128]{2,1,0:T(8,128)} %constant.6.clone.scal.refs_0_) | copy-start | bytes 276484
  2.1 15.7 %copy-start.2 = (f32[6,36,128]{2,1,0:T(8,128)S(1)}, f32[6,36,128]{2,1,0:T(8,128)}, u32[]{:S(2)}) copy-start(f32[6,36,128]{2,1,0:T(8,128)} %constant.7.clone.ang.refs_4_) | copy-start | bytes 331780
  2.1 23.9 %collective-permute-start.4 = (f32[656,128]{1,0:T(8,128)S(1)}, f32[656,128]{1,0:T(8,128)S(1)}, u32[]{:S(2)}, u32[]{:S(2)}) collective-permute-start(f32[656,128]{1,0:T(8,128)S(1)} %get-tuple-element.29), channel_id=1, source_target_pairs={{0,4},{4,0},{8,12},{12,8},{16,20},{20,16},{24,28},{28,24},{1,5},{5... | collective-permute-start | bytes 1007624 | tf_op jit(solution)/shard_map/ppermute | solution.py:616
  5.1 13.8 %collective-permute-start.9 = (f32[648,128]{1,0:T(8,128)S(1)}, f32[648,128]{1,0:T(8,128)S(1)}, u32[]{:S(2)}, u32[]{:S(2)}) collective-permute-start(f32[648,128]{1,0:T(8,128)S(1)} %get-tuple-element.36), channel_id=1, source_target_pairs={{0,28},{4,8},{8,4},{12,16},{16,12},{20,24},{24,20},{28,0},{1,29},{... | collective-permute-start | bytes 995336 | tf_op jit(solution)/shard_map/ppermute | solution.py:616
  8.6 0.7 %copy-start.4 = (s32[4,128]{1,0:T(4,128)S(1)}, s32[4,128]{1,0:T(4,128)}, u32[]{:S(2)}) copy-start(s32[4,128]{1,0:T(4,128)} %refs_5_.1) | copy-start | bytes 6148
  10.4 4.3 %collective-permute-start.1 = (f32[4,6,8,128]{3,2,1,0:T(8,128)S(1)}, f32[4,6,8,128]{3,2,1,0:T(8,128)S(1)}, u32[]{:S(2)}, u32[]{:S(2)}) collective-permute-start(f32[4,6,8,128]{3,2,1,0:T(8,128)S(1)} %pack_edges.1), channel_id=1, source_target_pairs={{1,0},{2,1},{3,2},{5,4},{6,5},{7,6},{9,8},{10,9},{11,10},{13,12},{... | collective-permute-start | bytes 294920 | tf_op jit(solution)/shard_map/ppermute | solution.py:625
  11.8 4.0 %collective-permute-start = (f32[4,6,8,128]{3,2,1,0:T(8,128)S(1)}, f32[4,6,8,128]{3,2,1,0:T(8,128)S(1)}, u32[]{:S(2)}, u32[]{:S(2)}) collective-permute-start(f32[4,6,8,128]{3,2,1,0:T(8,128)S(1)} %pack_edges.1), channel_id=1, source_target_pairs={{0,1},{1,2},{2,3},{4,5},{5,6},{6,7},{8,9},{9,10},{10,11},{12,13},{... | collective-permute-start | bytes 294920 | tf_op jit(solution)/shard_map/ppermute | solution.py:624
  15.8 23.4 %collective-permute-start.2 = (f32[512,128]{1,0:T(8,128)S(1)}, f32[512,128]{1,0:T(8,128)S(1)}, u32[]{:S(2)}, u32[]{:S(2)}) collective-permute-start(f32[512,128]{1,0:T(8,128)S(1)} %get-tuple-element.25), channel_id=1, source_target_pairs={{0,4},{4,0},{8,12},{12,8},{16,20},{20,16},{24,28},{28,24},{1,5},{5... | collective-permute-start | bytes 786440 | tf_op jit(solution)/shard_map/ppermute | solution.py:616
  15.9 23.4 %collective-permute-start.3 = (f32[512,128]{1,0:T(8,128)S(1)}, f32[512,128]{1,0:T(8,128)S(1)}, u32[]{:S(2)}, u32[]{:S(2)}) collective-permute-start(f32[512,128]{1,0:T(8,128)S(1)} %get-tuple-element.26), channel_id=1, source_target_pairs={{0,28},{4,8},{8,4},{12,16},{16,12},{20,24},{24,20},{28,0},{1,29},{... | collective-permute-start | bytes 786440 | tf_op jit(solution)/shard_map/ppermute | solution.py:616
  18.8 20.5 %copy-start.3 = (f32[5,5,8,128]{3,2,1,0:T(8,128)S(1)}, f32[5,5,8,128]{3,2,1,0:T(8,128)}, u32[]{:S(2)}) copy-start(f32[5,5,8,128]{3,2,1,0:T(8,128)} %constant.8.clone.refs_3_) | copy-start | bytes 307204
  18.8 23.3 %copy-start.5 = (s32[4,128]{1,0:T(4,128)S(1)}, s32[4,128]{1,0:T(4,128)}, u32[]{:S(2)}) copy-start(s32[4,128]{1,0:T(4,128)} %refs_5_.1) | copy-start | bytes 6148
  18.8 23.3 %copy-start.6 = (s32[4,4,128]{2,1,0:T(4,128)S(1)}, s32[4,4,128]{2,1,0:T(4,128)}, u32[]{:S(2)}) copy-start(s32[4,4,128]{2,1,0:T(4,128)} %param.17) | copy-start | bytes 24580
  18.8 23.3 %copy-start.7 = (f32[4,4,128]{2,1,0:T(4,128)S(1)}, f32[4,4,128]{2,1,0:T(4,128)}, u32[]{:S(2)}) copy-start(f32[4,4,128]{2,1,0:T(4,128)} %param.18) | copy-start | bytes 24580
  18.8 23.3 %copy-start.8 = (f32[2,4,128]{2,1,0:T(4,128)S(1)}, f32[2,4,128]{2,1,0:T(4,128)}, u32[]{:S(2)}) copy-start(f32[2,4,128]{2,1,0:T(4,128)} %refs_6_.1) | copy-start | bytes 12292
  26.0 23.7 %collective-permute-start.10 = (f32[648,128]{1,0:T(8,128)S(1)}, f32[648,128]{1,0:T(8,128)S(1)}, u32[]{:S(2)}, u32[]{:S(2)}) collective-permute-start(f32[648,128]{1,0:T(8,128)S(1)} %get-tuple-element.39), channel_id=1, source_target_pairs={{0,4},{4,0},{8,12},{12,8},{16,20},{20,16},{24,28},{28,24},{1,5},{5... | collective-permute-start | bytes 995336 | tf_op jit(solution)/shard_map/ppermute | solution.py:616
  28.7 21.1 %collective-permute-start.11 = (f32[648,128]{1,0:T(8,128)S(1)}, f32[648,128]{1,0:T(8,128)S(1)}, u32[]{:S(2)}, u32[]{:S(2)}) collective-permute-start(f32[648,128]{1,0:T(8,128)S(1)} %get-tuple-element.40), channel_id=1, source_target_pairs={{0,28},{4,8},{8,4},{12,16},{16,12},{20,24},{24,20},{28,0},{1,29},{... | collective-permute-start | bytes 995336 | tf_op jit(solution)/shard_map/ppermute | solution.py:616
  32.3 5.1 %collective-permute-start.5 = (f32[16,128]{1,0:T(8,128)S(1)}, f32[16,128]{1,0:T(8,128)S(1)}, u32[]{:S(2)}, u32[]{:S(2)}) collective-permute-start(f32[16,128]{1,0:T(8,128)S(1)} %pad_maximum_fusion.1.refs_7_), channel_id=1, source_target_pairs={{0,8},{4,12},{8,0},{12,4},{16,24},{20,28},{24,16},{28,20},{1,9},{5... | collective-permute-start | bytes 24584 | tf_op jit(solution)/shard_map/ppermute | solution.py:634
  37.5 4.6 %collective-permute-start.6 = (f32[32,128]{1,0:T(8,128)S(1)}, f32[32,128]{1,0:T(8,128)S(1)}, u32[]{:S(2)}, u32[]{:S(2)}) collective-permute-start(f32[32,128]{1,0:T(8,128)S(1)} %pad_maximum_fusion), channel_id=1, source_target_pairs={{0,16},{4,20},{8,24},{12,28},{16,0},{20,4},{24,8},{28,12},{1,17},{... | collective-permute-start | bytes 49160 | tf_op jit(solution)/shard_map/ppermute | solution.py:634
  43.0 8.4 %collective-permute-start.7 = (f32[216,128]{1,0:T(8,128)S(1)}, f32[216,128]{1,0:T(8,128)S(1)}, u32[]{:S(2)}, u32[]{:S(2)}) collective-permute-start(f32[216,128]{1,0:T(8,128)S(1)} %get-tuple-element.31), channel_id=1, source_target_pairs={{0,4},{4,0},{8,12},{12,8},{16,20},{20,16},{24,28},{28,24},{1,5},{5... | collective-permute-start | bytes 331784 | tf_op jit(solution)/shard_map/ppermute | solution.py:616
  43.5 8.0 %collective-permute-start.8 = (f32[216,128]{1,0:T(8,128)S(1)}, f32[216,128]{1,0:T(8,128)S(1)}, u32[]{:S(2)}, u32[]{:S(2)}) collective-permute-start(f32[216,128]{1,0:T(8,128)S(1)} %get-tuple-element.32), channel_id=1, source_target_pairs={{0,28},{4,8},{8,4},{12,16},{16,12},{20,24},{24,20},{28,0},{1,29},{... | collective-permute-start | bytes 331784 | tf_op jit(solution)/shard_map/ppermute | solution.py:616

commit v7 on v6

--- a/solution.py
+++ b/solution.py
@@ -329,7 +329,6 @@
 
 
 def wind_body(cap, sources, after, hour, slots, weights, ang, sea, refr, *rest):
-    picked = [[jnp.zeros((8, LANES), F32) for _ in range(2)] for _ in range(2)]
     pieces, (wind, sea8, turn, proj, table) = rest[:-5], rest[-5:]
     at = 0
     for piece in pieces:
@@ -339,24 +338,30 @@
     width = cap * sources
     me = lax.axis_index("lon")
     mine = cap * me
+    high = mine + cap > LANES
+    begin = jnp.where(high, mine - (width - LANES), mine)
+    lane = lane_ids()
+    rows = [jnp.zeros((8, LANES), F32)] * 2
+    for s in range(sources):
+        block = table[pl.ds(pl.multiple_of(8 * (s ^ me), 8), 8), :]
+        for n, to in enumerate((cap * s, cap * s - (width - LANES))):
+            if to < LANES and to + cap > 0:
+                moved = pltpu.roll(block, (to + 2 * LANES - begin) % LANES, 1)
+                rows[n] = jnp.where((lane >= to) & (lane < to + cap), moved, rows[n])
+
+    def entries(n, c):
+        now = [jnp.where(high, rows[n][r + 1 : r + 2], rows[n][r : r + 1]) for r in (2 * c, 2 * c + 4)]
+        return jnp.broadcast_to((1.0 - late) * now[0] + late * now[1], (8, LANES))
+
+    lists = [[entries(n, c) for n in range(2)] for c in range(2)]
+    picked = [[None, None], [None, None]]
     for half in range(2):
         index = slots[pl.ds(8 * half, 8), :]
-        for s in range(sources):
-            place = index - cap * s
-            here = (place >= 0) & (place < cap)
-            place = jnp.clip(place, 0, cap - 1) + mine
-            low = place < LANES
-            place = jnp.where(low, place, place - (width - LANES))
-            for c in range(2):
-                at = 8 * (s ^ me) + 2 * c
-                row = [
-                    (1.0 - late) * table[pl.ds(at + n, 1), :] + late * table[pl.ds(at + 4 + n, 1), :]
-                    for n in range(2)
-                ]
-                row = [jnp.broadcast_to(r, (8, LANES)) for r in row]
-                value = [jnp.take_along_axis(r, place, axis=1) for r in row]
-                value = jnp.where(low, value[0], value[1])
-                picked[half][c] = jnp.where(here, value, picked[half][c])
+        low = index < LANES
+        place = jnp.where(low, index, index - (width - LANES))
+        for c in range(2):
+            value = [jnp.take_along_axis(row, place, axis=1) for row in lists[c]]
+            picked[half][c] = jnp.where(low, value[0], value[1])
     for c in range(2):
         total = weights[pl.ds(0, 8), :] * picked[0][c]
         total = total + weights[pl.ds(8, 8), :] * picked[1][c]
@@ -374,7 +379,7 @@
     return pl.pallas_call(
         lambda *refs: wind_body(cap, sources, *refs),
         out_shape=(
-            jax.ShapeDtypeStruct((2, CELLS, LANES), F32),
+            pltpu.VMEM((2, CELLS, LANES), F32),
             pltpu.VMEM((CELLS, 8, LANES), F32),
             pltpu.VMEM((CELLS, DIRS, LANES), F32),
             pltpu.VMEM((CELLS, DIRS, LANES), F32),
@@ -412,8 +417,8 @@
     )(SCALARS, ANGLES, after)
 
 
-def chunk_pass(
-    first, count, scal, weights, x, one_ref, two_ref, ghosts, sea8, turn, proj, zs, gs, out, out_first
+def chunk_steps(
+    first, scal, weights, x, one_ref, two_ref, ghosts, sea8, turn, proj, zs, gs, out, out_first
 ):
     lane = lane_ids()
     sub = lax.broadcasted_iota(jnp.int32, (8, LANES), 0)
@@ -426,9 +431,9 @@
     def from_east(rows):
         return jnp.where(even, one_ref[rows, :], two_ref[rows, :])
 
-    def one(i, kk, sums):
+    def advect(i, kk, sums):
         k = first + i * GROUP + kk
-        bend, gain, floor = (scal[n, pl.ds(k, 1), :] for n in range(1, 4))
+        sums = list(sums)
         for b, j0 in enumerate(BLOCKS):
             w0, w1, w2, w3, v0, v1, v2, v3 = (weights[k, b, n] for n in range(8))
             cells = [x[k, pl.ds(c + 4 * j0, 8, stride=4), :] for c in range(CELLS)]
@@ -478,7 +483,12 @@
                     far = jnp.where(p, s2, n2)
                 z = v0 * far + v1 * up + v2 * z + v3 * down
                 zs[kk, c, pl.ds(8 + j0, 8), :] = z
-        out_sums = []
+                sums[c] = sums[c] + (jnp.where(sub >= 4, z, 0.0) if b == 4 else z)
+        return tuple(sums)
+
+    def bend_grow(i, kk):
+        k = first + i * GROUP + kk
+        bend, gain, floor = (scal[n, pl.ds(k, 1), :] for n in range(1, 4))
         for c in range(CELLS):
             zs[kk, c, pl.ds(8 + DIRS, 1), :] = zs[kk, c, pl.ds(8, 1), :]
             for b, j0 in enumerate(BLOCKS):
@@ -487,33 +497,36 @@
                 s = bend * turn[c, pl.ds(j0, 8), :]
                 gs[kk, c, pl.ds(8 + j0, 8), :] = s * jnp.where(s > 0, own, nxt)
             gs[kk, c, pl.ds(7, 1), :] = gs[kk, c, pl.ds(7 + DIRS, 1), :]
-            total = sums[c]
             for b, j0 in enumerate(BLOCKS):
                 own = zs[kk, c, pl.ds(8 + j0, 8), :]
                 flux = gs[kk, c, pl.ds(8 + j0, 8), :]
                 prev = gs[kk, c, pl.ds(7 + j0, 8), :]
                 refracted = own - (flux - prev)
-                total = total + (jnp.where(sub >= 4, refracted, 0.0) if b == 4 else refracted)
                 growth = jnp.maximum(proj[c, pl.ds(j0, 8), :] * gain - floor, 0.0)
                 out[out_first + i * GROUP + kk, pl.ds(c + 4 * j0, 8, stride=4), :] = refracted * jnp.exp2(growth)
-            out_sums.append(total)
-        return tuple(out_sums)
-
-    def body(i, sums):
-        for kk in range(GROUP):
-            sums = one(i, kk, sums)
-        return sums
-
-    zero = jnp.zeros((8, LANES), F32)
-    return lax.fori_loop(0, count // GROUP, body, (zero,) * CELLS)
+
+    return advect, bend_grow
+
+
+def no_sums():
+    return (jnp.zeros((8, LANES), F32),) * CELLS
 
 
 def main_body(
     first, count, scal, weights, x, west, east, ghosts, sea8, turn, proj, out, energy, zs, gs
 ):
-    sums = chunk_pass(first, count, scal, weights, x, west, east, ghosts, sea8, turn, proj, zs, gs, out, 0)
-    for c in range(CELLS):
-        energy[c] = sums[c]
+    advect, bend_grow = chunk_steps(
+        first, scal, weights, x, west, east, ghosts, sea8, turn, proj, zs, gs, out, 0
+    )
+
+    def body(i, sums):
+        for kk in range(GROUP):
+            sums = advect(i, kk, sums)
+            bend_grow(i, kk)
+        return sums
+
+    for c, total in enumerate(lax.fori_loop(0, count // GROUP, body, no_sums())):
+        energy[c] = total
 
 
 def pass_scratch():
@@ -536,15 +549,21 @@
     )(SCALARS, weights, x, west, east, ghosts, *tables)
 
 
-def tail_body(sizes, scal, weights, x, west, east, ghosts, sea8, turn, proj, *rest):
+def tail_body(sizes, scal, weights, x, west, east, ghosts, wind, sea8, turn, proj, *rest):
     done = len(sizes) - 1
     parts, energies = rest[:done], rest[done : 2 * done]
-    out_hbm, obuf, zs, gs, out_sem = rest[2 * done :]
+    out_hbm, wind_hbm, obuf, zs, gs, out_sem, wind_sem = rest[2 * done :]
+    stores, at = [pltpu.make_async_copy(wind, wind_hbm, wind_sem)], 0
+    stores[0].start()
     count = sizes[-1]
     first = FREQS - count
-    sums = chunk_pass(
-        first, count, scal, weights, x, west, east, ghosts, sea8, turn, proj, zs, gs, obuf, first
+    advect, bend_grow = chunk_steps(
+        first, scal, weights, x, west, east, ghosts, sea8, turn, proj, zs, gs, obuf, first
     )
+    assert count == GROUP
+    sums = no_sums()
+    for kk in range(GROUP):
+        sums = advect(0, kk, sums)
     sub = lax.broadcasted_iota(jnp.int32, (8, LANES), 0)
     pattern = mask = jnp.zeros((8, LANES), F32)
     for c in range(CELLS):
@@ -555,8 +574,10 @@
         level = mean * (1.0 / energy_ref)
         pattern = jnp.where(sub % CELLS == c, level * level, pattern)
         mask = jnp.where(sub % CELLS == c, sea8[c], mask)
-    stores, at = [], 0
     for n, size in enumerate(sizes):
+        if n == done:
+            for kk in range(GROUP):
+                bend_grow(0, kk)
         for low in range(0, size, PIECE):
             high = min(low + PIECE, size)
 
@@ -570,7 +591,7 @@
             lax.fori_loop(low, high, body, 0)
             span = pl.ds(at + low, high - low)
             stores.append(
-                pltpu.make_async_copy(obuf.at[span], out_hbm.at[span], out_sem.at[len(stores)])
+                pltpu.make_async_copy(obuf.at[span], out_hbm.at[span], out_sem.at[len(stores) - 1])
             )
             stores[-1].start()
         at += size
@@ -578,22 +599,26 @@
         store.wait()
 
 
-def tail_chunk(sizes, weights, x, west, east, ghosts, tables, parts, energies):
+def tail_chunk(sizes, weights, x, west, east, ghosts, wind, tables, parts, energies):
     done = len(sizes) - 1
     return pl.pallas_call(
         lambda *refs: tail_body(sizes, *refs),
-        out_shape=jax.ShapeDtypeStruct((FREQS, ROWS, LANES), F32),
-        in_specs=[vmem_spec()] * (9 + 2 * done),
-        out_specs=any_spec(),
+        out_shape=(
+            jax.ShapeDtypeStruct((FREQS, ROWS, LANES), F32),
+            jax.ShapeDtypeStruct((2, CELLS, LANES), F32),
+        ),
+        in_specs=[vmem_spec()] * (10 + 2 * done),
+        out_specs=(any_spec(), any_spec()),
         scratch_shapes=[
             pltpu.VMEM((FREQS, ROWS, LANES), F32),
             *pass_scratch(),
             pltpu.SemaphoreType.DMA((FREQS // PIECE,)),
+            pltpu.SemaphoreType.DMA,
         ],
         compiler_params=pltpu.CompilerParams(vmem_limit_bytes=VMEM),
         cost_estimate=pl.CostEstimate(flops=0, bytes_accessed=6000000, transcendentals=0),
         name="last_chunk",
-    )(SCALARS, weights, x, west, east, ghosts, *tables, *parts, *energies)
+    )(SCALARS, weights, x, west, east, ghosts, wind, *tables, *parts, *energies)
 
 
 def line(axis):
@@ -655,7 +680,9 @@
             parts.append(part)
             energies.append(energy)
         else:
-            out = tail_chunk(CHUNKS, weights, x, west, east, ghosts, tables, parts, energies)
+            out, surface_wind = tail_chunk(
+                CHUNKS, weights, x, west, east, ghosts, surface_wind, tables, parts, energies
+            )
     return (out.reshape(spectrum.shape), surface_wind)
 
 

time: 53.8 us -> 52.9 us (0.983)
  Pallas kernels: 12.3 us -> 11.3 us
    pallas_call x2, Pallas kernels: 3.05 us -> 2.24 us  [the longest x1 2.03 us: tail_chunk(): pl.pallas_call(lambda *refs: tail_body(sizes, *refs), out_shape=(jax.Shap...]
  transfers between devices with their start and end apart: 12 -> 12, of which waited for: 4 -> 4; matrix products, arithmetic and copies ran while one was open for 0% -> 0% of each run, Pallas kernels for 16% -> 15%
where the time goes in v7:
time: 52.9 us; the launch traced here: 52.7 us
  starting transfers between devices  24.3 us (46%)
  waiting for transfers between devices  14.8 us (28%)
  Pallas kernels  11.3 us (21%)
  between operations  1.54 us (3%)
  local copies, waits for them, and re-layouts  0.73 us (1%)
    ppermute x4, starting transfers between devices, exchange(): lax.ppermute(two, 'lon', swap_two)  12.6 us
    ppermute x4, waiting for transfers between devices, exchange(): lax.ppermute(one, 'lon', swap_one)  7.11 us
    ppermute x2, waiting for transfers between devices, local(): lax.ppermute(held, 'lon', [(i, i ^ step) for i in range(tiles)])  6.81 us
    ppermute x4, starting transfers between devices, exchange(): lax.ppermute(one, 'lon', swap_one)  6.23 us
    pallas_call x3, Pallas kernels, main_chunk(): pl.pallas_call(lambda *refs: main_body(first, count, *refs), out_shape=(p...  4.25 us
    ppermute x1, starting transfers between devices, local(): south = lax.ppermute(q, 'lat', north_way)  3.04 us
    pallas_call x1, Pallas kernels, tail_chunk(): pl.pallas_call(lambda *refs: tail_body(sizes, *refs), out_shape=(jax.Shap...  2.03 us
    pallas_call x1, Pallas kernels, first_halos(): pl.pallas_call(lambda *refs: first_body(count, *refs), out_shape=(message...  1.39 us
  transfers between devices with their start and end apart: 12, of which 4 were waited for; matrix products, arithmetic and copies ran while one was open for 0% of the time, Pallas kernels for 15%

profile of v7, /device:TPU:0, one launch (start us, length us, event | category | flops | bytes accessed | tf_op | source)
XLA Modules:
  0.0 52.7 jit_solution(17521189422918765764)
XLA Ops:
  0.6 0.0 copy-start
  0.6 1.4 %first_halos.1 = (f32[656,128]{1,0:T(8,128)S(1)}, f32[648,128]{1,0:T(8,128)S(1)}, f32[8,128]{1,0:T(8,128)S(1)}) custom-call(f32[36,144,128]{2,1,0:T(8,128)} %bitcast.7, f32[4,128]{1,0:T(4,128)} %bitcast.18, s32[1,192]{1,0:T(1,128)} %refs_2_.1), custom_call_target="tpu_custom_call" | custom-call | bytes 2000000 | tf_op jit(solution)/shard_map/first_halos/pallas_call | solution.py:171
  2.0 0.0 copy-start.1
  2.1 0.0 copy-start.2
  2.1 3.0 %collective-permute-start.4 = (f32[656,128]{1,0:T(8,128)S(1)}, f32[656,128]{1,0:T(8,128)S(1)}, u32[]{:S(2)}, u32[]{:S(2)}) collective-permute-start(f32[656,128]{1,0:T(8,128)S(1)} %get-tuple-element.31), channel_id=1, source_target_pairs={{0,4},{4,0},{8,12},{12,8},{16,20},{20,16},{24,28},{28,24},{1,5},{5... | collective-permute-start | bytes 1007624 | tf_op jit(solution)/shard_map/ppermute | solution.py:641
  5.1 3.5 %collective-permute-start.9 = (f32[648,128]{1,0:T(8,128)S(1)}, f32[648,128]{1,0:T(8,128)S(1)}, u32[]{:S(2)}, u32[]{:S(2)}) collective-permute-start(f32[648,128]{1,0:T(8,128)S(1)} %get-tuple-element.39), channel_id=1, source_target_pairs={{0,28},{4,8},{8,4},{12,16},{16,12},{20,24},{24,20},{28,0},{1,29},{... | collective-permute-start | bytes 995336 | tf_op jit(solution)/shard_map/ppermute | solution.py:641
  8.6 0.0 copy-done
  8.6 0.0 copy-start.4
  8.6 0.7 %copy-done.4 = s32[4,128]{1,0:T(4,128)S(1)} copy-done((s32[4,128]{1,0:T(4,128)S(1)}, s32[4,128]{1,0:T(4,128)}, u32[]{:S(2)}) %copy-start.4) | copy-done | bytes 2072
  9.3 1.1 %pack_edges.1 = f32[4,6,8,128]{3,2,1,0:T(8,128)S(1)} custom-call(f32[36,144,128]{2,1,0:T(8,128)S(1)} %bitcast.8, s32[4,128]{1,0:T(4,128)S(1)} %copy-done.4, f32[8,128]{1,0:T(8,128)S(1)} %get-tuple-element.26.after), custom_call_target="tpu_custom_call" | custom-call | bytes 4000000 | tf_op jit(solution)/shard_map/pack_edges/pallas_call | solution.py:229
  10.4 1.3 %collective-permute-start.1 = (f32[4,6,8,128]{3,2,1,0:T(8,128)S(1)}, f32[4,6,8,128]{3,2,1,0:T(8,128)S(1)}, u32[]{:S(2)}, u32[]{:S(2)}) collective-permute-start(f32[4,6,8,128]{3,2,1,0:T(8,128)S(1)} %pack_edges.1), channel_id=1, source_target_pairs={{1,0},{2,1},{3,2},{5,4},{6,5},{7,6},{9,8},{10,9},{11,10},{13,12},{... | collective-permute-start | bytes 294920 | tf_op jit(solution)/shard_map/ppermute | solution.py:650
  11.8 3.0 %collective-permute-start = (f32[4,6,8,128]{3,2,1,0:T(8,128)S(1)}, f32[4,6,8,128]{3,2,1,0:T(8,128)S(1)}, u32[]{:S(2)}, u32[]{:S(2)}) collective-permute-start(f32[4,6,8,128]{3,2,1,0:T(8,128)S(1)} %pack_edges.1), channel_id=1, source_target_pairs={{0,1},{1,2},{2,3},{4,5},{5,6},{6,7},{8,9},{9,10},{10,11},{12,13},{... | collective-permute-start | bytes 294920 | tf_op jit(solution)/shard_map/ppermute | solution.py:649
  14.8 0.0 collective-permute-done.1.refs_2_
  14.8 0.9 %collective-permute-done.refs_1_ = f32[4,6,8,128]{3,2,1,0:T(8,128)S(1)} collective-permute-done((f32[4,6,8,128]{3,2,1,0:T(8,128)S(1)}, f32[4,6,8,128]{3,2,1,0:T(8,128)S(1)}, u32[]{:S(2)}, u32[]{:S(2)}) %collective-permute-start) | collective-permute-done | bytes 98336 | tf_op jit(solution)/shard_map/ppermute | solution.py:649
  15.7 0.1 second_halos.1
  15.8 0.1 collective-permute-start.2
  15.9 1.9 %collective-permute-start.3 = (f32[512,128]{1,0:T(8,128)S(1)}, f32[512,128]{1,0:T(8,128)S(1)}, u32[]{:S(2)}, u32[]{:S(2)}) collective-permute-start(f32[512,128]{1,0:T(8,128)S(1)} %get-tuple-element.28), channel_id=1, source_target_pairs={{0,28},{4,8},{8,4},{12,16},{16,12},{20,24},{24,20},{28,0},{1,29},{... | collective-permute-start | bytes 786440 | tf_op jit(solution)/shard_map/ppermute | solution.py:641
  17.8 0.0 copy-done.1
  17.8 0.0 copy-done.2
  17.8 1.0 %stencil_weights.1.refs_1_.refs_2_ = f32[36,5,8,8,128]{4,3,2,1,0:T(8,128)S(1)} custom-call(f32[5,36,128]{2,1,0:T(8,128)S(1)} %copy-done.1, f32[6,36,128]{2,1,0:T(8,128)S(1)} %copy-done.2, f32[8,128]{1,0:T(8,128)S(1)} %get-tuple-element.26.after), custom_call_target="tpu_custom_call" | custom-call | bytes 2000000 | tf_op jit(solution)/shard_map/stencil_weights/pallas_call | solution.py:409
  18.8 0.0 copy-start.3
  18.8 0.0 copy-start.5
  18.8 0.0 copy-start.6
  18.8 0.0 copy-start.7
  18.8 0.0 copy-start.8
  18.8 0.0 collective-permute-done.9.refs_4_.refs_1_
  18.9 7.1 %collective-permute-done.4.refs_3_.refs_0_ = f32[656,128]{1,0:T(8,128)S(1)} collective-permute-done((f32[656,128]{1,0:T(8,128)S(1)}, f32[656,128]{1,0:T(8,128)S(1)}, u32[]{:S(2)}, u32[]{:S(2)}) %collective-permute-start.4) | collective-permute-done | bytes 335904 | tf_op jit(solution)/shard_map/ppermute | solution.py:641
  26.0 0.1 later_halos.3
  26.0 2.7 %collective-permute-start.10 = (f32[648,128]{1,0:T(8,128)S(1)}, f32[648,128]{1,0:T(8,128)S(1)}, u32[]{:S(2)}, u32[]{:S(2)}) collective-permute-start(f32[648,128]{1,0:T(8,128)S(1)} %get-tuple-element.42), channel_id=1, source_target_pairs={{0,4},{4,0},{8,12},{12,8},{16,20},{20,16},{24,28},{28,24},{1,5},{5... | collective-permute-start | bytes 995336 | tf_op jit(solution)/shard_map/ppermute | solution.py:641
  28.7 3.6 %collective-permute-start.11 = (f32[648,128]{1,0:T(8,128)S(1)}, f32[648,128]{1,0:T(8,128)S(1)}, u32[]{:S(2)}, u32[]{:S(2)}) collective-permute-start(f32[648,128]{1,0:T(8,128)S(1)} %get-tuple-element.43), channel_id=1, source_target_pairs={{0,28},{4,8},{8,4},{12,16},{16,12},{20,24},{24,20},{28,0},{1,29},{... | collective-permute-start | bytes 995336 | tf_op jit(solution)/shard_map/ppermute | solution.py:641
  32.3 0.0 collective-permute-start.5
  32.3 5.1 %collective-permute-done.5.refs_8_ = f32[16,128]{1,0:T(8,128)S(1)} collective-permute-done((f32[16,128]{1,0:T(8,128)S(1)}, f32[16,128]{1,0:T(8,128)S(1)}, u32[]{:S(2)}, u32[]{:S(2)}) %collective-permute-start.5) | collective-permute-done | bytes 8224 | tf_op jit(solution)/shard_map/ppermute | solution.py:659
  37.5 1.2 %collective-permute-start.6 = (f32[32,128]{1,0:T(8,128)S(1)}, f32[32,128]{1,0:T(8,128)S(1)}, u32[]{:S(2)}, u32[]{:S(2)}) collective-permute-start(f32[32,128]{1,0:T(8,128)S(1)} %pad_maximum_fusion), channel_id=1, source_target_pairs={{0,16},{4,20},{8,24},{12,28},{16,0},{20,4},{24,8},{28,12},{1,17},{... | collective-permute-start | bytes 49160 | tf_op jit(solution)/shard_map/ppermute | solution.py:659
  39.3 0.0 collective-permute-done.2.refs_1_.refs_0_.refs_3_
  39.3 0.0 collective-permute-done.3.refs_2_.refs_1_.refs_4_
  39.3 0.0 copy-done.3
  39.3 1.1 %move_ghosts.1 = (f32[36,4,5,8,128]{4,3,2,1,0:T(8,128)S(1)}, f32[8,128]{1,0:T(8,128)S(1)}) custom-call(f32[4,6,8,128]{3,2,1,0:T(8,128)S(1)} %get-tuple-element.29.refs_0_, f32[512,128]{1,0:T(8,128)S(1)} %collective-permute-done.2.refs_1_.refs_0_.refs_3_, f32[512,128]{1,0:T(8,128)S(1)} %collective-permute-done.3.refs_2_.refs_1_.refs_4_, ...), custom_call_target="tpu_custom_call" | custom-call | bytes 2000000 | tf_op jit(solution)/shard_map/move_ghosts/pallas_call | solution.py:317
  40.4 1.7 %collective-permute-done.6.refs_9_ = f32[32,128]{1,0:T(8,128)S(1)} collective-permute-done((f32[32,128]{1,0:T(8,128)S(1)}, f32[32,128]{1,0:T(8,128)S(1)}, u32[]{:S(2)}, u32[]{:S(2)}) %collective-permute-start.6) | collective-permute-done | bytes 16416 | tf_op jit(solution)/shard_map/ppermute | solution.py:659
  42.1 0.0 copy-done.5
  42.1 0.0 copy-done.6
  42.1 0.0 copy-done.7
  42.1 0.0 copy-done.8
  42.1 0.2 surface_wind.1
  42.4 0.4 collective-permute-start.7
  42.8 3.6 %collective-permute-start.8 = (f32[216,128]{1,0:T(8,128)S(1)}, f32[216,128]{1,0:T(8,128)S(1)}, u32[]{:S(2)}, u32[]{:S(2)}) collective-permute-start(f32[216,128]{1,0:T(8,128)S(1)} %get-tuple-element.34), channel_id=1, source_target_pairs={{0,28},{4,8},{8,4},{12,16},{16,12},{20,24},{24,20},{28,0},{1,29},{... | collective-permute-start | bytes 331784 | tf_op jit(solution)/shard_map/ppermute | solution.py:641
  46.4 1.1 %chunk.4 = (f32[8,144,128]{2,1,0:T(8,128)S(1)}, f32[4,8,128]{2,1,0:T(8,128)S(1)}) custom-call(f32[5,36,128]{2,1,0:T(8,128)S(1)} %copy-done.1, f32[36,5,8,8,128]{4,3,2,1,0:T(8,128)S(1)} %stencil_weights.1.refs_1_.refs_2_, f32[36,144,128]{2,1,0:T(8,128)S(1)} %bitcast.12, f32[512,128]{1,0:T(8,128)S(1)} %collective-permute-done.2.refs_1_.refs_0_.refs_3_, ...), custom_call_target="tpu_custom_call" | custom-call | bytes 1000000 | tf_op jit(solution)/shard_map/chunk/pallas_call | solution.py:537
  47.4 1.6 %chunk.3 = (f32[12,144,128]{2,1,0:T(8,128)S(1)}, f32[4,8,128]{2,1,0:T(8,128)S(1)}) custom-call(f32[5,36,128]{2,1,0:T(8,128)S(1)} %copy-done.1, f32[36,5,8,8,128]{4,3,2,1,0:T(8,128)S(1)} %stencil_weights.1.refs_1_.refs_2_, f32[36,144,128]{2,1,0:T(8,128)S(1)} %bitcast.13, f32[656,128]{1,0:T(8,128)S(1)} %collective-permute-done.4.refs_3_.refs_0_, ...), custom_call_target="tpu_custom_call" | custom-call | bytes 1000000 | tf_op jit(solution)/shard_map/chunk/pallas_call | solution.py:537
  49.0 0.0 collective-permute-done.10.refs_3_
  49.0 0.0 collective-permute-done.11.refs_4_
  49.1 1.6 %chunk.5 = (f32[12,144,128]{2,1,0:T(8,128)S(1)}, f32[4,8,128]{2,1,0:T(8,128)S(1)}) custom-call(f32[5,36,128]{2,1,0:T(8,128)S(1)} %copy-done.1, f32[36,5,8,8,128]{4,3,2,1,0:T(8,128)S(1)} %stencil_weights.1.refs_1_.refs_2_, f32[36,144,128]{2,1,0:T(8,128)S(1)} %bitcast.14, f32[648,128]{1,0:T(8,128)S(1)} %collective-permute-done.10.refs_3_, ...), custom_call_target="tpu_custom_call" | custom-call | bytes 1000000 | tf_op jit(solution)/shard_map/chunk/pallas_call | solution.py:537
  50.7 0.0 collective-permute-done.7.refs_3_
  50.7 0.0 collective-permute-done.8.refs_4_
  50.7 2.0 %last_chunk.1 = (f32[36,144,128]{2,1,0:T(8,128)}, f32[2,4,128]{2,1,0:T(4,128)}) custom-call(f32[5,36,128]{2,1,0:T(8,128)S(1)} %copy-done.1, f32[36,5,8,8,128]{4,3,2,1,0:T(8,128)S(1)} %stencil_weights.1.refs_1_.refs_2_, f32[36,144,128]{2,1,0:T(8,128)S(1)} %bitcast.15, f32[216,128]{1,0:T(8,128)S(1)} %collective-permute-done.7.refs_3_, ...), custom_call_target="tpu_custom_call" | custom-call | bytes 6000000 | tf_op jit(solution)/shard_map/last_chunk/pallas_call | solution.py:604
  (4 shorter events, 0.0 us)
Async XLA Ops:
  0.6 8.0 %copy-start = (f32[36,36,4,128]{3,2,1,0:T(4,128)S(1)}, f32[36,36,4,128]{3,2,1,0:T(4,128)}, u32[]{:S(2)}) copy-start(f32[36,36,4,128]{3,2,1,0:T(4,128)} %param.11) | copy-start | bytes 7962628
  2.0 15.8 %copy-start.1 = (f32[5,36,128]{2,1,0:T(8,128)S(1)}, f32[5,36,128]{2,1,0:T(8,128)}, u32[]{:S(2)}) copy-start(f32[5,36,128]{2,1,0:T(8,128)} %constant.6.clone.scal.refs_0_) | copy-start | bytes 276484
  2.1 15.7 %copy-start.2 = (f32[6,36,128]{2,1,0:T(8,128)S(1)}, f32[6,36,128]{2,1,0:T(8,128)}, u32[]{:S(2)}) copy-start(f32[6,36,128]{2,1,0:T(8,128)} %constant.7.clone.ang.refs_4_) | copy-start | bytes 331780
  2.1 23.9 %collective-permute-start.4 = (f32[656,128]{1,0:T(8,128)S(1)}, f32[656,128]{1,0:T(8,128)S(1)}, u32[]{:S(2)}, u32[]{:S(2)}) collective-permute-start(f32[656,128]{1,0:T(8,128)S(1)} %get-tuple-element.31), channel_id=1, source_target_pairs={{0,4},{4,0},{8,12},{12,8},{16,20},{20,16},{24,28},{28,24},{1,5},{5... | collective-permute-start | bytes 1007624 | tf_op jit(solution)/shard_map/ppermute | solution.py:641
  5.1 13.8 %collective-permute-start.9 = (f32[648,128]{1,0:T(8,128)S(1)}, f32[648,128]{1,0:T(8,128)S(1)}, u32[]{:S(2)}, u32[]{:S(2)}) collective-permute-start(f32[648,128]{1,0:T(8,128)S(1)} %get-tuple-element.39), channel_id=1, source_target_pairs={{0,28},{4,8},{8,4},{12,16},{16,12},{20,24},{24,20},{28,0},{1,29},{... | collective-permute-start | bytes 995336 | tf_op jit(solution)/shard_map/ppermute | solution.py:641
  8.6 0.7 %copy-start.4 = (s32[4,128]{1,0:T(4,128)S(1)}, s32[4,128]{1,0:T(4,128)}, u32[]{:S(2)}) copy-start(s32[4,128]{1,0:T(4,128)} %refs_5_.1) | copy-start | bytes 6148
  10.4 4.3 %collective-permute-start.1 = (f32[4,6,8,128]{3,2,1,0:T(8,128)S(1)}, f32[4,6,8,128]{3,2,1,0:T(8,128)S(1)}, u32[]{:S(2)}, u32[]{:S(2)}) collective-permute-start(f32[4,6,8,128]{3,2,1,0:T(8,128)S(1)} %pack_edges.1), channel_id=1, source_target_pairs={{1,0},{2,1},{3,2},{5,4},{6,5},{7,6},{9,8},{10,9},{11,10},{13,12},{... | collective-permute-start | bytes 294920 | tf_op jit(solution)/shard_map/ppermute | solution.py:650
  11.8 4.0 %collective-permute-start = (f32[4,6,8,128]{3,2,1,0:T(8,128)S(1)}, f32[4,6,8,128]{3,2,1,0:T(8,128)S(1)}, u32[]{:S(2)}, u32[]{:S(2)}) collective-permute-start(f32[4,6,8,128]{3,2,1,0:T(8,128)S(1)} %pack_edges.1), channel_id=1, source_target_pairs={{0,1},{1,2},{2,3},{4,5},{5,6},{6,7},{8,9},{9,10},{10,11},{12,13},{... | collective-permute-start | bytes 294920 | tf_op jit(solution)/shard_map/ppermute | solution.py:649
  15.8 23.4 %collective-permute-start.2 = (f32[512,128]{1,0:T(8,128)S(1)}, f32[512,128]{1,0:T(8,128)S(1)}, u32[]{:S(2)}, u32[]{:S(2)}) collective-permute-start(f32[512,128]{1,0:T(8,128)S(1)} %get-tuple-element.27), channel_id=1, source_target_pairs={{0,4},{4,0},{8,12},{12,8},{16,20},{20,16},{24,28},{28,24},{1,5},{5... | collective-permute-start | bytes 786440 | tf_op jit(solution)/shard_map/ppermute | solution.py:641
  15.9 23.4 %collective-permute-start.3 = (f32[512,128]{1,0:T(8,128)S(1)}, f32[512,128]{1,0:T(8,128)S(1)}, u32[]{:S(2)}, u32[]{:S(2)}) collective-permute-start(f32[512,128]{1,0:T(8,128)S(1)} %get-tuple-element.28), channel_id=1, source_target_pairs={{0,28},{4,8},{8,4},{12,16},{16,12},{20,24},{24,20},{28,0},{1,29},{... | collective-permute-start | bytes 786440 | tf_op jit(solution)/shard_map/ppermute | solution.py:641
  18.8 20.5 %copy-start.3 = (f32[5,5,8,128]{3,2,1,0:T(8,128)S(1)}, f32[5,5,8,128]{3,2,1,0:T(8,128)}, u32[]{:S(2)}) copy-start(f32[5,5,8,128]{3,2,1,0:T(8,128)} %constant.8.clone.refs_3_) | copy-start | bytes 307204
  18.8 23.3 %copy-start.5 = (s32[4,128]{1,0:T(4,128)S(1)}, s32[4,128]{1,0:T(4,128)}, u32[]{:S(2)}) copy-start(s32[4,128]{1,0:T(4,128)} %refs_5_.1) | copy-start | bytes 6148
  18.8 23.3 %copy-start.6 = (s32[4,4,128]{2,1,0:T(4,128)S(1)}, s32[4,4,128]{2,1,0:T(4,128)}, u32[]{:S(2)}) copy-start(s32[4,4,128]{2,1,0:T(4,128)} %param.17) | copy-start | bytes 24580
  18.8 23.3 %copy-start.7 = (f32[4,4,128]{2,1,0:T(4,128)S(1)}, f32[4,4,128]{2,1,0:T(4,128)}, u32[]{:S(2)}) copy-start(f32[4,4,128]{2,1,0:T(4,128)} %param.18) | copy-start | bytes 24580
  18.8 23.3 %copy-start.8 = (f32[2,4,128]{2,1,0:T(4,128)S(1)}, f32[2,4,128]{2,1,0:T(4,128)}, u32[]{:S(2)}) copy-start(f32[2,4,128]{2,1,0:T(4,128)} %refs_6_.1) | copy-start | bytes 12292
  26.0 23.0 %collective-permute-start.10 = (f32[648,128]{1,0:T(8,128)S(1)}, f32[648,128]{1,0:T(8,128)S(1)}, u32[]{:S(2)}, u32[]{:S(2)}) collective-permute-start(f32[648,128]{1,0:T(8,128)S(1)} %get-tuple-element.42), channel_id=1, source_target_pairs={{0,4},{4,0},{8,12},{12,8},{16,20},{20,16},{24,28},{28,24},{1,5},{5... | collective-permute-start | bytes 995336 | tf_op jit(solution)/shard_map/ppermute | solution.py:641
  28.7 20.3 %collective-permute-start.11 = (f32[648,128]{1,0:T(8,128)S(1)}, f32[648,128]{1,0:T(8,128)S(1)}, u32[]{:S(2)}, u32[]{:S(2)}) collective-permute-start(f32[648,128]{1,0:T(8,128)S(1)} %get-tuple-element.43), channel_id=1, source_target_pairs={{0,28},{4,8},{8,4},{12,16},{16,12},{20,24},{24,20},{28,0},{1,29},{... | collective-permute-start | bytes 995336 | tf_op jit(solution)/shard_map/ppermute | solution.py:641
  32.3 5.1 %collective-permute-start.5 = (f32[16,128]{1,0:T(8,128)S(1)}, f32[16,128]{1,0:T(8,128)S(1)}, u32[]{:S(2)}, u32[]{:S(2)}) collective-permute-start(f32[16,128]{1,0:T(8,128)S(1)} %pad_maximum_fusion.1.refs_7_), channel_id=1, source_target_pairs={{0,8},{4,12},{8,0},{12,4},{16,24},{20,28},{24,16},{28,20},{1,9},{5... | collective-permute-start | bytes 24584 | tf_op jit(solution)/shard_map/ppermute | solution.py:659
  37.5 4.6 %collective-permute-start.6 = (f32[32,128]{1,0:T(8,128)S(1)}, f32[32,128]{1,0:T(8,128)S(1)}, u32[]{:S(2)}, u32[]{:S(2)}) collective-permute-start(f32[32,128]{1,0:T(8,128)S(1)} %pad_maximum_fusion), channel_id=1, source_target_pairs={{0,16},{4,20},{8,24},{12,28},{16,0},{20,4},{24,8},{28,12},{1,17},{... | collective-permute-start | bytes 49160 | tf_op jit(solution)/shard_map/ppermute | solution.py:659
  42.4 8.3 %collective-permute-start.7 = (f32[216,128]{1,0:T(8,128)S(1)}, f32[216,128]{1,0:T(8,128)S(1)}, u32[]{:S(2)}, u32[]{:S(2)}) collective-permute-start(f32[216,128]{1,0:T(8,128)S(1)} %get-tuple-element.33), channel_id=1, source_target_pairs={{0,4},{4,0},{8,12},{12,8},{16,20},{20,16},{24,28},{28,24},{1,5},{5... | collective-permute-start | bytes 331784 | tf_op jit(solution)/shard_map/ppermute | solution.py:641
  42.8 7.9 %collective-permute-start.8 = (f32[216,128]{1,0:T(8,128)S(1)}, f32[216,128]{1,0:T(8,128)S(1)}, u32[]{:S(2)}, u32[]{:S(2)}) collective-permute-start(f32[216,128]{1,0:T(8,128)S(1)} %get-tuple-element.34), channel_id=1, source_target_pairs={{0,28},{4,8},{8,4},{12,16},{16,12},{20,24},{24,20},{28,0},{1,29},{... | collective-permute-start | bytes 331784 | tf_op jit(solution)/shard_map/ppermute | solution.py:641

commit v8 on v7

--- a/solution.py
+++ b/solution.py
@@ -33,7 +33,7 @@
 CHUNKS = (12, 8, 12, 4)
 GROUPS = -(-FREQS // PACK)
 PIECE = 4
-EDGE_ROWS = 2 * (-(-FREQS // PACK)) * 8
+EDGE_ROWS = (2 * (-(-FREQS // PACK)) - 1) * 8
 VMEM = 32 * 1024 * 1024
 FIRST_VMEM = 63000000
 
@@ -194,6 +194,10 @@
     return edge
 
 
+def edge_slot(n, g, joined):
+    return 2 * (GROUPS - 1) if joined else n * (GROUPS - 1) + g
+
+
 def edge_shift(r, b):
     return (r * SPAN + OFFSETS[b] + 2 - EDGES[b]) % LANES
 
@@ -241,17 +245,25 @@
     pick = edge_ids() < 2
     even = is_even()
 
-    def body(g, _):
+    def group(g, joined):
         both = [jnp.where(pick, south[c, g], north[c, g]) for c in range(CELLS)]
         for c in range(CELLS):
             merged[c, g] = both[c]
-        for n in range(2):
-            row = pl.ds(pl.multiple_of(count * HALO + (n * GROUPS + g) * 8, 8), 8)
-            one[row, :] = jnp.where(even, both[2 + n], both[n])
-            two[row, :] = jnp.where(even, both[n], both[2 + n])
+        east, west = both[2:], both[:2]
+        if joined:
+            half = lane_ids() < LANES // 2
+            east, west = ([jnp.where(half, a, pltpu.roll(b, LANES // 2, 1))] for a, b in (east, west))
+        for n, (e, w) in enumerate(zip(east, west)):
+            row = pl.ds(pl.multiple_of(count * HALO + edge_slot(n, g, joined) * 8, 8), 8)
+            one[row, :] = jnp.where(even, e, w)
+            two[row, :] = jnp.where(even, w, e)
+
+    def body(g, _):
+        group(g, False)
         return 0
 
-    lax.fori_loop(0, GROUPS, body, 0)
+    lax.fori_loop(0, GROUPS - 1, body, 0)
+    group(GROUPS - 1, True)
     for c in range(CELLS):
         merged[c, GROUPS] = jnp.where(pick, south[c, GROUPS], north[c, GROUPS])
     halo_rows(x, start, one, two, 0, count)
@@ -289,12 +301,15 @@
     even = is_even()
     token[...] = jnp.zeros_like(token)
 
-    def spread(g, freqs):
+    def spread(g, freqs, joined):
         rows = [
-            pl.ds(pl.multiple_of(count * HALO + (n * GROUPS + g) * 8, 8), 8) for n in range(2)
+            pl.ds(pl.multiple_of(count * HALO + edge_slot(n, g, joined) * 8, 8), 8)
+            for n in range(1 if joined else 2)
         ]
         west = [jnp.where(even, two[row, :], one[row, :]) for row in rows]
         east = [jnp.where(even, one[row, :], two[row, :]) for row in rows]
+        if joined:
+            west, east = ([a, pltpu.roll(a, LANES // 2, 1)] for (a,) in (west, east))
         ext = west + [merged[c, g] for c in range(CELLS)] + east
         for c in range(CELLS):
             total = weights[0, g] * ext[c]
@@ -306,11 +321,11 @@
                     ghosts[g * PACK + r, c, b] = pltpu.roll(total, (LANES - edge_shift(r, b)) % LANES, 1)
 
     def body(g, _):
-        spread(g, PACK)
+        spread(g, PACK, False)
         return 0
 
     lax.fori_loop(0, FREQS // PACK, body, 0)
-    spread(GROUPS - 1, FREQS - (GROUPS - 1) * PACK)
+    spread(GROUPS - 1, FREQS - (GROUPS - 1) * PACK, True)
 
 
 def move_ghosts(count, merged, one, two):

time: 52.9 us -> 52.7 us (level)
  no operation moved by 1% of the time
where the time goes in v8:
time: 52.7 us; the launch traced here: 52.5 us
  starting transfers between devices  24.2 us (46%)
  waiting for transfers between devices  14.7 us (28%)
  Pallas kernels  11.4 us (22%)
  between operations  1.54 us (3%)
  local copies, waits for them, and re-layouts  0.73 us (1%)
    ppermute x4, starting transfers between devices, exchange(): lax.ppermute(two, 'lon', swap_two)  12.6 us
    ppermute x4, waiting for transfers between devices, exchange(): lax.ppermute(one, 'lon', swap_one)  6.96 us
    ppermute x2, waiting for transfers between devices, local(): lax.ppermute(held, 'lon', [(i, i ^ step) for i in range(tiles)])  6.8 us
    ppermute x4, starting transfers between devices, exchange(): lax.ppermute(one, 'lon', swap_one)  6.16 us
    pallas_call x3, Pallas kernels, main_chunk(): pl.pallas_call(lambda *refs: main_body(first, count, *refs), out_shape=(p...  4.23 us
    ppermute x1, starting transfers between devices, local(): south = lax.ppermute(q, 'lat', north_way)  3.04 us
    pallas_call x1, Pallas kernels, tail_chunk(): pl.pallas_call(lambda *refs: tail_body(sizes, *refs), out_shape=(jax.Shap...  2.03 us
    pallas_call x1, Pallas kernels, first_halos(): pl.pallas_call(lambda *refs: first_body(count, *refs), out_shape=(message...  1.39 us
  transfers between devices with their start and end apart: 12, of which 4 were waited for; matrix products, arithmetic and copies ran while one was open for 0% of the time, Pallas kernels for 15%

profile of v8, /device:TPU:0, one launch (start us, length us, event | category | flops | bytes accessed | tf_op | source)
XLA Modules:
  0.0 52.5 jit_solution(17998650837242449275)
XLA Ops:
  0.6 0.0 copy-start
  0.6 1.4 %first_halos.1 = (f32[656,128]{1,0:T(8,128)S(1)}, f32[648,128]{1,0:T(8,128)S(1)}, f32[8,128]{1,0:T(8,128)S(1)}) custom-call(f32[36,144,128]{2,1,0:T(8,128)} %bitcast.7, f32[4,128]{1,0:T(4,128)} %bitcast.18, s32[1,192]{1,0:T(1,128)} %refs_2_.1), custom_call_target="tpu_custom_call" | custom-call | bytes 2000000 | tf_op jit(solution)/shard_map/first_halos/pallas_call | solution.py:171
  2.0 0.0 copy-start.1
  2.1 0.0 copy-start.2
  2.1 3.0 %collective-permute-start.4 = (f32[656,128]{1,0:T(8,128)S(1)}, f32[656,128]{1,0:T(8,128)S(1)}, u32[]{:S(2)}, u32[]{:S(2)}) collective-permute-start(f32[656,128]{1,0:T(8,128)S(1)} %get-tuple-element.31), channel_id=1, source_target_pairs={{0,4},{4,0},{8,12},{12,8},{16,20},{20,16},{24,28},{28,24},{1,5},{5... | collective-permute-start | bytes 1007624 | tf_op jit(solution)/shard_map/ppermute | solution.py:656
  5.1 3.5 %collective-permute-start.9 = (f32[648,128]{1,0:T(8,128)S(1)}, f32[648,128]{1,0:T(8,128)S(1)}, u32[]{:S(2)}, u32[]{:S(2)}) collective-permute-start(f32[648,128]{1,0:T(8,128)S(1)} %get-tuple-element.39), channel_id=1, source_target_pairs={{0,28},{4,8},{8,4},{12,16},{16,12},{20,24},{24,20},{28,0},{1,29},{... | collective-permute-start | bytes 995336 | tf_op jit(solution)/shard_map/ppermute | solution.py:656
  8.6 0.0 copy-done
  8.6 0.0 copy-start.4
  8.6 0.7 %copy-done.4 = s32[4,128]{1,0:T(4,128)S(1)} copy-done((s32[4,128]{1,0:T(4,128)S(1)}, s32[4,128]{1,0:T(4,128)}, u32[]{:S(2)}) %copy-start.4) | copy-done | bytes 2072
  9.3 1.1 %pack_edges.1 = f32[4,6,8,128]{3,2,1,0:T(8,128)S(1)} custom-call(f32[36,144,128]{2,1,0:T(8,128)S(1)} %bitcast.8, s32[4,128]{1,0:T(4,128)S(1)} %copy-done.4, f32[8,128]{1,0:T(8,128)S(1)} %get-tuple-element.26.after), custom_call_target="tpu_custom_call" | custom-call | bytes 4000000 | tf_op jit(solution)/shard_map/pack_edges/pallas_call | solution.py:233
  10.4 1.3 %collective-permute-start.1 = (f32[4,6,8,128]{3,2,1,0:T(8,128)S(1)}, f32[4,6,8,128]{3,2,1,0:T(8,128)S(1)}, u32[]{:S(2)}, u32[]{:S(2)}) collective-permute-start(f32[4,6,8,128]{3,2,1,0:T(8,128)S(1)} %pack_edges.1), channel_id=1, source_target_pairs={{1,0},{2,1},{3,2},{5,4},{6,5},{7,6},{9,8},{10,9},{11,10},{13,12},{... | collective-permute-start | bytes 294920 | tf_op jit(solution)/shard_map/ppermute | solution.py:665
  11.8 3.0 %collective-permute-start = (f32[4,6,8,128]{3,2,1,0:T(8,128)S(1)}, f32[4,6,8,128]{3,2,1,0:T(8,128)S(1)}, u32[]{:S(2)}, u32[]{:S(2)}) collective-permute-start(f32[4,6,8,128]{3,2,1,0:T(8,128)S(1)} %pack_edges.1), channel_id=1, source_target_pairs={{0,1},{1,2},{2,3},{4,5},{5,6},{6,7},{8,9},{9,10},{10,11},{12,13},{... | collective-permute-start | bytes 294920 | tf_op jit(solution)/shard_map/ppermute | solution.py:664
  14.8 0.0 collective-permute-done.1.refs_2_
  14.8 0.9 %collective-permute-done.refs_1_ = f32[4,6,8,128]{3,2,1,0:T(8,128)S(1)} collective-permute-done((f32[4,6,8,128]{3,2,1,0:T(8,128)S(1)}, f32[4,6,8,128]{3,2,1,0:T(8,128)S(1)}, u32[]{:S(2)}, u32[]{:S(2)}) %collective-permute-start) | collective-permute-done | bytes 98336 | tf_op jit(solution)/shard_map/ppermute | solution.py:664
  15.7 0.2 second_halos.1
  15.9 0.1 collective-permute-start.2
  16.0 1.9 %collective-permute-start.3 = (f32[504,128]{1,0:T(8,128)S(1)}, f32[504,128]{1,0:T(8,128)S(1)}, u32[]{:S(2)}, u32[]{:S(2)}) collective-permute-start(f32[504,128]{1,0:T(8,128)S(1)} %get-tuple-element.28), channel_id=1, source_target_pairs={{0,28},{4,8},{8,4},{12,16},{16,12},{20,24},{24,20},{28,0},{1,29},{... | collective-permute-start | bytes 774152 | tf_op jit(solution)/shard_map/ppermute | solution.py:656
  17.9 0.0 copy-done.1
  17.9 0.0 copy-done.2
  17.9 1.0 %stencil_weights.1.refs_1_.refs_2_ = f32[36,5,8,8,128]{4,3,2,1,0:T(8,128)S(1)} custom-call(f32[5,36,128]{2,1,0:T(8,128)S(1)} %copy-done.1, f32[6,36,128]{2,1,0:T(8,128)S(1)} %copy-done.2, f32[8,128]{1,0:T(8,128)S(1)} %get-tuple-element.26.after), custom_call_target="tpu_custom_call" | custom-call | bytes 2000000 | tf_op jit(solution)/shard_map/stencil_weights/pallas_call | solution.py:424
  18.8 0.0 copy-start.3
  18.9 0.0 copy-start.5
  18.9 0.0 copy-start.6
  18.9 0.0 copy-start.7
  18.9 0.0 copy-start.8
  18.9 0.0 collective-permute-done.9.refs_4_.refs_1_
  18.9 7.0 %collective-permute-done.4.refs_3_.refs_0_ = f32[656,128]{1,0:T(8,128)S(1)} collective-permute-done((f32[656,128]{1,0:T(8,128)S(1)}, f32[656,128]{1,0:T(8,128)S(1)}, u32[]{:S(2)}, u32[]{:S(2)}) %collective-permute-start.4) | collective-permute-done | bytes 335904 | tf_op jit(solution)/shard_map/ppermute | solution.py:656
  25.9 0.1 later_halos.3
  26.0 2.7 %collective-permute-start.10 = (f32[648,128]{1,0:T(8,128)S(1)}, f32[648,128]{1,0:T(8,128)S(1)}, u32[]{:S(2)}, u32[]{:S(2)}) collective-permute-start(f32[648,128]{1,0:T(8,128)S(1)} %get-tuple-element.42), channel_id=1, source_target_pairs={{0,4},{4,0},{8,12},{12,8},{16,20},{20,16},{24,28},{28,24},{1,5},{5... | collective-permute-start | bytes 995336 | tf_op jit(solution)/shard_map/ppermute | solution.py:656
  28.6 3.6 %collective-permute-start.11 = (f32[648,128]{1,0:T(8,128)S(1)}, f32[648,128]{1,0:T(8,128)S(1)}, u32[]{:S(2)}, u32[]{:S(2)}) collective-permute-start(f32[648,128]{1,0:T(8,128)S(1)} %get-tuple-element.43), channel_id=1, source_target_pairs={{0,28},{4,8},{8,4},{12,16},{16,12},{20,24},{24,20},{28,0},{1,29},{... | collective-permute-start | bytes 995336 | tf_op jit(solution)/shard_map/ppermute | solution.py:656
  32.2 0.0 collective-permute-start.5
  32.2 5.1 %collective-permute-done.5.refs_8_ = f32[16,128]{1,0:T(8,128)S(1)} collective-permute-done((f32[16,128]{1,0:T(8,128)S(1)}, f32[16,128]{1,0:T(8,128)S(1)}, u32[]{:S(2)}, u32[]{:S(2)}) %collective-permute-start.5) | collective-permute-done | bytes 8224 | tf_op jit(solution)/shard_map/ppermute | solution.py:674
  37.4 1.2 %collective-permute-start.6 = (f32[32,128]{1,0:T(8,128)S(1)}, f32[32,128]{1,0:T(8,128)S(1)}, u32[]{:S(2)}, u32[]{:S(2)}) collective-permute-start(f32[32,128]{1,0:T(8,128)S(1)} %pad_maximum_fusion), channel_id=1, source_target_pairs={{0,16},{4,20},{8,24},{12,28},{16,0},{20,4},{24,8},{28,12},{1,17},{... | collective-permute-start | bytes 49160 | tf_op jit(solution)/shard_map/ppermute | solution.py:674
  39.2 0.0 collective-permute-done.2.refs_1_.refs_0_.refs_3_
  39.2 0.0 collective-permute-done.3.refs_2_.refs_1_.refs_4_
  39.2 0.0 copy-done.3
  39.2 1.1 %move_ghosts.1 = (f32[36,4,5,8,128]{4,3,2,1,0:T(8,128)S(1)}, f32[8,128]{1,0:T(8,128)S(1)}) custom-call(f32[4,6,8,128]{3,2,1,0:T(8,128)S(1)} %get-tuple-element.29.refs_0_, f32[504,128]{1,0:T(8,128)S(1)} %collective-permute-done.2.refs_1_.refs_0_.refs_3_, f32[504,128]{1,0:T(8,128)S(1)} %collective-permute-done.3.refs_2_.refs_1_.refs_4_, ...), custom_call_target="tpu_custom_call" | custom-call | bytes 2000000 | tf_op jit(solution)/shard_map/move_ghosts/pallas_call | solution.py:332
  40.3 1.7 %collective-permute-done.6.refs_9_ = f32[32,128]{1,0:T(8,128)S(1)} collective-permute-done((f32[32,128]{1,0:T(8,128)S(1)}, f32[32,128]{1,0:T(8,128)S(1)}, u32[]{:S(2)}, u32[]{:S(2)}) %collective-permute-start.6) | collective-permute-done | bytes 16416 | tf_op jit(solution)/shard_map/ppermute | solution.py:674
  42.0 0.0 copy-done.5
  42.0 0.0 copy-done.6
  42.0 0.0 copy-done.7
  42.0 0.0 copy-done.8
  42.0 0.2 surface_wind.1
  42.3 0.4 collective-permute-start.7
  42.7 3.6 %collective-permute-start.8 = (f32[216,128]{1,0:T(8,128)S(1)}, f32[216,128]{1,0:T(8,128)S(1)}, u32[]{:S(2)}, u32[]{:S(2)}) collective-permute-start(f32[216,128]{1,0:T(8,128)S(1)} %get-tuple-element.34), channel_id=1, source_target_pairs={{0,28},{4,8},{8,4},{12,16},{16,12},{20,24},{24,20},{28,0},{1,29},{... | collective-permute-start | bytes 331784 | tf_op jit(solution)/shard_map/ppermute | solution.py:656
  46.2 1.1 %chunk.4 = (f32[8,144,128]{2,1,0:T(8,128)S(1)}, f32[4,8,128]{2,1,0:T(8,128)S(1)}) custom-call(f32[5,36,128]{2,1,0:T(8,128)S(1)} %copy-done.1, f32[36,5,8,8,128]{4,3,2,1,0:T(8,128)S(1)} %stencil_weights.1.refs_1_.refs_2_, f32[36,144,128]{2,1,0:T(8,128)S(1)} %bitcast.12, f32[504,128]{1,0:T(8,128)S(1)} %collective-permute-done.2.refs_1_.refs_0_.refs_3_, ...), custom_call_target="tpu_custom_call" | custom-call | bytes 1000000 | tf_op jit(solution)/shard_map/chunk/pallas_call | solution.py:552
  47.3 1.6 %chunk.3 = (f32[12,144,128]{2,1,0:T(8,128)S(1)}, f32[4,8,128]{2,1,0:T(8,128)S(1)}) custom-call(f32[5,36,128]{2,1,0:T(8,128)S(1)} %copy-done.1, f32[36,5,8,8,128]{4,3,2,1,0:T(8,128)S(1)} %stencil_weights.1.refs_1_.refs_2_, f32[36,144,128]{2,1,0:T(8,128)S(1)} %bitcast.13, f32[656,128]{1,0:T(8,128)S(1)} %collective-permute-done.4.refs_3_.refs_0_, ...), custom_call_target="tpu_custom_call" | custom-call | bytes 1000000 | tf_op jit(solution)/shard_map/chunk/pallas_call | solution.py:552
  48.9 0.0 collective-permute-done.10.refs_3_
  48.9 0.0 collective-permute-done.11.refs_4_
  48.9 1.6 %chunk.5 = (f32[12,144,128]{2,1,0:T(8,128)S(1)}, f32[4,8,128]{2,1,0:T(8,128)S(1)}) custom-call(f32[5,36,128]{2,1,0:T(8,128)S(1)} %copy-done.1, f32[36,5,8,8,128]{4,3,2,1,0:T(8,128)S(1)} %stencil_weights.1.refs_1_.refs_2_, f32[36,144,128]{2,1,0:T(8,128)S(1)} %bitcast.14, f32[648,128]{1,0:T(8,128)S(1)} %collective-permute-done.10.refs_3_, ...), custom_call_target="tpu_custom_call" | custom-call | bytes 1000000 | tf_op jit(solution)/shard_map/chunk/pallas_call | solution.py:552
  50.5 0.0 collective-permute-done.7.refs_3_
  50.5 0.0 collective-permute-done.8.refs_4_
  50.5 2.0 %last_chunk.1 = (f32[36,144,128]{2,1,0:T(8,128)}, f32[2,4,128]{2,1,0:T(4,128)}) custom-call(f32[5,36,128]{2,1,0:T(8,128)S(1)} %copy-done.1, f32[36,5,8,8,128]{4,3,2,1,0:T(8,128)S(1)} %stencil_weights.1.refs_1_.refs_2_, f32[36,144,128]{2,1,0:T(8,128)S(1)} %bitcast.15, f32[216,128]{1,0:T(8,128)S(1)} %collective-permute-done.7.refs_3_, ...), custom_call_target="tpu_custom_call" | custom-call | bytes 6000000 | tf_op jit(solution)/shard_map/last_chunk/pallas_call | solution.py:619
  (4 shorter events, 0.0 us)
Async XLA Ops:
  0.6 8.0 %copy-start = (f32[36,36,4,128]{3,2,1,0:T(4,128)S(1)}, f32[36,36,4,128]{3,2,1,0:T(4,128)}, u32[]{:S(2)}) copy-start(f32[36,36,4,128]{3,2,1,0:T(4,128)} %param.11) | copy-start | bytes 7962628
  2.0 15.8 %copy-start.1 = (f32[5,36,128]{2,1,0:T(8,128)S(1)}, f32[5,36,128]{2,1,0:T(8,128)}, u32[]{:S(2)}) copy-start(f32[5,36,128]{2,1,0:T(8,128)} %constant.6.clone.scal.refs_0_) | copy-start | bytes 276484
  2.1 15.8 %copy-start.2 = (f32[6,36,128]{2,1,0:T(8,128)S(1)}, f32[6,36,128]{2,1,0:T(8,128)}, u32[]{:S(2)}) copy-start(f32[6,36,128]{2,1,0:T(8,128)} %constant.7.clone.ang.refs_4_) | copy-start | bytes 331780
  2.1 23.8 %collective-permute-start.4 = (f32[656,128]{1,0:T(8,128)S(1)}, f32[656,128]{1,0:T(8,128)S(1)}, u32[]{:S(2)}, u32[]{:S(2)}) collective-permute-start(f32[656,128]{1,0:T(8,128)S(1)} %get-tuple-element.31), channel_id=1, source_target_pairs={{0,4},{4,0},{8,12},{12,8},{16,20},{20,16},{24,28},{28,24},{1,5},{5... | collective-permute-start | bytes 1007624 | tf_op jit(solution)/shard_map/ppermute | solution.py:656
  5.1 13.8 %collective-permute-start.9 = (f32[648,128]{1,0:T(8,128)S(1)}, f32[648,128]{1,0:T(8,128)S(1)}, u32[]{:S(2)}, u32[]{:S(2)}) collective-permute-start(f32[648,128]{1,0:T(8,128)S(1)} %get-tuple-element.39), channel_id=1, source_target_pairs={{0,28},{4,8},{8,4},{12,16},{16,12},{20,24},{24,20},{28,0},{1,29},{... | collective-permute-start | bytes 995336 | tf_op jit(solution)/shard_map/ppermute | solution.py:656
  8.6 0.7 %copy-start.4 = (s32[4,128]{1,0:T(4,128)S(1)}, s32[4,128]{1,0:T(4,128)}, u32[]{:S(2)}) copy-start(s32[4,128]{1,0:T(4,128)} %refs_5_.1) | copy-start | bytes 6148
  10.4 4.3 %collective-permute-start.1 = (f32[4,6,8,128]{3,2,1,0:T(8,128)S(1)}, f32[4,6,8,128]{3,2,1,0:T(8,128)S(1)}, u32[]{:S(2)}, u32[]{:S(2)}) collective-permute-start(f32[4,6,8,128]{3,2,1,0:T(8,128)S(1)} %pack_edges.1), channel_id=1, source_target_pairs={{1,0},{2,1},{3,2},{5,4},{6,5},{7,6},{9,8},{10,9},{11,10},{13,12},{... | collective-permute-start | bytes 294920 | tf_op jit(solution)/shard_map/ppermute | solution.py:665
  11.8 4.0 %collective-permute-start = (f32[4,6,8,128]{3,2,1,0:T(8,128)S(1)}, f32[4,6,8,128]{3,2,1,0:T(8,128)S(1)}, u32[]{:S(2)}, u32[]{:S(2)}) collective-permute-start(f32[4,6,8,128]{3,2,1,0:T(8,128)S(1)} %pack_edges.1), channel_id=1, source_target_pairs={{0,1},{1,2},{2,3},{4,5},{5,6},{6,7},{8,9},{9,10},{10,11},{12,13},{... | collective-permute-start | bytes 294920 | tf_op jit(solution)/shard_map/ppermute | solution.py:664
  15.9 23.3 %collective-permute-start.2 = (f32[504,128]{1,0:T(8,128)S(1)}, f32[504,128]{1,0:T(8,128)S(1)}, u32[]{:S(2)}, u32[]{:S(2)}) collective-permute-start(f32[504,128]{1,0:T(8,128)S(1)} %get-tuple-element.27), channel_id=1, source_target_pairs={{0,4},{4,0},{8,12},{12,8},{16,20},{20,16},{24,28},{28,24},{1,5},{5... | collective-permute-start | bytes 774152 | tf_op jit(solution)/shard_map/ppermute | solution.py:656
  16.0 23.2 %collective-permute-start.3 = (f32[504,128]{1,0:T(8,128)S(1)}, f32[504,128]{1,0:T(8,128)S(1)}, u32[]{:S(2)}, u32[]{:S(2)}) collective-permute-start(f32[504,128]{1,0:T(8,128)S(1)} %get-tuple-element.28), channel_id=1, source_target_pairs={{0,28},{4,8},{8,4},{12,16},{16,12},{20,24},{24,20},{28,0},{1,29},{... | collective-permute-start | bytes 774152 | tf_op jit(solution)/shard_map/ppermute | solution.py:656
  18.8 20.3 %copy-start.3 = (f32[5,5,8,128]{3,2,1,0:T(8,128)S(1)}, f32[5,5,8,128]{3,2,1,0:T(8,128)}, u32[]{:S(2)}) copy-start(f32[5,5,8,128]{3,2,1,0:T(8,128)} %constant.8.clone.refs_3_) | copy-start | bytes 307204
  18.9 23.1 %copy-start.5 = (s32[4,128]{1,0:T(4,128)S(1)}, s32[4,128]{1,0:T(4,128)}, u32[]{:S(2)}) copy-start(s32[4,128]{1,0:T(4,128)} %refs_5_.1) | copy-start | bytes 6148
  18.9 23.1 %copy-start.6 = (s32[4,4,128]{2,1,0:T(4,128)S(1)}, s32[4,4,128]{2,1,0:T(4,128)}, u32[]{:S(2)}) copy-start(s32[4,4,128]{2,1,0:T(4,128)} %param.17) | copy-start | bytes 24580
  18.9 23.1 %copy-start.7 = (f32[4,4,128]{2,1,0:T(4,128)S(1)}, f32[4,4,128]{2,1,0:T(4,128)}, u32[]{:S(2)}) copy-start(f32[4,4,128]{2,1,0:T(4,128)} %param.18) | copy-start | bytes 24580
  18.9 23.1 %copy-start.8 = (f32[2,4,128]{2,1,0:T(4,128)S(1)}, f32[2,4,128]{2,1,0:T(4,128)}, u32[]{:S(2)}) copy-start(f32[2,4,128]{2,1,0:T(4,128)} %refs_6_.1) | copy-start | bytes 12292
  26.0 22.9 %collective-permute-start.10 = (f32[648,128]{1,0:T(8,128)S(1)}, f32[648,128]{1,0:T(8,128)S(1)}, u32[]{:S(2)}, u32[]{:S(2)}) collective-permute-start(f32[648,128]{1,0:T(8,128)S(1)} %get-tuple-element.42), channel_id=1, source_target_pairs={{0,4},{4,0},{8,12},{12,8},{16,20},{20,16},{24,28},{28,24},{1,5},{5... | collective-permute-start | bytes 995336 | tf_op jit(solution)/shard_map/ppermute | solution.py:656
  28.6 20.2 %collective-permute-start.11 = (f32[648,128]{1,0:T(8,128)S(1)}, f32[648,128]{1,0:T(8,128)S(1)}, u32[]{:S(2)}, u32[]{:S(2)}) collective-permute-start(f32[648,128]{1,0:T(8,128)S(1)} %get-tuple-element.43), channel_id=1, source_target_pairs={{0,28},{4,8},{8,4},{12,16},{16,12},{20,24},{24,20},{28,0},{1,29},{... | collective-permute-start | bytes 995336 | tf_op jit(solution)/shard_map/ppermute | solution.py:656
  32.2 5.1 %collective-permute-start.5 = (f32[16,128]{1,0:T(8,128)S(1)}, f32[16,128]{1,0:T(8,128)S(1)}, u32[]{:S(2)}, u32[]{:S(2)}) collective-permute-start(f32[16,128]{1,0:T(8,128)S(1)} %pad_maximum_fusion.1.refs_7_), channel_id=1, source_target_pairs={{0,8},{4,12},{8,0},{12,4},{16,24},{20,28},{24,16},{28,20},{1,9},{5... | collective-permute-start | bytes 24584 | tf_op jit(solution)/shard_map/ppermute | solution.py:674
  37.4 4.6 %collective-permute-start.6 = (f32[32,128]{1,0:T(8,128)S(1)}, f32[32,128]{1,0:T(8,128)S(1)}, u32[]{:S(2)}, u32[]{:S(2)}) collective-permute-start(f32[32,128]{1,0:T(8,128)S(1)} %pad_maximum_fusion), channel_id=1, source_target_pairs={{0,16},{4,20},{8,24},{12,28},{16,0},{20,4},{24,8},{28,12},{1,17},{... | collective-permute-start | bytes 49160 | tf_op jit(solution)/shard_map/ppermute | solution.py:674
  42.3 8.2 %collective-permute-start.7 = (f32[216,128]{1,0:T(8,128)S(1)}, f32[216,128]{1,0:T(8,128)S(1)}, u32[]{:S(2)}, u32[]{:S(2)}) collective-permute-start(f32[216,128]{1,0:T(8,128)S(1)} %get-tuple-element.33), channel_id=1, source_target_pairs={{0,4},{4,0},{8,12},{12,8},{16,20},{20,16},{24,28},{28,24},{1,5},{5... | collective-permute-start | bytes 331784 | tf_op jit(solution)/shard_map/ppermute | solution.py:656
  42.7 7.8 %collective-permute-start.8 = (f32[216,128]{1,0:T(8,128)S(1)}, f32[216,128]{1,0:T(8,128)S(1)}, u32[]{:S(2)}, u32[]{:S(2)}) collective-permute-start(f32[216,128]{1,0:T(8,128)S(1)} %get-tuple-element.34), channel_id=1, source_target_pairs={{0,28},{4,8},{8,4},{12,16},{16,12},{20,24},{24,20},{28,0},{1,29},{... | collective-permute-start | bytes 331784 | tf_op jit(solution)/shard_map/ppermute | solution.py:656

commit v9 on v8

--- a/solution.py
+++ b/solution.py
@@ -143,13 +143,17 @@
         pltpu.make_async_copy(wind_hbm, wind, small.at[0]),
         pltpu.make_async_copy(cells_hbm, cells, small.at[1]),
     ]
-    for copy in few:
-        copy.start()
     copies = []
     for n in range(count // GROUP):
         span = pl.ds(n * GROUP, GROUP)
         copies.append(pltpu.make_async_copy(x_hbm.at[span], x.at[span], sem.at[n]))
         copies[-1].start()
+        if n == 0:
+            for copy in few:
+                copy.start()
+    for n in range(count // GROUP - 1):
+        copies[n].wait()
+        halo_rows(x, 0, one, two, n * GROUP, (n + 1) * GROUP)
     for copy in few:
         copy.wait()
     width = cells.shape[1]
@@ -158,9 +162,8 @@
     listed = jnp.take_along_axis(table, index, axis=1)
     packed[...] = listed
     one[pl.ds(count * HALO, 8), :] = listed
-    for n in range(count // GROUP):
-        copies[n].wait()
-        halo_rows(x, 0, one, two, n * GROUP, (n + 1) * GROUP)
+    copies[-1].wait()
+    halo_rows(x, 0, one, two, count - GROUP, count)
 
 
 def message(count, extra=0):

time: 52.7 us -> 52.8 us (level)
  no operation moved by 1% of the time
where the time goes in v9:
time: 52.8 us; the launch traced here: 52.6 us
  starting transfers between devices  24.2 us (46%)
  waiting for transfers between devices  14.7 us (28%)
  Pallas kernels  11.4 us (22%)
  between operations  1.54 us (3%)
  local copies, waits for them, and re-layouts  0.73 us (1%)
    ppermute x4, starting transfers between devices, exchange(): lax.ppermute(two, 'lon', swap_two)  12.6 us
    ppermute x4, waiting for transfers between devices, exchange(): lax.ppermute(one, 'lon', swap_one)  6.96 us
    ppermute x2, waiting for transfers between devices, local(): lax.ppermute(held, 'lon', [(i, i ^ step) for i in range(tiles)])  6.8 us
    ppermute x4, starting transfers between devices, exchange(): lax.ppermute(one, 'lon', swap_one)  6.16 us
    pallas_call x3, Pallas kernels, main_chunk(): pl.pallas_call(lambda *refs: main_body(first, count, *refs), out_shape=(p...  4.23 us
    ppermute x1, starting transfers between devices, local(): south = lax.ppermute(q, 'lat', north_way)  3.04 us
    pallas_call x1, Pallas kernels, tail_chunk(): pl.pallas_call(lambda *refs: tail_body(sizes, *refs), out_shape=(jax.Shap...  2.03 us
    pallas_call x1, Pallas kernels, first_halos(): pl.pallas_call(lambda *refs: first_body(count, *refs), out_shape=(message...  1.46 us
  transfers between devices with their start and end apart: 12, of which 4 were waited for; matrix products, arithmetic and copies ran while one was open for 0% of the time, Pallas kernels for 15%

profile of v9, /device:TPU:0, one launch (start us, length us, event | category | flops | bytes accessed | tf_op | source)
XLA Modules:
  0.0 52.6 jit_solution(8773140695970365652)
XLA Ops:
  0.6 0.0 copy-start
  0.6 1.5 %first_halos.1 = (f32[656,128]{1,0:T(8,128)S(1)}, f32[648,128]{1,0:T(8,128)S(1)}, f32[8,128]{1,0:T(8,128)S(1)}) custom-call(f32[36,144,128]{2,1,0:T(8,128)} %bitcast.7, f32[4,128]{1,0:T(4,128)} %bitcast.18, s32[1,192]{1,0:T(1,128)} %refs_2_.1), custom_call_target="tpu_custom_call" | custom-call | bytes 2000000 | tf_op jit(solution)/shard_map/first_halos/pallas_call | solution.py:174
  2.1 0.0 copy-start.1
  2.1 0.0 copy-start.2
  2.1 3.0 %collective-permute-start.4 = (f32[656,128]{1,0:T(8,128)S(1)}, f32[656,128]{1,0:T(8,128)S(1)}, u32[]{:S(2)}, u32[]{:S(2)}) collective-permute-start(f32[656,128]{1,0:T(8,128)S(1)} %get-tuple-element.31), channel_id=1, source_target_pairs={{0,4},{4,0},{8,12},{12,8},{16,20},{20,16},{24,28},{28,24},{1,5},{5... | collective-permute-start | bytes 1007624 | tf_op jit(solution)/shard_map/ppermute | solution.py:659
  5.2 3.5 %collective-permute-start.9 = (f32[648,128]{1,0:T(8,128)S(1)}, f32[648,128]{1,0:T(8,128)S(1)}, u32[]{:S(2)}, u32[]{:S(2)}) collective-permute-start(f32[648,128]{1,0:T(8,128)S(1)} %get-tuple-element.39), channel_id=1, source_target_pairs={{0,28},{4,8},{8,4},{12,16},{16,12},{20,24},{24,20},{28,0},{1,29},{... | collective-permute-start | bytes 995336 | tf_op jit(solution)/shard_map/ppermute | solution.py:659
  8.7 0.0 copy-done
  8.7 0.0 copy-start.4
  8.7 0.7 %copy-done.4 = s32[4,128]{1,0:T(4,128)S(1)} copy-done((s32[4,128]{1,0:T(4,128)S(1)}, s32[4,128]{1,0:T(4,128)}, u32[]{:S(2)}) %copy-start.4) | copy-done | bytes 2072
  9.4 1.1 %pack_edges.1 = f32[4,6,8,128]{3,2,1,0:T(8,128)S(1)} custom-call(f32[36,144,128]{2,1,0:T(8,128)S(1)} %bitcast.8, s32[4,128]{1,0:T(4,128)S(1)} %copy-done.4, f32[8,128]{1,0:T(8,128)S(1)} %get-tuple-element.26.after), custom_call_target="tpu_custom_call" | custom-call | bytes 4000000 | tf_op jit(solution)/shard_map/pack_edges/pallas_call | solution.py:236
  10.5 1.3 %collective-permute-start.1 = (f32[4,6,8,128]{3,2,1,0:T(8,128)S(1)}, f32[4,6,8,128]{3,2,1,0:T(8,128)S(1)}, u32[]{:S(2)}, u32[]{:S(2)}) collective-permute-start(f32[4,6,8,128]{3,2,1,0:T(8,128)S(1)} %pack_edges.1), channel_id=1, source_target_pairs={{1,0},{2,1},{3,2},{5,4},{6,5},{7,6},{9,8},{10,9},{11,10},{13,12},{... | collective-permute-start | bytes 294920 | tf_op jit(solution)/shard_map/ppermute | solution.py:668
  11.8 3.0 %collective-permute-start = (f32[4,6,8,128]{3,2,1,0:T(8,128)S(1)}, f32[4,6,8,128]{3,2,1,0:T(8,128)S(1)}, u32[]{:S(2)}, u32[]{:S(2)}) collective-permute-start(f32[4,6,8,128]{3,2,1,0:T(8,128)S(1)} %pack_edges.1), channel_id=1, source_target_pairs={{0,1},{1,2},{2,3},{4,5},{5,6},{6,7},{8,9},{9,10},{10,11},{12,13},{... | collective-permute-start | bytes 294920 | tf_op jit(solution)/shard_map/ppermute | solution.py:667
  14.9 0.0 collective-permute-done.1.refs_2_
  14.9 0.9 %collective-permute-done.refs_1_ = f32[4,6,8,128]{3,2,1,0:T(8,128)S(1)} collective-permute-done((f32[4,6,8,128]{3,2,1,0:T(8,128)S(1)}, f32[4,6,8,128]{3,2,1,0:T(8,128)S(1)}, u32[]{:S(2)}, u32[]{:S(2)}) %collective-permute-start) | collective-permute-done | bytes 98336 | tf_op jit(solution)/shard_map/ppermute | solution.py:667
  15.8 0.2 second_halos.1
  15.9 0.1 collective-permute-start.2
  16.0 1.9 %collective-permute-start.3 = (f32[504,128]{1,0:T(8,128)S(1)}, f32[504,128]{1,0:T(8,128)S(1)}, u32[]{:S(2)}, u32[]{:S(2)}) collective-permute-start(f32[504,128]{1,0:T(8,128)S(1)} %get-tuple-element.28), channel_id=1, source_target_pairs={{0,28},{4,8},{8,4},{12,16},{16,12},{20,24},{24,20},{28,0},{1,29},{... | collective-permute-start | bytes 774152 | tf_op jit(solution)/shard_map/ppermute | solution.py:659
  17.9 0.0 copy-done.1
  17.9 0.0 copy-done.2
  17.9 1.0 %stencil_weights.1.refs_1_.refs_2_ = f32[36,5,8,8,128]{4,3,2,1,0:T(8,128)S(1)} custom-call(f32[5,36,128]{2,1,0:T(8,128)S(1)} %copy-done.1, f32[6,36,128]{2,1,0:T(8,128)S(1)} %copy-done.2, f32[8,128]{1,0:T(8,128)S(1)} %get-tuple-element.26.after), custom_call_target="tpu_custom_call" | custom-call | bytes 2000000 | tf_op jit(solution)/shard_map/stencil_weights/pallas_call | solution.py:427
  18.9 0.0 copy-start.3
  18.9 0.0 copy-start.5
  18.9 0.0 copy-start.6
  19.0 0.0 copy-start.7
  19.0 0.0 copy-start.8
  19.0 0.0 collective-permute-done.9.refs_4_.refs_1_
  19.0 7.0 %collective-permute-done.4.refs_3_.refs_0_ = f32[656,128]{1,0:T(8,128)S(1)} collective-permute-done((f32[656,128]{1,0:T(8,128)S(1)}, f32[656,128]{1,0:T(8,128)S(1)}, u32[]{:S(2)}, u32[]{:S(2)}) %collective-permute-start.4) | collective-permute-done | bytes 335904 | tf_op jit(solution)/shard_map/ppermute | solution.py:659
  25.9 0.1 later_halos.3
  26.0 2.7 %collective-permute-start.10 = (f32[648,128]{1,0:T(8,128)S(1)}, f32[648,128]{1,0:T(8,128)S(1)}, u32[]{:S(2)}, u32[]{:S(2)}) collective-permute-start(f32[648,128]{1,0:T(8,128)S(1)} %get-tuple-element.42), channel_id=1, source_target_pairs={{0,4},{4,0},{8,12},{12,8},{16,20},{20,16},{24,28},{28,24},{1,5},{5... | collective-permute-start | bytes 995336 | tf_op jit(solution)/shard_map/ppermute | solution.py:659
  28.7 3.6 %collective-permute-start.11 = (f32[648,128]{1,0:T(8,128)S(1)}, f32[648,128]{1,0:T(8,128)S(1)}, u32[]{:S(2)}, u32[]{:S(2)}) collective-permute-start(f32[648,128]{1,0:T(8,128)S(1)} %get-tuple-element.43), channel_id=1, source_target_pairs={{0,28},{4,8},{8,4},{12,16},{16,12},{20,24},{24,20},{28,0},{1,29},{... | collective-permute-start | bytes 995336 | tf_op jit(solution)/shard_map/ppermute | solution.py:659
  32.3 0.0 collective-permute-start.5
  32.3 5.1 %collective-permute-done.5.refs_8_ = f32[16,128]{1,0:T(8,128)S(1)} collective-permute-done((f32[16,128]{1,0:T(8,128)S(1)}, f32[16,128]{1,0:T(8,128)S(1)}, u32[]{:S(2)}, u32[]{:S(2)}) %collective-permute-start.5) | collective-permute-done | bytes 8224 | tf_op jit(solution)/shard_map/ppermute | solution.py:677
  37.4 1.2 %collective-permute-start.6 = (f32[32,128]{1,0:T(8,128)S(1)}, f32[32,128]{1,0:T(8,128)S(1)}, u32[]{:S(2)}, u32[]{:S(2)}) collective-permute-start(f32[32,128]{1,0:T(8,128)S(1)} %pad_maximum_fusion), channel_id=1, source_target_pairs={{0,16},{4,20},{8,24},{12,28},{16,0},{20,4},{24,8},{28,12},{1,17},{... | collective-permute-start | bytes 49160 | tf_op jit(solution)/shard_map/ppermute | solution.py:677
  39.2 0.0 collective-permute-done.2.refs_1_.refs_0_.refs_3_
  39.2 0.0 collective-permute-done.3.refs_2_.refs_1_.refs_4_
  39.3 0.0 copy-done.3
  39.3 1.1 %move_ghosts.1 = (f32[36,4,5,8,128]{4,3,2,1,0:T(8,128)S(1)}, f32[8,128]{1,0:T(8,128)S(1)}) custom-call(f32[4,6,8,128]{3,2,1,0:T(8,128)S(1)} %get-tuple-element.29.refs_0_, f32[504,128]{1,0:T(8,128)S(1)} %collective-permute-done.2.refs_1_.refs_0_.refs_3_, f32[504,128]{1,0:T(8,128)S(1)} %collective-permute-done.3.refs_2_.refs_1_.refs_4_, ...), custom_call_target="tpu_custom_call" | custom-call | bytes 2000000 | tf_op jit(solution)/shard_map/move_ghosts/pallas_call | solution.py:335
  40.4 1.7 %collective-permute-done.6.refs_9_ = f32[32,128]{1,0:T(8,128)S(1)} collective-permute-done((f32[32,128]{1,0:T(8,128)S(1)}, f32[32,128]{1,0:T(8,128)S(1)}, u32[]{:S(2)}, u32[]{:S(2)}) %collective-permute-start.6) | collective-permute-done | bytes 16416 | tf_op jit(solution)/shard_map/ppermute | solution.py:677
  42.1 0.0 copy-done.5
  42.1 0.0 copy-done.6
  42.1 0.0 copy-done.7
  42.1 0.0 copy-done.8
  42.1 0.2 surface_wind.1
  42.4 0.4 collective-permute-start.7
  42.7 3.6 %collective-permute-start.8 = (f32[216,128]{1,0:T(8,128)S(1)}, f32[216,128]{1,0:T(8,128)S(1)}, u32[]{:S(2)}, u32[]{:S(2)}) collective-permute-start(f32[216,128]{1,0:T(8,128)S(1)} %get-tuple-element.34), channel_id=1, source_target_pairs={{0,28},{4,8},{8,4},{12,16},{16,12},{20,24},{24,20},{28,0},{1,29},{... | collective-permute-start | bytes 331784 | tf_op jit(solution)/shard_map/ppermute | solution.py:659
  46.3 1.1 %chunk.4 = (f32[8,144,128]{2,1,0:T(8,128)S(1)}, f32[4,8,128]{2,1,0:T(8,128)S(1)}) custom-call(f32[5,36,128]{2,1,0:T(8,128)S(1)} %copy-done.1, f32[36,5,8,8,128]{4,3,2,1,0:T(8,128)S(1)} %stencil_weights.1.refs_1_.refs_2_, f32[36,144,128]{2,1,0:T(8,128)S(1)} %bitcast.12, f32[504,128]{1,0:T(8,128)S(1)} %collective-permute-done.2.refs_1_.refs_0_.refs_3_, ...), custom_call_target="tpu_custom_call" | custom-call | bytes 1000000 | tf_op jit(solution)/shard_map/chunk/pallas_call | solution.py:555
  47.4 1.6 %chunk.3 = (f32[12,144,128]{2,1,0:T(8,128)S(1)}, f32[4,8,128]{2,1,0:T(8,128)S(1)}) custom-call(f32[5,36,128]{2,1,0:T(8,128)S(1)} %copy-done.1, f32[36,5,8,8,128]{4,3,2,1,0:T(8,128)S(1)} %stencil_weights.1.refs_1_.refs_2_, f32[36,144,128]{2,1,0:T(8,128)S(1)} %bitcast.13, f32[656,128]{1,0:T(8,128)S(1)} %collective-permute-done.4.refs_3_.refs_0_, ...), custom_call_target="tpu_custom_call" | custom-call | bytes 1000000 | tf_op jit(solution)/shard_map/chunk/pallas_call | solution.py:555
  48.9 0.0 collective-permute-done.10.refs_3_
  49.0 0.0 collective-permute-done.11.refs_4_
  49.0 1.6 %chunk.5 = (f32[12,144,128]{2,1,0:T(8,128)S(1)}, f32[4,8,128]{2,1,0:T(8,128)S(1)}) custom-call(f32[5,36,128]{2,1,0:T(8,128)S(1)} %copy-done.1, f32[36,5,8,8,128]{4,3,2,1,0:T(8,128)S(1)} %stencil_weights.1.refs_1_.refs_2_, f32[36,144,128]{2,1,0:T(8,128)S(1)} %bitcast.14, f32[648,128]{1,0:T(8,128)S(1)} %collective-permute-done.10.refs_3_, ...), custom_call_target="tpu_custom_call" | custom-call | bytes 1000000 | tf_op jit(solution)/shard_map/chunk/pallas_call | solution.py:555
  50.6 0.0 collective-permute-done.7.refs_3_
  50.6 0.0 collective-permute-done.8.refs_4_
  50.6 2.0 %last_chunk.1 = (f32[36,144,128]{2,1,0:T(8,128)}, f32[2,4,128]{2,1,0:T(4,128)}) custom-call(f32[5,36,128]{2,1,0:T(8,128)S(1)} %copy-done.1, f32[36,5,8,8,128]{4,3,2,1,0:T(8,128)S(1)} %stencil_weights.1.refs_1_.refs_2_, f32[36,144,128]{2,1,0:T(8,128)S(1)} %bitcast.15, f32[216,128]{1,0:T(8,128)S(1)} %collective-permute-done.7.refs_3_, ...), custom_call_target="tpu_custom_call" | custom-call | bytes 6000000 | tf_op jit(solution)/shard_map/last_chunk/pallas_call | solution.py:622
  (4 shorter events, 0.0 us)
Async XLA Ops:
  0.6 8.1 %copy-start = (f32[36,36,4,128]{3,2,1,0:T(4,128)S(1)}, f32[36,36,4,128]{3,2,1,0:T(4,128)}, u32[]{:S(2)}) copy-start(f32[36,36,4,128]{3,2,1,0:T(4,128)} %param.11) | copy-start | bytes 7962628
  2.1 15.8 %copy-start.1 = (f32[5,36,128]{2,1,0:T(8,128)S(1)}, f32[5,36,128]{2,1,0:T(8,128)}, u32[]{:S(2)}) copy-start(f32[5,36,128]{2,1,0:T(8,128)} %constant.6.clone.scal.refs_0_) | copy-start | bytes 276484
  2.1 15.8 %copy-start.2 = (f32[6,36,128]{2,1,0:T(8,128)S(1)}, f32[6,36,128]{2,1,0:T(8,128)}, u32[]{:S(2)}) copy-start(f32[6,36,128]{2,1,0:T(8,128)} %constant.7.clone.ang.refs_4_) | copy-start | bytes 331780
  2.1 23.8 %collective-permute-start.4 = (f32[656,128]{1,0:T(8,128)S(1)}, f32[656,128]{1,0:T(8,128)S(1)}, u32[]{:S(2)}, u32[]{:S(2)}) collective-permute-start(f32[656,128]{1,0:T(8,128)S(1)} %get-tuple-element.31), channel_id=1, source_target_pairs={{0,4},{4,0},{8,12},{12,8},{16,20},{20,16},{24,28},{28,24},{1,5},{5... | collective-permute-start | bytes 1007624 | tf_op jit(solution)/shard_map/ppermute | solution.py:659
  5.2 13.8 %collective-permute-start.9 = (f32[648,128]{1,0:T(8,128)S(1)}, f32[648,128]{1,0:T(8,128)S(1)}, u32[]{:S(2)}, u32[]{:S(2)}) collective-permute-start(f32[648,128]{1,0:T(8,128)S(1)} %get-tuple-element.39), channel_id=1, source_target_pairs={{0,28},{4,8},{8,4},{12,16},{16,12},{20,24},{24,20},{28,0},{1,29},{... | collective-permute-start | bytes 995336 | tf_op jit(solution)/shard_map/ppermute | solution.py:659
  8.7 0.7 %copy-start.4 = (s32[4,128]{1,0:T(4,128)S(1)}, s32[4,128]{1,0:T(4,128)}, u32[]{:S(2)}) copy-start(s32[4,128]{1,0:T(4,128)} %refs_5_.1) | copy-start | bytes 6148
  10.5 4.3 %collective-permute-start.1 = (f32[4,6,8,128]{3,2,1,0:T(8,128)S(1)}, f32[4,6,8,128]{3,2,1,0:T(8,128)S(1)}, u32[]{:S(2)}, u32[]{:S(2)}) collective-permute-start(f32[4,6,8,128]{3,2,1,0:T(8,128)S(1)} %pack_edges.1), channel_id=1, source_target_pairs={{1,0},{2,1},{3,2},{5,4},{6,5},{7,6},{9,8},{10,9},{11,10},{13,12},{... | collective-permute-start | bytes 294920 | tf_op jit(solution)/shard_map/ppermute | solution.py:668
  11.8 4.0 %collective-permute-start = (f32[4,6,8,128]{3,2,1,0:T(8,128)S(1)}, f32[4,6,8,128]{3,2,1,0:T(8,128)S(1)}, u32[]{:S(2)}, u32[]{:S(2)}) collective-permute-start(f32[4,6,8,128]{3,2,1,0:T(8,128)S(1)} %pack_edges.1), channel_id=1, source_target_pairs={{0,1},{1,2},{2,3},{4,5},{5,6},{6,7},{8,9},{9,10},{10,11},{12,13},{... | collective-permute-start | bytes 294920 | tf_op jit(solution)/shard_map/ppermute | solution.py:667
  15.9 23.3 %collective-permute-start.2 = (f32[504,128]{1,0:T(8,128)S(1)}, f32[504,128]{1,0:T(8,128)S(1)}, u32[]{:S(2)}, u32[]{:S(2)}) collective-permute-start(f32[504,128]{1,0:T(8,128)S(1)} %get-tuple-element.27), channel_id=1, source_target_pairs={{0,4},{4,0},{8,12},{12,8},{16,20},{20,16},{24,28},{28,24},{1,5},{5... | collective-permute-start | bytes 774152 | tf_op jit(solution)/shard_map/ppermute | solution.py:659
  16.0 23.2 %collective-permute-start.3 = (f32[504,128]{1,0:T(8,128)S(1)}, f32[504,128]{1,0:T(8,128)S(1)}, u32[]{:S(2)}, u32[]{:S(2)}) collective-permute-start(f32[504,128]{1,0:T(8,128)S(1)} %get-tuple-element.28), channel_id=1, source_target_pairs={{0,28},{4,8},{8,4},{12,16},{16,12},{20,24},{24,20},{28,0},{1,29},{... | collective-permute-start | bytes 774152 | tf_op jit(solution)/shard_map/ppermute | solution.py:659
  18.9 20.3 %copy-start.3 = (f32[5,5,8,128]{3,2,1,0:T(8,128)S(1)}, f32[5,5,8,128]{3,2,1,0:T(8,128)}, u32[]{:S(2)}) copy-start(f32[5,5,8,128]{3,2,1,0:T(8,128)} %constant.8.clone.refs_3_) | copy-start | bytes 307204
  18.9 23.1 %copy-start.5 = (s32[4,128]{1,0:T(4,128)S(1)}, s32[4,128]{1,0:T(4,128)}, u32[]{:S(2)}) copy-start(s32[4,128]{1,0:T(4,128)} %refs_5_.1) | copy-start | bytes 6148
  18.9 23.1 %copy-start.6 = (s32[4,4,128]{2,1,0:T(4,128)S(1)}, s32[4,4,128]{2,1,0:T(4,128)}, u32[]{:S(2)}) copy-start(s32[4,4,128]{2,1,0:T(4,128)} %param.17) | copy-start | bytes 24580
  19.0 23.1 %copy-start.7 = (f32[4,4,128]{2,1,0:T(4,128)S(1)}, f32[4,4,128]{2,1,0:T(4,128)}, u32[]{:S(2)}) copy-start(f32[4,4,128]{2,1,0:T(4,128)} %param.18) | copy-start | bytes 24580
  19.0 23.1 %copy-start.8 = (f32[2,4,128]{2,1,0:T(4,128)S(1)}, f32[2,4,128]{2,1,0:T(4,128)}, u32[]{:S(2)}) copy-start(f32[2,4,128]{2,1,0:T(4,128)} %refs_6_.1) | copy-start | bytes 12292
  26.0 22.9 %collective-permute-start.10 = (f32[648,128]{1,0:T(8,128)S(1)}, f32[648,128]{1,0:T(8,128)S(1)}, u32[]{:S(2)}, u32[]{:S(2)}) collective-permute-start(f32[648,128]{1,0:T(8,128)S(1)} %get-tuple-element.42), channel_id=1, source_target_pairs={{0,4},{4,0},{8,12},{12,8},{16,20},{20,16},{24,28},{28,24},{1,5},{5... | collective-permute-start | bytes 995336 | tf_op jit(solution)/shard_map/ppermute | solution.py:659
  28.7 20.2 %collective-permute-start.11 = (f32[648,128]{1,0:T(8,128)S(1)}, f32[648,128]{1,0:T(8,128)S(1)}, u32[]{:S(2)}, u32[]{:S(2)}) collective-permute-start(f32[648,128]{1,0:T(8,128)S(1)} %get-tuple-element.43), channel_id=1, source_target_pairs={{0,28},{4,8},{8,4},{12,16},{16,12},{20,24},{24,20},{28,0},{1,29},{... | collective-permute-start | bytes 995336 | tf_op jit(solution)/shard_map/ppermute | solution.py:659
  32.3 5.1 %collective-permute-start.5 = (f32[16,128]{1,0:T(8,128)S(1)}, f32[16,128]{1,0:T(8,128)S(1)}, u32[]{:S(2)}, u32[]{:S(2)}) collective-permute-start(f32[16,128]{1,0:T(8,128)S(1)} %pad_maximum_fusion.1.refs_7_), channel_id=1, source_target_pairs={{0,8},{4,12},{8,0},{12,4},{16,24},{20,28},{24,16},{28,20},{1,9},{5... | collective-permute-start | bytes 24584 | tf_op jit(solution)/shard_map/ppermute | solution.py:677
  37.4 4.6 %collective-permute-start.6 = (f32[32,128]{1,0:T(8,128)S(1)}, f32[32,128]{1,0:T(8,128)S(1)}, u32[]{:S(2)}, u32[]{:S(2)}) collective-permute-start(f32[32,128]{1,0:T(8,128)S(1)} %pad_maximum_fusion), channel_id=1, source_target_pairs={{0,16},{4,20},{8,24},{12,28},{16,0},{20,4},{24,8},{28,12},{1,17},{... | collective-permute-start | bytes 49160 | tf_op jit(solution)/shard_map/ppermute | solution.py:677
  42.4 8.2 %collective-permute-start.7 = (f32[216,128]{1,0:T(8,128)S(1)}, f32[216,128]{1,0:T(8,128)S(1)}, u32[]{:S(2)}, u32[]{:S(2)}) collective-permute-start(f32[216,128]{1,0:T(8,128)S(1)} %get-tuple-element.33), channel_id=1, source_target_pairs={{0,4},{4,0},{8,12},{12,8},{16,20},{20,16},{24,28},{28,24},{1,5},{5... | collective-permute-start | bytes 331784 | tf_op jit(solution)/shard_map/ppermute | solution.py:659
  42.7 7.8 %collective-permute-start.8 = (f32[216,128]{1,0:T(8,128)S(1)}, f32[216,128]{1,0:T(8,128)S(1)}, u32[]{:S(2)}, u32[]{:S(2)}) collective-permute-start(f32[216,128]{1,0:T(8,128)S(1)} %get-tuple-element.34), channel_id=1, source_target_pairs={{0,28},{4,8},{8,4},{12,16},{16,12},{20,24},{24,20},{28,0},{1,29},{... | collective-permute-start | bytes 331784 | tf_op jit(solution)/shard_map/ppermute | solution.py:659
